TPU v7x, 256 devices: a whole 4x4x8 slice. The times are simulated.
256 devices in a mesh: lat: 8 (over x_hi, y), lon: 32 (over z, x_lo, core).
Axes of the slice: x: 4 (x_hi: 2, x_lo: 2; x = x_hi * 2 + x_lo), y: 4, z: 8, core: 2. Of those that a mesh axis runs over, the one named last changes fastest.
Arguments:
- tokens: bfloat16 [1, 96, 384, 2, 512], P(None, 'lat', 'lon'), may hold values from -6 to 6
- layer_norm_gain: float32 [512], replicated, may hold values from 0.25 to 1.75
- cotangent: bfloat16 [1, 96, 384, 2, 512], P(None, 'lat', 'lon'), may hold values from -6 to 6
- w_qkv: bfloat16 [512, 1536], replicated, may hold values from -2 to 2
- w_out: bfloat16 [512, 512], replicated, may hold values from -0.25 to 0.25
Outputs:
- mixed: bfloat16 [1, 96, 384, 2, 512], P(None, 'lat', 'lon')
- grad_tokens: bfloat16 [1, 96, 384, 2, 512], P(None, 'lat', 'lon')
- gain_gradient: float32 [512], replicated
- grad_qkv: bfloat16 [512, 1536], replicated
- grad_out: bfloat16 [512, 512], replicated
All inputs are finite; a program needn't handle non-finite values.
Results may differ from a plain program's by a relative error of at most 0.02.
Values may be sent and summed in bfloat16 or wider, within the bound.
No kernel may reach another device: no remote copies, remote signals or barrier semaphores. Data moves between devices by JAX's collectives and lax.ppermute only.
A program may use at most 64 MiB of HBM per device.

v0:
```python
import math

import jax
import jax.numpy as jnp
from jax import lax
from jax.sharding import PartitionSpec as P

HEADS = 16
WIN = 12
SHIFT = 6


EPS = 1e-05
MASKED = -1e30


def shifted(shard, axis, by):
    peers = lax.axis_size(axis)
    return lax.ppermute(shard, axis, [(i, (i + by) % peers) for i in range(peers)])


def to_windows(block):
    samples, lat_rows, lon_cols, levels, channels = block.shape
    parted = block.reshape(samples, lat_rows // WIN, WIN, lon_cols // WIN, WIN, levels, channels)
    parted = parted.transpose(0, 1, 3, 2, 4, 5, 6)
    return parted.reshape(
        samples * (lat_rows // WIN) * (lon_cols // WIN), WIN * WIN * levels, channels
    )


def from_windows(windows, leading):
    samples, lat_rows, lon_cols, levels = leading
    channels = windows.shape[-1]
    parted = windows.reshape(samples, lat_rows // WIN, lon_cols // WIN, WIN, WIN, levels, channels)
    return parted.transpose(0, 1, 3, 2, 4, 5, 6).reshape(
        samples, lat_rows, lon_cols, levels, channels
    )


def frame_move(stacked, direction):
    lat_rows = stacked.shape[2]
    first_row = 0 if direction < 0 else lat_rows - SHIFT
    keep_row = SHIFT if direction < 0 else 0
    arrived = shifted(
        lax.slice_in_dim(stacked, first_row, first_row + SHIFT, axis=2), "lat", direction
    )
    remain = lax.slice_in_dim(stacked, keep_row, keep_row + lat_rows - SHIFT, axis=2)
    stacked = jnp.concatenate((remain, arrived) if direction < 0 else (arrived, remain), 2)
    lon_cols = stacked.shape[3]
    first_col = 0 if direction < 0 else lon_cols - SHIFT
    keep_col = SHIFT if direction < 0 else 0
    arrived = shifted(
        lax.slice_in_dim(stacked, first_col, first_col + SHIFT, axis=3), "lon", direction
    )
    remain = lax.slice_in_dim(stacked, keep_col, keep_col + lon_cols - SHIFT, axis=3)
    return jnp.concatenate((remain, arrived) if direction < 0 else (arrived, remain), 3)


def split_heads(qkv_rows):
    groups, win_tokens, columns = qkv_rows.shape
    features = columns // 3
    head_size = features // HEADS
    queries = qkv_rows[..., :features].reshape(groups, win_tokens, HEADS, head_size)
    key_rows = qkv_rows[..., features : 2 * features].reshape(groups, win_tokens, HEADS, head_size)
    values = qkv_rows[..., 2 * features :].reshape(groups, win_tokens, HEADS, head_size)
    return (queries, key_rows, values)


def probabilities(queries, key_rows, labels):
    inv_root = 1.0 / math.sqrt(queries.shape[-1])
    scores = (
        jnp.einsum("nqhd,nkhd->nhqk", queries, key_rows, preferred_element_type=jnp.float32)
        * inv_root
    )
    allow = labels[:, None, :, None] == labels[:, None, None, :]
    scores = jnp.where(allow, scores, MASKED)
    row_max = jnp.max(scores, -1, keepdims=True)
    exponent = jnp.exp(scores - row_max)
    return exponent / jnp.sum(exponent, -1, keepdims=True)


def attend_forward(window_item):
    qkv_rows, labels = window_item
    groups, win_tokens, columns = qkv_rows.shape
    queries, key_rows, values = split_heads(qkv_rows)
    attn_probs = probabilities(queries, key_rows, labels)
    heads_out = jnp.einsum(
        "nhqk,nkhd->nqhd",
        attn_probs.astype(jnp.bfloat16),
        values,
        preferred_element_type=jnp.float32,
    )
    return heads_out.astype(jnp.bfloat16).reshape(groups, win_tokens, columns // 3)


def attend_backward(window_item):
    qkv_rows, labels, grad_attn = window_item
    groups, win_tokens, columns = qkv_rows.shape
    features = columns // 3
    queries, key_rows, values = split_heads(qkv_rows)
    inv_root = 1.0 / math.sqrt(queries.shape[-1])
    attn_probs = probabilities(queries, key_rows, labels)
    probs_low = attn_probs.astype(jnp.bfloat16)
    grad_heads = grad_attn.reshape(queries.shape)
    grad_probs = jnp.einsum(
        "nqhd,nkhd->nhqk", grad_heads, values, preferred_element_type=jnp.float32
    )
    grad_values = jnp.einsum(
        "nhqk,nqhd->nkhd", probs_low, grad_heads, preferred_element_type=jnp.float32
    ).astype(jnp.bfloat16)
    grad_scores = (
        attn_probs * (grad_probs - jnp.sum(grad_probs * attn_probs, -1, keepdims=True)) * inv_root
    ).astype(jnp.bfloat16)
    grad_queries = jnp.einsum(
        "nhqk,nkhd->nqhd", grad_scores, key_rows, preferred_element_type=jnp.float32
    ).astype(jnp.bfloat16)
    grad_keys = jnp.einsum(
        "nhqk,nqhd->nkhd", grad_scores, queries, preferred_element_type=jnp.float32
    ).astype(jnp.bfloat16)
    return jnp.concatenate(
        [
            grad_queries.reshape(groups, win_tokens, features),
            grad_keys.reshape(groups, win_tokens, features),
            grad_values.reshape(groups, win_tokens, features),
        ],
        -1,
    )


def by_groups(function, items):
    win_count = items[0].shape[0]
    group_size = 1
    packed = tuple(
        (array.reshape((win_count // group_size, group_size) + array.shape[1:]) for array in items)
    )
    result = lax.map(function, packed)
    return result.reshape((win_count,) + result.shape[2:])


def shards(tokens, layer_norm_gain, cotangent, w_qkv, w_out):
    full_shape = tokens.shape
    samples, lat_rows, lon_cols, levels, features = full_shape
    leading = full_shape[:-1]
    tokens_wide = tokens.astype(jnp.float32)
    average = jnp.mean(tokens_wide, -1, keepdims=True)
    mean_removed = tokens_wide - average
    inverse_deviation = lax.rsqrt(jnp.mean(mean_removed * mean_removed, -1, keepdims=True) + EPS)
    standardized_input = mean_removed * inverse_deviation
    normalized_input = (standardized_input * layer_norm_gain).astype(jnp.bfloat16)
    rolled = frame_move(normalized_input[None], -1)[0]
    flat_rows = rolled.reshape(-1, features)
    qkv_rows = jnp.dot(flat_rows, w_qkv, preferred_element_type=jnp.float32).astype(jnp.bfloat16)
    qkv_win = to_windows(qkv_rows.reshape(leading + (3 * features,)))
    lat_total = lat_rows * lax.axis_size("lat")
    row_global = lax.axis_index("lat") * lat_rows + jnp.arange(lat_rows, dtype=jnp.int32)
    region = (row_global >= lat_total - SHIFT).astype(jnp.int32)
    label_win = to_windows(jnp.broadcast_to(region[None, :, None, None, None], leading + (1,)))[
        :, :, 0
    ]
    attn_win = by_groups(attend_forward, (qkv_win, label_win))
    attn = from_windows(attn_win, leading)
    back = frame_move(attn[None], 1)[0]
    mixed = (
        tokens_wide
        + jnp.dot(back.reshape(-1, features), w_out, preferred_element_type=jnp.float32).reshape(
            full_shape
        )
    ).astype(jnp.bfloat16)
    g_rolled = frame_move(cotangent[None], -1)[0]
    g_flat = g_rolled.reshape(-1, features)
    grad_attn = jnp.dot(g_flat, w_out.T, preferred_element_type=jnp.float32).astype(jnp.bfloat16)
    part_out = jnp.einsum(
        "tc,td->cd", attn.reshape(-1, features), g_flat, preferred_element_type=jnp.float32
    )
    dqkv_win = by_groups(
        attend_backward, (qkv_win, label_win, to_windows(grad_attn.reshape(full_shape)))
    )
    dqkv_rows = from_windows(dqkv_win, leading).reshape(-1, 3 * features)
    part_qkv = jnp.einsum("tc,td->cd", flat_rows, dqkv_rows, preferred_element_type=jnp.float32)
    d_rolled = (
        jnp.dot(dqkv_rows, w_qkv.T, preferred_element_type=jnp.float32)
        .astype(jnp.bfloat16)
        .reshape(full_shape)
    )
    normalized_gradient = frame_move(d_rolled[None], 1)[0].astype(jnp.float32)
    partial_gain = jnp.sum(normalized_gradient * standardized_input, axis=(0, 1, 2, 3))
    out_total, qkv_total, gain_total = lax.psum((part_out, part_qkv, partial_gain), ("lat", "lon"))
    token_total = samples * lat_total * lon_cols * lax.axis_size("lon") * levels
    gradient_factor = 1.0 / math.sqrt(token_total)
    scaled_output = normalized_gradient * layer_norm_gain
    inner_product = (
        scaled_output
        - jnp.mean(scaled_output, -1, keepdims=True)
        - standardized_input * jnp.mean(scaled_output * standardized_input, -1, keepdims=True)
    )
    grad_tokens = (cotangent.astype(jnp.float32) + inverse_deviation * inner_product).astype(
        jnp.bfloat16
    )
    gain_gradient = gain_total * gradient_factor
    grad_qkv = (qkv_total * gradient_factor).astype(jnp.bfloat16)
    grad_out = (out_total * gradient_factor).astype(jnp.bfloat16)
    return (mixed, grad_tokens, gain_gradient, grad_qkv, grad_out)


def solution(mesh):
    in_specs = (P(None, "lat", "lon", None, None), P(), P(None, "lat", "lon", None, None), P(), P())
    out_specs = (
        P(None, "lat", "lon", None, None),
        P(None, "lat", "lon", None, None),
        P(),
        P(),
        P(),
    )
    return jax.shard_map(shards, mesh=mesh, in_specs=in_specs, out_specs=out_specs, check_vma=False)
```

profile of v0, /device:TPU:1, one launch (start us, length us, event | category | flops | bytes accessed | tf_op | source)
XLA Modules:
  0.0 372.5 jit_solution(721627766249018833)
XLA Ops:
  7.2 1.2 convert_reduce_fusion
  8.5 1.2 fusion.46
  9.7 1.2 fusion.53
  10.9 6.1 %collective-permute-start = (bf16[1,1,6,12,2,512]{5,3,4,2,1,0:T(8,128)(2,1)S(1)}, bf16[1,1,6,12,2,512]{5,3,4,2,1,0:T(8,128)(2,1)S(1)}, u32[]{:S(2)}, u32[]{:S(2)}) collective-permute-start(bf16[1,1,6,12,2,512]{5,3,4,2,1,0:T(8,128)(2,1)S(1)} %get-tuple-element.57), channel_id=1, source_target_pairs={{0,224},{32,0},{64,32},{96,64},{128,96},{160,128},{192,160},{224,1... | collective-permute-start | bytes 442376 | tf_op jit(solution)/shard_map/ppermute | solution.py:19
  17.0 1.2 fusion.72
  18.2 0.5 collective-permute-start.4
  19.0 1.6 collective-permute-done
  20.7 2.8 collective-permute-start.1
  23.4 0.8 broadcast_compare_fusion
  24.2 1.0 fusion.57
  25.3 3.3 collective-permute-start.5
  28.7 0.3 copy.29
  29.2 0.6 fusion.15
  29.9 0.9 copy.31
  30.8 0.9 copy.32
  31.9 1.3 pad_maximum_fusion.1
  33.4 1.4 convolution_convert_fusion.2
  35.0 4.1 %fusion.75 = f32[16,288,288]{1,2,0:T(8,128)} fusion(bf16[288,16,32]{0,2,1:T(8,128)(2,1)S(1)} %bitcast.82, bf16[288,16,32]{0,2,1:T(8,128)(2,1)S(1)} %bitcast.80), kind=kOutput, calls=%fused_computation.97 | convolution fusion | flops 84934656 | bytes 5898240 | tf_op jit(solution)/shard_map/while/body/eval_jaxpr/nqhd,nkhd->nhqk/dot_general | solution.py:105
  39.1 6.4 %fusion.74 = (f32[16,288]{1,0:T(8,128)S(1)}, f32[16,288,288]{1,2,0:T(8,128)}) fusion(pred[288,288]{0,1:T(8,128)(4,1)S(1)} %copy-done.6, bf16[288,16,32]{0,2,1:T(8,128)(2,1)S(1)} %bitcast.92, bf16[288,16,32]{0,2,1:T(8,128)(2,1)} %bitcast.93), kind=kOutput, calls=%fused_computation.96 | convolution fusion | flops 90243360 | bytes 5999616 | tf_op jit(solution)/shard_map/while/body/eval_jaxpr/sub | solution.py:78
  45.5 11.1 %fusion.28 = bf16[16,32,288]{2,1,0:T(8,128)(2,1)S(1)} fusion(bf16[288,16,32]{0,2,1:T(8,128)(2,1)} %bitcast.94, f32[16,288,288]{1,2,0:T(8,128)} %fusion.75, f32[16,288,288]{1,2,0:T(8,128)} %get-tuple-element.67, f32[16,288]{1,0:T(8,128)S(1)} %get-tuple-element.66), kind=kOutput, calls=%fused_computation.26 | convolution fusion | flops 94376736 | bytes 11225088 | tf_op jit(solution)/shard_map/while/body/eval_jaxpr/nhqk,nkhd->nqhd/dot_general | solution.py:114
  56.6 12.0 %fusion.31 = bf16[16,32,288]{2,1,0:T(8,128)(2,1)} fusion(bf16[288,16,32]{0,2,1:T(8,128)(2,1)} %bitcast.91, f32[16,288,288]{1,2,0:T(8,128)} %fusion.75, f32[16,288,288]{1,2,0:T(8,128)} %get-tuple-element.67, f32[16,288]{1,0:T(8,128)S(1)} %get-tuple-element.66), kind=kOutput, calls=%fused_computation.27 | convolution fusion | flops 94376736 | bytes 11225088 | tf_op jit(solution)/shard_map/while/body/eval_jaxpr/nhqk,nqhd->nkhd/dot_general | solution.py:117
  68.6 4.2 %fusion.25 = bf16[16,32,288]{2,1,0:T(8,128)(2,1)S(1)} fusion(bf16[288,16,32]{0,2,1:T(8,128)(2,1)S(1)} %bitcast.83, f32[16,288,288]{1,2,0:T(8,128)} %get-tuple-element.67, f32[16,288]{1,0:T(8,128)S(1)} %get-tuple-element.66), kind=kOutput, calls=%fused_computation.25 | convolution fusion | flops 87736320 | bytes 5916672 | tf_op jit(solution)/shard_map/while/body/eval_jaxpr/nhqk,nqhd->nkhd/dot_general | solution.py:108
  72.8 0.8 copy-done.8
  73.6 1.5 fusion.22
  75.1 2.9 fusion.52
  78.0 0.9 convolution_convert_fusion.1
  79.3 0.7 copy.53
  80.0 2.1 copy.34
  82.1 1.6 broadcast_in_dim_reshape_transpose_reshape_reshape.3
  83.7 1.3 fusion.73
  85.0 0.7 copy.51
  85.7 0.5 collective-permute-start.2
  86.1 2.4 fusion.76
  88.6 1.2 collective-permute-done.6
  89.7 0.9 constant_dynamic-update-slice_fusion.1
  90.9 4.6 %collective-permute-done.2 = bf16[1,1,6,12,2,512]{5,3,4,2,1,0:T(8,128)(2,1)} collective-permute-done((bf16[1,1,6,12,2,512]{5,3,4,2,1,0:T(8,128)(2,1)}, bf16[1,1,6,12,2,512]{5,3,4,2,1,0:T(8,128)(2,1)}, u32[]{:S(2)}, u32[]{:S(2)}) %collective-permute-start.2) | collective-permute-done | bytes 147488 | tf_op jit(solution)/shard_map/ppermute | solution.py:19
  95.4 0.9 constant_dynamic-update-slice_fusion
  96.6 0.6 fusion.48
  97.2 0.4 fusion.45
  97.6 1.0 copy.45
  98.6 4.1 %collective-permute-done.3 = bf16[1,1,12,6,2,512]{5,3,4,2,1,0:T(8,128)(2,1)S(1)} collective-permute-done((bf16[1,1,12,6,2,512]{5,3,4,2,1,0:T(8,128)(2,1)S(1)}, bf16[1,1,12,6,2,512]{5,3,4,2,1,0:T(8,128)(2,1)S(1)}, u32[]{:S(2)}, u32[]{:S(2)}) %collective-permute-start.3) | collective-permute-done | bytes 147488 | tf_op jit(solution)/shard_map/ppermute | solution.py:19
  102.8 0.4 fusion.21
  103.2 1.0 copy.44
  104.2 78.8 %psum.21 = f32[512]{0:T(512)S(1)} all-reduce(f32[512]{0:T(512)S(1)} %get-tuple-element.42), channel_id=1, replica_groups=mesh['lat'=8,'lon'=32] {'lat','lon'}, use_global_device_ids=true, to_apply=%region_8.9 | all-reduce | flops 512 | bytes 4096 | tf_op jit(solution)/shard_map/psum | solution.py:187
  183.0 0.6 broadcast_multiply_fusion.3
  183.6 176.5 %all-reduce.3.cloned.1.call-done = (f32[512,1536]{1,0:T(8,128)}, f32[512,512]{1,0:T(8,128)}) async-done(((f32[512,1536]{1,0:T(8,128)}, f32[512,512]{1,0:T(8,128)}), (f32[512,1536]{1,0:T(8,128)}, f32[512,512]{1,0:T(8,128)})) %all-reduce.3.cloned.1.call-update) | async-done | bytes 4194320 | tf_op jit(solution)/shard_map/psum | solution.py:187
  360.1 3.4 multiply_convert_fusion.1
  363.5 2.1 multiply_convert_fusion.2
  (46 shorter events, 2.0 us)
Async XLA Ops:
  7.2 22.0 %copy-start = (bf16[512,1536]{1,0:T(8,128)(2,1)S(1)}, bf16[512,1536]{1,0:T(8,128)(2,1)}, u32[]{:S(2)}) copy-start(bf16[512,1536]{1,0:T(8,128)(2,1)} %param.8) | copy-start | bytes 4718596
  7.2 353.0 %all-reduce.3.cloned.1.call-start = ((), (), s32[]{:S(2)}) async-start(), calls=%async_computation | async-start | bytes 8388608 | tf_op jit(solution)/shard_map/psum | solution.py:187
  10.9 9.7 %collective-permute-start = (bf16[1,1,6,12,2,512]{5,3,4,2,1,0:T(8,128)(2,1)S(1)}, bf16[1,1,6,12,2,512]{5,3,4,2,1,0:T(8,128)(2,1)S(1)}, u32[]{:S(2)}, u32[]{:S(2)}) collective-permute-start(bf16[1,1,6,12,2,512]{5,3,4,2,1,0:T(8,128)(2,1)S(1)} %get-tuple-element.57), channel_id=1, source_target_pairs={{0,224},{32,0},{64,32},{96,64},{128,96},{160,128},{192,160},{224,1... | collective-permute-start | bytes 442376 | tf_op jit(solution)/shard_map/ppermute | solution.py:19
  18.2 6.0 %collective-permute-start.4 = (bf16[1,1,6,12,2,512]{5,4,3,2,1,0:T(2,128)(2,1)S(1)}, bf16[1,1,6,12,2,512]{5,4,3,2,1,0:T(2,128)(2,1)S(1)}, u32[]{:S(2)}, u32[]{:S(2)}) collective-permute-start(bf16[1,1,6,12,2,512]{5,4,3,2,1,0:T(2,128)(2,1)S(1)} %get-tuple-element.63), channel_id=1, source_target_pairs={{0,224},{32,0},{64,32},{96,64},{128,96},{160,128},{192,160},{224,1... | collective-permute-start | bytes 442376 | tf_op jit(solution)/shard_map/ppermute | solution.py:19
  20.7 7.9 %collective-permute-start.1 = (bf16[1,1,12,6,2,512]{5,3,4,2,1,0:T(8,128)(2,1)S(1)}, bf16[1,1,12,6,2,512]{5,3,4,2,1,0:T(8,128)(2,1)S(1)}, u32[]{:S(2)}, u32[]{:S(2)}) collective-permute-start(bf16[1,1,12,6,2,512]{5,3,4,2,1,0:T(8,128)(2,1)S(1)} %get-tuple-element.55), channel_id=1, source_target_pairs={{0,31},{1,0},{2,1},{3,2},{4,3},{5,4},{6,5},{7,6},{8,7},{9,8},{10,9... | collective-permute-start | bytes 442376 | tf_op jit(solution)/shard_map/ppermute | solution.py:19
  25.3 6.7 %collective-permute-start.5 = (bf16[1,1,12,6,2,512]{5,4,3,2,1,0:T(2,128)(2,1)}, bf16[1,1,12,6,2,512]{5,4,3,2,1,0:T(2,128)(2,1)}, u32[]{:S(2)}, u32[]{:S(2)}) collective-permute-start(bf16[1,1,12,6,2,512]{5,4,3,2,1,0:T(2,128)(2,1)} %get-tuple-element.61), channel_id=1, source_target_pairs={{0,31},{1,0},{2,1},{3,2},{4,3},{5,4},{6,5},{7,6},{8,7},{9,8},{10,9... | collective-permute-start | bytes 442376 | tf_op jit(solution)/shard_map/ppermute | solution.py:19
  29.8 9.3 %copy-start.6 = (pred[288,288]{0,1:T(8,128)(4,1)S(1)}, pred[288,288]{0,1:T(8,128)(4,1)}, u32[]{:S(2)}) copy-start(pred[288,288]{0,1:T(8,128)(4,1)} %broadcast_compare_fusion) | copy-start | bytes 248836
  35.0 4.1 %copy-start.5 = (bf16[1,288,512]{1,2,0:T(8,128)(2,1)S(1)}, bf16[1,288,512]{1,2,0:T(8,128)(2,1)}, u32[]{:S(2)}) copy-start(bf16[1,288,512]{1,2,0:T(8,128)(2,1)} %copy.31) | copy-start | bytes 884740
  68.6 5.0 %copy-start.8 = (f32[16,288,288]{1,2,0:T(8,128)S(1)}, f32[16,288,288]{1,2,0:T(8,128)}, u32[]{:S(2)}) copy-start(f32[16,288,288]{1,2,0:T(8,128)} %get-tuple-element.67) | copy-start | bytes 15925252
  73.6 1.5 copy-start.4
  79.0 17.6 %copy-start.1 = (bf16[1,12,12,2,512]{4,3,2,1,0:T(2,128)(2,1)S(1)}, bf16[1,12,12,2,512]{4,3,2,1,0:T(2,128)(2,1)}, u32[]{:S(2)}) copy-start(bf16[1,12,12,2,512]{4,3,2,1,0:T(2,128)(2,1)} %param.5) | copy-start | bytes 884740
  79.0 17.6 %copy-start.7 = (f32[512]{0:T(512)S(1)}, f32[512]{0:T(512)}, u32[]{:S(2)}) copy-start(f32[512]{0:T(512)} %param.6) | copy-start | bytes 6148
  80.0 9.8 %collective-permute-start.6 = (bf16[1,1,6,12,2,512]{5,3,4,2,1,0:T(8,128)(2,1)}, bf16[1,1,6,12,2,512]{5,3,4,2,1,0:T(8,128)(2,1)}, u32[]{:S(2)}, u32[]{:S(2)}) collective-permute-start(bf16[1,1,6,12,2,512]{5,3,4,2,1,0:T(8,128)(2,1)} %copy.53), channel_id=1, source_target_pairs={{0,32},{32,64},{64,96},{96,128},{128,160},{160,192},{192,224},{224... | collective-permute-start | bytes 442376 | tf_op jit(solution)/shard_map/ppermute | solution.py:19
  83.7 13.5 %copy-start.2 = (bf16[1,12,12,2,512]{4,3,2,1,0:T(2,128)(2,1)S(1)}, bf16[1,12,12,2,512]{4,3,2,1,0:T(2,128)(2,1)}, u32[]{:S(2)}) copy-start(bf16[1,12,12,2,512]{4,3,2,1,0:T(2,128)(2,1)} %param.7) | copy-start | bytes 884740
  83.7 19.1 %copy-start.3 = (bf16[512,512]{1,0:T(8,128)(2,1)S(1)}, bf16[512,512]{1,0:T(8,128)(2,1)}, u32[]{:S(2)}) copy-start(bf16[512,512]{1,0:T(8,128)(2,1)} %param.9) | copy-start | bytes 1572868
  85.7 9.8 %collective-permute-start.2 = (bf16[1,1,6,12,2,512]{5,3,4,2,1,0:T(8,128)(2,1)}, bf16[1,1,6,12,2,512]{5,3,4,2,1,0:T(8,128)(2,1)}, u32[]{:S(2)}, u32[]{:S(2)}) collective-permute-start(bf16[1,1,6,12,2,512]{5,3,4,2,1,0:T(8,128)(2,1)} %copy.51), channel_id=1, source_target_pairs={{0,32},{32,64},{64,96},{96,128},{128,160},{160,192},{192,224},{224... | collective-permute-start | bytes 442376 | tf_op jit(solution)/shard_map/ppermute | solution.py:19
  90.8 5.8 %collective-permute-start.7 = (bf16[1,1,12,6,2,512]{5,3,4,2,1,0:T(8,128)(2,1)S(1)}, bf16[1,1,12,6,2,512]{5,3,4,2,1,0:T(8,128)(2,1)S(1)}, u32[]{:S(2)}, u32[]{:S(2)}) collective-permute-start(bf16[1,1,12,6,2,512]{5,3,4,2,1,0:T(8,128)(2,1)S(1)} %get-tuple-element.50), channel_id=1, source_target_pairs={{0,1},{1,2},{2,3},{3,4},{4,5},{5,6},{6,7},{7,8},{8,9},{9,10},{10,1... | collective-permute-start | bytes 442376 | tf_op jit(solution)/shard_map/ppermute | solution.py:19
  96.5 6.3 %collective-permute-start.3 = (bf16[1,1,12,6,2,512]{5,3,4,2,1,0:T(8,128)(2,1)S(1)}, bf16[1,1,12,6,2,512]{5,3,4,2,1,0:T(8,128)(2,1)S(1)}, u32[]{:S(2)}, u32[]{:S(2)}) collective-permute-start(bf16[1,1,12,6,2,512]{5,3,4,2,1,0:T(8,128)(2,1)S(1)} %get-tuple-element.52), channel_id=1, source_target_pairs={{0,1},{1,2},{2,3},{3,4},{4,5},{5,6},{6,7},{7,8},{8,9},{9,10},{10,1... | collective-permute-start | bytes 442376 | tf_op jit(solution)/shard_map/ppermute | solution.py:19
Sparse Core Ops, SparseCore 0:
  88.7 271.4 all-reduce.2
where the time goes:
time: 374 us; the launch traced here: 373 us
  waiting for transfers between devices  188 us (50%)
  blocking collectives  78.8 us (21%)
  matrix products  47.9 us (13%)
  local copies, waits for them, and re-layouts  15.9 us (4%)
  between operations  14.4 us (4%)
  other arithmetic  14.1 us (4%)
  starting transfers between devices  13.4 us (4%)
    psum x1, waiting for transfers between devices, shards(): lax.psum((part_out, part_qkv, partial_gain), ('lat', 'lon'))  177 us
    psum x1, blocking collectives, shards(): lax.psum((part_out, part_qkv, partial_gain), ('lat', 'lon'))  78.8 us
    ppermute x8, starting transfers between devices, shifted(): lax.ppermute(shard, axis, [(i, (i + by) % peers) for i in range(peers)])  13.4 us
    dot_general x1, matrix products, attend_backward(): jnp.einsum('nhqk,nqhd->nkhd', grad_scores, queries, preferred_element_typ...  12 us
    ppermute x8, waiting for transfers between devices, shifted(): lax.ppermute(shard, axis, [(i, (i + by) % peers) for i in range(peers)])  11.5 us
    dot_general x1, matrix products, attend_backward(): jnp.einsum('nhqk,nkhd->nqhd', grad_scores, key_rows, preferred_element_ty...  11.1 us
  transfers between devices with their start and end apart: 9, of which 5 were waited for; matrix products, arithmetic and copies ran while one was open for 6% of the time, Pallas kernels for 0%

commit v1 on v0

v1 whole, which is shorter than its diff:
```python
import math

import jax
import jax.numpy as jnp
from jax import lax
from jax.experimental import pallas as pl
from jax.experimental.pallas import tpu as pltpu
from jax.sharding import Mesh
from jax.sharding import PartitionSpec as P

HEADS = 16
WIN = 12
SHIFT = 6
EPS = 1e-05
MASKED = -1e30
F32 = jnp.float32
BF16 = jnp.bfloat16

LAT = ("xh", "y")
LON = ("z", "xl", "core")
CHIPS = ("xh", "y", "z", "xl")
EVERY = LAT + LON


def dot(a, b, dims=((1,), (0,))):
    return lax.dot_general(a, b, (dims, ((), ())), preferred_element_type=F32)


def normalise(tok):
    mean = jnp.mean(tok, -1, keepdims=True)
    centred = tok - mean
    inv = lax.rsqrt(jnp.mean(centred * centred, -1, keepdims=True) + EPS)
    return centred * inv, inv


def gather_quads(refs, which, out):
    rows = refs[0].shape[1]
    for j, ref in enumerate(refs):
        out[j * rows : (j + 1) * rows, :] = ref[which].astype(F32)


def grads_kernel(
    ids, q0, q1, q2, q3, gain, wqkv, wqkv_t, wout,
    keep, send, attn_t, d_t,
    wide, normed, g_low, qkv_t, kv, do_t,
):
    quads = (q0, q1, q2, q3)
    tokens, feat = normed.shape
    size = feat // HEADS
    per = 128 // size
    gather_quads(quads, 1, wide)
    g_low[...] = wide[...].astype(BF16)
    do_t[...] = dot(wout[...], g_low[...], ((1,), (1,))).astype(BF16)
    gather_quads(quads, 0, wide)
    xhat, _ = normalise(wide[...])
    normed[...] = (xhat * gain[...]).astype(BF16)
    qkv_t[...] = dot(wqkv_t[...], normed[...], ((1,), (1,))).astype(BF16)
    kv[...] = dot(normed[...], wqkv[:, feat:]).astype(BF16)

    half = tokens // 2
    lane = lax.broadcasted_iota(jnp.int32, (1, tokens), 1)
    edge = ids[0] == 1
    top = jnp.where(jnp.logical_and(edge, lane >= half), MASKED, 0.0).astype(F32)
    low = jnp.where(jnp.logical_and(edge, lane < half), MASKED, 0.0).astype(F32)
    inv_root = 1.0 / math.sqrt(size)
    to_exp2 = inv_root * math.log2(math.e)

    def spread(block, h):
        parts = []
        if h > 0:
            parts.append(jnp.zeros((h * size, tokens), BF16))
        parts.append(block)
        if h < per - 1:
            parts.append(jnp.zeros(((per - 1 - h) * size, tokens), BF16))
        return jnp.concatenate(parts, 0)

    def group(i, carry):
        at = pl.multiple_of(i * 128, 128)
        k4 = kv[:, pl.ds(at, 128)]
        v4 = kv[:, pl.ds(pl.multiple_of(feat + at, 128), 128)]
        for h in range(per):
            row = pl.multiple_of(at + h * size, size)
            q_h = qkv_t[pl.ds(row, size), :]
            k_h = qkv_t[pl.ds(pl.multiple_of(feat + row, size), size), :]
            v_h = qkv_t[pl.ds(pl.multiple_of(2 * feat + row, size), size), :]
            do_h = do_t[pl.ds(row, size), :]
            s = dot(k4, spread(q_h, h))
            s = jnp.concatenate([s[:half] + top, s[half:] + low], 0)
            e = jnp.exp2((s - jnp.max(s, 0, keepdims=True)) * to_exp2)
            p = e * (1.0 / jnp.sum(e, 0, keepdims=True))
            p_low = p.astype(BF16)
            dp = dot(v4, spread(do_h, h))
            delta = jnp.sum(dp * p, 0, keepdims=True)
            ds = (p * (dp - delta) * inv_root).astype(BF16)
            attn_t[pl.ds(row, size), :] = dot(v_h, p_low).astype(BF16)
            d_t[pl.ds(row, size), :] = dot(k_h, ds).astype(BF16)
            d_t[pl.ds(pl.multiple_of(feat + row, size), size), :] = dot(
                q_h, ds, ((1,), (1,))
            ).astype(BF16)
            d_t[pl.ds(pl.multiple_of(2 * feat + row, size), size), :] = dot(
                do_h, p_low, ((1,), (1,))
            ).astype(BF16)
        return carry

    lax.fori_loop(0, HEADS // per, group, 0)

    normed_t = normed[...].T
    core = ids[1]

    def emit(block, value):
        value = value.astype(BF16)
        at = (block % 2) * feat

        @pl.when(core == block // 2)
        def _():
            keep[at : at + feat, :] = value

        @pl.when(core != block // 2)
        def _():
            send[at : at + feat, :] = value

    for block in range(3):
        emit(block, dot(normed_t, d_t[block * feat : (block + 1) * feat, :], ((1,), (1,))))
    emit(3, dot(attn_t[...], g_low[...]))


def tokens_kernel(
    q0, q1, q2, q3, gain, wqkv, wout, attn_t, d_t, o0, o1, o2, o3, wide, back
):
    quads, outs = (q0, q1, q2, q3), (o0, o1, o2, o3)
    rows = q0.shape[1]
    gather_quads(quads, 0, wide)
    tok = wide[...]
    mixed = tok + dot(attn_t[...], wout[...], ((0,), (0,)))
    for j, out in enumerate(outs):
        out[0] = mixed[j * rows : (j + 1) * rows].astype(BF16)
    xhat, inv = normalise(tok)
    back[...] = dot(wqkv[...], d_t[...]).astype(BF16).astype(F32).T
    scaled = back[...] * gain[...]
    inner = (
        scaled
        - jnp.mean(scaled, -1, keepdims=True)
        - xhat * jnp.mean(scaled * xhat, -1, keepdims=True)
    )
    gather_quads(quads, 1, wide)
    grad = wide[...] + inv * inner
    for j, out in enumerate(outs):
        out[1] = grad[j * rows : (j + 1) * rows].astype(BF16)


def shards(tokens, layer_norm_gain, cotangent, w_qkv, w_out):
    _, lat_rows, lon_cols, levels, feat = tokens.shape
    lat_n, lon_n = lax.axis_size(LAT), lax.axis_size(LON)
    quad_tokens = SHIFT * SHIFT * levels
    n_tokens = 4 * quad_tokens
    keep_part, go_part = slice(SHIFT, lat_rows), slice(0, SHIFT)

    def pairs(d_lat, d_lon):
        return [
            (a * lon_n + o, (a + d_lat) % lat_n * lon_n + (o + d_lon) % lon_n)
            for a in range(lat_n)
            for o in range(lon_n)
        ]

    def quad(rows, cols):
        both = jnp.stack([tokens[0, rows, cols], cotangent[0, rows, cols]])
        return both.reshape(2, quad_tokens, feat)

    shifts = ((0, 0), (0, 1), (1, 0), (1, 1))
    cuts = [(go_part if a else keep_part, go_part if o else keep_part) for a, o in shifts]
    with jax.named_scope("window_in"):
        quads = [quad(*cut) for cut in cuts]
        quads = [
            q if s == (0, 0) else lax.ppermute(q, EVERY, pairs(-s[0], -s[1]))
            for q, s in zip(quads, shifts)
        ]
    gain_row = layer_norm_gain[None, :]
    core = lax.axis_index("core")
    ids = jnp.stack([(lax.axis_index(LAT) == lat_n - 1).astype(jnp.int32), core.astype(jnp.int32)])
    vmem = pl.BlockSpec(memory_space=pltpu.VMEM)
    smem = pl.BlockSpec(memory_space=pltpu.SMEM)
    params = pltpu.CompilerParams(vmem_limit_bytes=40 * 1024 * 1024)
    with jax.named_scope("window_grads"):
        keep, send, attn_t, d_t = pl.pallas_call(
            grads_kernel,
            in_specs=[smem] + [vmem] * 8,
            out_specs=[vmem] * 4,
            out_shape=[
                jax.ShapeDtypeStruct((2 * feat, feat), BF16),
                jax.ShapeDtypeStruct((2 * feat, feat), BF16),
                jax.ShapeDtypeStruct((feat, n_tokens), BF16),
                jax.ShapeDtypeStruct((3 * feat, n_tokens), BF16),
            ],
            scratch_shapes=[
                pltpu.VMEM((n_tokens, feat), F32),
                pltpu.VMEM((n_tokens, feat), BF16),
                pltpu.VMEM((n_tokens, feat), BF16),
                pltpu.VMEM((3 * feat, n_tokens), BF16),
                pltpu.VMEM((n_tokens, 2 * feat), BF16),
                pltpu.VMEM((feat, n_tokens), BF16),
            ],
            compiler_params=params,
        )(ids, *quads, gain_row, w_qkv, w_qkv.T, w_out)
    swap = [(0, 1), (1, 0)]
    with jax.named_scope("sum_cores"):
        other = lax.ppermute(send, "core", swap)
    with jax.named_scope("window_tokens"):
        outs = pl.pallas_call(
            tokens_kernel,
            in_specs=[vmem] * 9,
            out_specs=[vmem] * 4,
            out_shape=[jax.ShapeDtypeStruct((2, quad_tokens, feat), BF16)] * 4,
            scratch_shapes=[
                pltpu.VMEM((n_tokens, feat), F32),
                pltpu.VMEM((n_tokens, feat), F32),
            ],
            compiler_params=params,
        )(*quads, gain_row, w_qkv, w_out, attn_t, d_t)
    with jax.named_scope("window_out"):
        outs = [
            q if s == (0, 0) else lax.ppermute(q, EVERY, pairs(s[0], s[1]))
            for q, s in zip(outs, shifts)
        ]
        blocks = [o.reshape(2, SHIFT, SHIFT, levels, feat) for o in outs]
        lower = jnp.concatenate([blocks[1], blocks[0]], 2)
        upper = jnp.concatenate([blocks[3], blocks[2]], 2)
        both = jnp.concatenate([upper, lower], 1)
        mixed, grad_tokens = both[0][None], both[1][None]
    chips = lax.axis_size(CHIPS)
    factor = 1.0 / math.sqrt(lat_n * lat_rows * lon_n * lon_cols * levels)
    with jax.named_scope("sum_chips"):
        pair_sum = (keep.astype(F32) + other.astype(F32)).astype(BF16)
        pieces = lax.all_to_all(pair_sum.reshape(chips, -1, feat), CHIPS, 0, 0)
        piece = (jnp.sum(pieces.astype(F32), 0) * factor).astype(BF16)
    with jax.named_scope("share"):
        mine = lax.all_to_all(jnp.broadcast_to(piece[None], (chips,) + piece.shape), CHIPS, 0, 0)
        mine = mine.reshape(2, feat, feat)
        theirs = lax.ppermute(mine, "core", swap)
        first = jnp.where(core == 0, mine, theirs)
        second = jnp.where(core == 0, theirs, mine)
        grad_qkv = jnp.concatenate([first[0], first[1], second[0]], 1)
        grad_out = second[1]
    gain_gradient = (
        jnp.sum(grad_qkv.astype(F32) * w_qkv.astype(F32), 1) / layer_norm_gain
    )
    return mixed, grad_tokens, gain_gradient, grad_qkv, grad_out


def solution(mesh):
    fine = Mesh(mesh.devices.reshape(2, 4, 8, 2, 2), EVERY)
    grid = P(None, LAT, LON, None, None)
    return jax.shard_map(
        shards,
        mesh=fine,
        in_specs=(grid, P(), grid, P(), P()),
        out_specs=(grid, grid, P(), P(), P()),
        check_vma=False,
    )
```

time: 374 us -> 141 us (0.38)
  waiting for transfers between devices: 188 us -> 12.4 us
  matrix products: 47.9 us -> 0 us
  Pallas kernels: 0 us -> 16.4 us
  between operations: 14.4 us -> 0.79 us
  other arithmetic: 14.1 us -> 6.06 us
  local copies, waits for them, and re-layouts: 15.9 us -> 8.13 us
  starting transfers between devices: 13.4 us -> 20.4 us
    psum x1 -> x0, waiting for transfers between devices: 177 us -> none  [shards(): lax.psum((part_out, part_qkv, partial_gain), ('lat', 'lon'))]
    psum x1 -> x0, blocking collectives: 78.8 us -> none  [shards(): lax.psum((part_out, part_qkv, partial_gain), ('lat', 'lon'))]
    all_to_all x0 -> x2, blocking collectives: none -> 75.1 us  [the longest x1 39.3 us: shards(): pieces = lax.all_to_all(pair_sum.reshape(chips, -1, feat), CHIPS, 0, 0)]
    dot_general x11 -> x0, matrix products: 41.5 us -> none  [the longest x1 12 us: attend_backward(): jnp.einsum('nhqk,nqhd->nkhd', grad_scores, queries, preferred_element_typ...]
    pallas_call x0 -> x2, Pallas kernels: none -> 16.4 us  [the longest x1 14 us: shards(): pl.pallas_call(grads_kernel, in_specs=[smem] + [vmem] * 8, out_specs=[vme...]
    ppermute x8, starting transfers between devices: 13.4 us -> 20.4 us  [the longest x3 13 us: shards(): lax.ppermute(q, EVERY, pairs(-s[0], -s[1]))]
    sub x1 -> x0, matrix products: 6.4 us -> none  [probabilities(): exponent = jnp.exp(scores - row_max)]
    convert_element_type x4 -> x1, other arithmetic: 5.92 us -> 0.01 us  [shards(): piece = (jnp.sum(pieces.astype(F32), 0) * factor).astype(BF16)]
  transfers between devices with their start and end apart: 9 -> 8, of which waited for: 5 -> 3; matrix products, arithmetic and copies ran while one was open for 6% -> 4% of each run, Pallas kernels for 0% -> 2%
where the time goes in v1:
time: 141 us; the launch traced here: 139 us
  blocking collectives  75.1 us (53%)
  starting transfers between devices  20.4 us (14%)
  Pallas kernels  16.4 us (12%)
  waiting for transfers between devices  12.4 us (9%)
  local copies, waits for them, and re-layouts  8.13 us (6%)
  other arithmetic  6.06 us (4%)
    all_to_all x1, blocking collectives, shards(): pieces = lax.all_to_all(pair_sum.reshape(chips, -1, feat), CHIPS, 0, 0)  39.3 us
    all_to_all x1, blocking collectives, shards(): lax.all_to_all(jnp.broadcast_to(piece[None], (chips,) + piece.shape), CHI...  35.8 us
    pallas_call x1, Pallas kernels, shards(): pl.pallas_call(grads_kernel, in_specs=[smem] + [vmem] * 8, out_specs=[vme...  14 us
    ppermute x3, starting transfers between devices, shards(): lax.ppermute(q, EVERY, pairs(-s[0], -s[1]))  13 us
    ppermute x3, waiting for transfers between devices, shards(): lax.ppermute(q, EVERY, pairs(s[0], s[1]))  8.76 us
    ppermute x1, starting transfers between devices, shards(): theirs = lax.ppermute(mine, 'core', swap)  3.38 us
  transfers between devices with their start and end apart: 8, of which 3 were waited for; matrix products, arithmetic and copies ran while one was open for 4% of the time, Pallas kernels for 2%

profile of v1, /device:TPU:1, one launch (start us, length us, event | category | flops | bytes accessed | tf_op | source)
XLA Modules:
  0.0 139.2 jit_solution(16158362475050487448)
XLA Ops:
  0.6 0.0 copy-start
  0.6 1.7 %fusion.2 = (bf16[1,6,6,2,512]{4,3,2,1,0:T(2,128)(2,1)S(1)}, bf16[1,6,6,2,512]{4,3,2,1,0:T(2,128)(2,1)S(1)}, bf16[1,6,6,2,512]{4,3,2,1,0:T(2,128)(2,1)S(1)}, bf1...) fusion(bf16[1,12,12,2,512]{4,3,2,1,0:T(2,128)(2,1)} %param.5, ...), kind=kLoop, calls=%fused_computation.19 | loop fusion | bytes 1179648 | tf_op jit(solution)/shard_map/window_in/slice | solution.py:166
  2.3 0.2 pad_maximum_fusion.3
  2.5 0.7 reshape.46
  3.3 6.0 %collective-permute-start.1 = (bf16[2,72,512]{2,1,0:T(8,128)(2,1)}, bf16[2,72,512]{2,1,0:T(8,128)(2,1)S(1)}, u32[]{:S(2)}, u32[]{:S(2)}) collective-permute-start(bf16[2,72,512]{2,1,0:T(8,128)(2,1)} %reshape.46), channel_id=1, source_target_pairs={{0,224},{1,225},{2,226},{3,227},{4,228},{5,229},{6,230},{7,231},{8... | collective-permute-start | bytes 442376 | tf_op jit(solution)/shard_map/window_in/ppermute | solution.py:174
  9.3 0.2 pad_maximum_fusion.2
  9.5 0.7 reshape.45
  10.2 1.0 collective-permute-start
  11.2 0.2 pad_maximum_fusion.4
  11.4 0.7 reshape.47
  12.1 6.0 %collective-permute-start.2 = (bf16[2,72,512]{2,1,0:T(8,128)(2,1)}, bf16[2,72,512]{2,1,0:T(8,128)(2,1)}, u32[]{:S(2)}, u32[]{:S(2)}) collective-permute-start(bf16[2,72,512]{2,1,0:T(8,128)(2,1)} %reshape.47), channel_id=1, source_target_pairs={{0,255},{1,224},{2,225},{3,226},{4,227},{5,228},{6,229},{7,230},{8... | collective-permute-start | bytes 442376 | tf_op jit(solution)/shard_map/window_in/ppermute | solution.py:174
  18.1 0.2 pad_maximum_fusion.1
  18.3 0.1 reshape.44.q0
  18.4 0.0 copy-start.2
  18.4 0.7 copy.10
  19.1 0.1 pad_add_fusion.ids
  19.2 0.0 collective-permute-done.1.q2
  19.2 0.0 collective-permute-done.q1
  19.2 1.3 collective-permute-done.2.q3
  20.5 1.0 copy-done.1
  21.6 14.0 %window_grads.1 = (bf16[1024,512]{1,0:T(8,128)(2,1)S(1)}, bf16[1024,512]{1,0:T(8,128)(2,1)S(1)}, bf16[512,288]{1,0:T(8,128)(2,1)S(1)}, bf16[1536,288]{1,0:T(8,128)(2,1)S(1)}) custom-call(s32[2]{0:T(128)S(1)} %pad_add_fusion.ids, bf16[2,72,512]{2,1,0:T(8,128)(2,1)S(1)} %reshape.44.q0, bf16[2,72,512]{2,1,0:T(8,128)(2,1)} %collective-permute-done.q1, ...), custom_call_target="tpu_custom_call" | custom-call | tf_op jit(solution)/shard_map/window_grads/pallas_call | solution.py:184
  35.5 1.6 %collective-permute-start.6 = (bf16[1024,512]{1,0:T(8,128)(2,1)S(1)}, bf16[1024,512]{1,0:T(8,128)(2,1)S(1)}, u32[]{:S(2)}, u32[]{:S(2)}) collective-permute-start(bf16[1024,512]{1,0:T(8,128)(2,1)S(1)} %get-tuple-element.20), channel_id=1, source_target_pairs={{0,1},{1,0},{2,3},{3,2},{4,5},{5,4},{6,7},{7,6},{8,9},{9,8},{10,11... | collective-permute-start | bytes 3145736 | tf_op jit(solution)/shard_map/sum_cores/ppermute | solution.py:206
  37.1 2.3 %collective-permute-done.6 = bf16[1024,512]{1,0:T(8,128)(2,1)S(1)} collective-permute-done((bf16[1024,512]{1,0:T(8,128)(2,1)S(1)}, bf16[1024,512]{1,0:T(8,128)(2,1)S(1)}, u32[]{:S(2)}, u32[]{:S(2)}) %collective-permute-start.6) | collective-permute-done | bytes 1048608 | tf_op jit(solution)/shard_map/sum_cores/ppermute | solution.py:206
  39.4 0.3 fusion
  39.7 39.3 %all_to_all.10 = bf16[128,8,512]{2,1,0:T(8,128)(2,1)S(1)} all-to-all(bf16[128,8,512]{2,1,0:T(8,128)(2,1)S(1)} %fusion), channel_id=1, replica_groups=mesh['xh'=2,'y'=4,'z'=8,'xl'=2,'core'=2] {'xh','y','z','xl'}, dimensions={0} | all-to-all | bytes 2097152 | tf_op jit(solution)/shard_map/sum_chips/all_to_all | solution.py:233
  79.1 0.2 convert_reduce_fusion
  79.3 0.1 broadcast_in_dim.10
  79.3 35.8 %all_to_all.11 = bf16[128,8,512]{2,1,0:T(8,128)(2,1)} all-to-all(bf16[128,8,512]{2,1,0:T(8,128)(2,1)S(1)} %broadcast_in_dim.10), channel_id=1, replica_groups=mesh['xh'=2,'y'=4,'z'=8,'xl'=2,'core'=2] {'xh','y','z','xl'}, dimensions={0} | all-to-all | bytes 2097152 | tf_op jit(solution)/shard_map/share/all_to_all | solution.py:236
  115.1 3.4 %collective-permute-start.7 = (bf16[2,512,512]{2,1,0:T(8,128)(2,1)}, bf16[2,512,512]{2,1,0:T(8,128)(2,1)}, u32[]{:S(2)}, u32[]{:S(2)}) collective-permute-start(bf16[2,512,512]{2,1,0:T(8,128)(2,1)} %bitcast.5), channel_id=1, source_target_pairs={{0,1},{1,0},{2,3},{3,2},{4,5},{5,4},{6,7},{7,6},{8,9},{9,8},{10,11... | collective-permute-start | bytes 3145736 | tf_op jit(solution)/shard_map/share/ppermute | solution.py:238
  118.5 2.4 %window_tokens.1 = (bf16[2,72,512]{2,1,0:T(8,128)(2,1)S(1)}, bf16[2,72,512]{2,1,0:T(8,128)(2,1)S(1)}, bf16[2,72,512]{2,1,0:T(8,128)(2,1)S(1)}, bf16[2,72,512]{2,1,0:T(8,128)(2,1)S(1)}) custom-call(bf16[2,72,512]{2,1,0:T(8,128)(2,1)S(1)} %reshape.44.q0, bf16[2,72,512]{2,1,0:T(8,128)(2,1)} %collective-permute-done.q1, ...), custom_call_target="tpu_custom_call" | custom-call | tf_op jit(solution)/shard_map/window_tokens/pallas_call | solution.py:208
  120.9 0.5 collective-permute-start.3
  121.4 1.0 collective-permute-start.4
  122.4 1.0 collective-permute-start.5
  123.4 0.1 reshape.51
  123.4 8.8 %collective-permute-done.3 = bf16[2,72,512]{2,1,0:T(8,128)(2,1)S(1)} collective-permute-done((bf16[2,72,512]{2,1,0:T(8,128)(2,1)S(1)}, bf16[2,72,512]{2,1,0:T(8,128)(2,1)S(1)}, u32[]{:S(2)}, u32[]{:S(2)}) %collective-permute-start.3) | collective-permute-done | bytes 147488 | tf_op jit(solution)/shard_map/window_out/ppermute | solution.py:221
  132.2 0.1 reshape.48
  132.2 0.0 collective-permute-done.4
  132.2 0.1 reshape.49
  132.3 0.0 collective-permute-done.5
  132.3 0.1 reshape.50
  132.4 0.8 maximum_maximum_fusion
  133.2 1.2 fusion.1
  134.5 0.0 collective-permute-done.7
  134.5 1.7 %broadcast_select_fusion.1 = (bf16[2,512,512]{2,1,0:T(8,128)(2,1)S(1)}, bf16[2,512,512]{2,1,0:T(8,128)(2,1)S(1)}) fusion(bf16[2,512,512]{2,1,0:T(8,128)(2,1)} %collective-permute-done.7, pred[]{:T(512)S(6)} %eq.8, bf16[2,512,512]{2,1,0:T(8,128)(2,1)} %bitcast.17), kind=kLoop, calls=%fused_computation.6 | loop fusion | flops 1048576 | bytes 4194305 | tf_op jit(solution)/shard_map/share/jit(_where)/select_n | solution.py:239
  136.1 0.1 slice_bitcast_fusion.3
  136.2 0.9 slice_bitcast_fusion
  137.1 1.5 %multiply_reduce_fusion = (f32[512]{0:T(512)S(1)}, bf16[512,1536]{1,0:T(8,128)(2,1)}) fusion(bf16[512,1536]{1,0:T(8,128)(2,1)S(1)} %copy-done, bf16[512,512]{1,0:T(8,128)(2,1)S(1)} %get-tuple-element.26, bf16[512,512]{1,0:T(8,128)(2,1)S(1)} %get-tuple-element.28, bf16[512,512]{1,0:T(8,128)(2,1)S(1)} %get-tuple-element.27), kind=kLoop, calls=%fused_computation | loop fusion | flops 7863808 | bytes 4720640 | tf_op jit(solution)/shard_map/reduce_sum | solution.py:244
  138.6 0.6 div.3
  (4 shorter events, 0.0 us)
Async XLA Ops:
  0.6 17.8 %copy-start = (bf16[512,1536]{1,0:T(8,128)(2,1)S(1)}, bf16[512,1536]{1,0:T(8,128)(2,1)}, u32[]{:S(2)}) copy-start(bf16[512,1536]{1,0:T(8,128)(2,1)} %wqkv.3) | copy-start | bytes 4718596
  3.3 16.0 %collective-permute-start.1 = (bf16[2,72,512]{2,1,0:T(8,128)(2,1)}, bf16[2,72,512]{2,1,0:T(8,128)(2,1)S(1)}, u32[]{:S(2)}, u32[]{:S(2)}) collective-permute-start(bf16[2,72,512]{2,1,0:T(8,128)(2,1)} %reshape.46), channel_id=1, source_target_pairs={{0,224},{1,225},{2,226},{3,227},{4,228},{5,229},{6,230},{7,231},{8... | collective-permute-start | bytes 442376 | tf_op jit(solution)/shard_map/window_in/ppermute | solution.py:174
  10.2 9.0 %collective-permute-start = (bf16[2,72,512]{2,1,0:T(8,128)(2,1)}, bf16[2,72,512]{2,1,0:T(8,128)(2,1)}, u32[]{:S(2)}, u32[]{:S(2)}) collective-permute-start(bf16[2,72,512]{2,1,0:T(8,128)(2,1)} %reshape.45), channel_id=1, source_target_pairs={{0,31},{1,0},{2,1},{3,2},{4,3},{5,4},{6,5},{7,6},{8,7},{9,8},{10,9... | collective-permute-start | bytes 442376 | tf_op jit(solution)/shard_map/window_in/ppermute | solution.py:174
  12.1 8.4 %collective-permute-start.2 = (bf16[2,72,512]{2,1,0:T(8,128)(2,1)}, bf16[2,72,512]{2,1,0:T(8,128)(2,1)}, u32[]{:S(2)}, u32[]{:S(2)}) collective-permute-start(bf16[2,72,512]{2,1,0:T(8,128)(2,1)} %reshape.47), channel_id=1, source_target_pairs={{0,255},{1,224},{2,225},{3,226},{4,227},{5,228},{6,229},{7,230},{8... | collective-permute-start | bytes 442376 | tf_op jit(solution)/shard_map/window_in/ppermute | solution.py:174
  18.4 2.1 %copy-start.2 = (f32[512]{0:T(512)S(1)}, f32[512]{0:T(512)}, u32[]{:S(2)}) copy-start(f32[512]{0:T(512)} %param.6) | copy-start | bytes 6148
  20.5 1.0 copy-start.1
  35.5 3.9 %collective-permute-start.6 = (bf16[1024,512]{1,0:T(8,128)(2,1)S(1)}, bf16[1024,512]{1,0:T(8,128)(2,1)S(1)}, u32[]{:S(2)}, u32[]{:S(2)}) collective-permute-start(bf16[1024,512]{1,0:T(8,128)(2,1)S(1)} %get-tuple-element.20), channel_id=1, source_target_pairs={{0,1},{1,0},{2,3},{3,2},{4,5},{5,4},{6,7},{7,6},{8,9},{9,8},{10,11... | collective-permute-start | bytes 3145736 | tf_op jit(solution)/shard_map/sum_cores/ppermute | solution.py:206
  115.1 19.4 %collective-permute-start.7 = (bf16[2,512,512]{2,1,0:T(8,128)(2,1)}, bf16[2,512,512]{2,1,0:T(8,128)(2,1)}, u32[]{:S(2)}, u32[]{:S(2)}) collective-permute-start(bf16[2,512,512]{2,1,0:T(8,128)(2,1)} %bitcast.5), channel_id=1, source_target_pairs={{0,1},{1,0},{2,3},{3,2},{4,5},{5,4},{6,7},{7,6},{8,9},{9,8},{10,11... | collective-permute-start | bytes 3145736 | tf_op jit(solution)/shard_map/share/ppermute | solution.py:238
  120.9 11.3 %collective-permute-start.3 = (bf16[2,72,512]{2,1,0:T(8,128)(2,1)S(1)}, bf16[2,72,512]{2,1,0:T(8,128)(2,1)S(1)}, u32[]{:S(2)}, u32[]{:S(2)}) collective-permute-start(bf16[2,72,512]{2,1,0:T(8,128)(2,1)S(1)} %get-tuple-element.15), channel_id=1, source_target_pairs={{0,33},{1,34},{2,35},{3,36},{4,37},{5,38},{6,39},{7,40},{8,41},{9,... | collective-permute-start | bytes 442376 | tf_op jit(solution)/shard_map/window_out/ppermute | solution.py:221
  121.4 10.8 %collective-permute-start.4 = (bf16[2,72,512]{2,1,0:T(8,128)(2,1)S(1)}, bf16[2,72,512]{2,1,0:T(8,128)(2,1)S(1)}, u32[]{:S(2)}, u32[]{:S(2)}) collective-permute-start(bf16[2,72,512]{2,1,0:T(8,128)(2,1)S(1)} %get-tuple-element.16), channel_id=1, source_target_pairs={{0,32},{1,33},{2,34},{3,35},{4,36},{5,37},{6,38},{7,39},{8,40},{9,... | collective-permute-start | bytes 442376 | tf_op jit(solution)/shard_map/window_out/ppermute | solution.py:221
  122.4 9.9 %collective-permute-start.5 = (bf16[2,72,512]{2,1,0:T(8,128)(2,1)S(1)}, bf16[2,72,512]{2,1,0:T(8,128)(2,1)S(1)}, u32[]{:S(2)}, u32[]{:S(2)}) collective-permute-start(bf16[2,72,512]{2,1,0:T(8,128)(2,1)S(1)} %get-tuple-element.17), channel_id=1, source_target_pairs={{0,1},{1,2},{2,3},{3,4},{4,5},{5,6},{6,7},{7,8},{8,9},{9,10},{10,1... | collective-permute-start | bytes 442376 | tf_op jit(solution)/shard_map/window_out/ppermute | solution.py:221

commit v2 on v1

--- a/solution.py
+++ b/solution.py
@@ -1,3 +1,4 @@
+import functools
 import math
 
 import jax
@@ -17,8 +18,9 @@
 BF16 = jnp.bfloat16
 
 LAT = ("xh", "y")
-LON = ("z", "xl", "core")
-CHIPS = ("xh", "y", "z", "xl")
+LON = ("zh", "zl", "xl", "core")
+NEAR = ("xh", "y", "zl", "xl")
+FAR = "zh"
 EVERY = LAT + LON
 
 
@@ -39,10 +41,25 @@
         out[j * rows : (j + 1) * rows, :] = ref[which].astype(F32)
 
 
+def lanes(shape):
+    return lax.broadcasted_iota(jnp.int32, shape, len(shape) - 1)
+
+
+def split_low(value, terms):
+    lane = lanes(value.shape)
+    out = jnp.zeros_like(value)
+    rest = value
+    for i in range(terms):
+        part = rest.astype(BF16).astype(F32)
+        out = jnp.where(lane == i, part, out)
+        rest = rest - part
+    return out.astype(BF16)
+
+
 def grads_kernel(
     ids, q0, q1, q2, q3, gain, wqkv, wqkv_t, wout,
-    keep, send, attn_t, d_t,
-    wide, normed, g_low, qkv_t, kv, do_t,
+    keep, send, attn_t, back,
+    wide, normed, g_low, qkv_t, kv, do_t, d_t, normed_t, gain_col,
 ):
     quads = (q0, q1, q2, q3)
     tokens, feat = normed.shape
@@ -53,12 +70,14 @@
     do_t[...] = dot(wout[...], g_low[...], ((1,), (1,))).astype(BF16)
     gather_quads(quads, 0, wide)
     xhat, _ = normalise(wide[...])
+    wide[...] = xhat
     normed[...] = (xhat * gain[...]).astype(BF16)
+    normed_t[...] = normed[...].T
     qkv_t[...] = dot(wqkv_t[...], normed[...], ((1,), (1,))).astype(BF16)
     kv[...] = dot(normed[...], wqkv[:, feat:]).astype(BF16)
 
     half = tokens // 2
-    lane = lax.broadcasted_iota(jnp.int32, (1, tokens), 1)
+    lane = lanes((1, tokens))
     edge = ids[0] == 1
     top = jnp.where(jnp.logical_and(edge, lane >= half), MASKED, 0.0).astype(F32)
     low = jnp.where(jnp.logical_and(edge, lane < half), MASKED, 0.0).astype(F32)
@@ -104,29 +123,26 @@
 
     lax.fori_loop(0, HEADS // per, group, 0)
 
-    normed_t = normed[...].T
-    core = ids[1]
-
-    def emit(block, value):
-        value = value.astype(BF16)
-        at = (block % 2) * feat
-
-        @pl.when(core == block // 2)
-        def _():
-            keep[at : at + feat, :] = value
-
-        @pl.when(core != block // 2)
-        def _():
-            send[at : at + feat, :] = value
-
+    back[...] = dot(wqkv[...], d_t[...]).astype(BF16).astype(F32).T.astype(BF16)
+    part_gain = jnp.sum(back[...].astype(F32) * wide[...], 0, keepdims=True)
+    column = jnp.broadcast_to(part_gain, (128, feat)).T
+    gain_col[...] = jnp.where(lanes(column.shape) == 0, column, 0.0)
+
+    rows = feat // 2
+    mine = pl.multiple_of(ids[1] * rows, rows)
+    theirs = pl.multiple_of((1 - ids[1]) * rows, rows)
     for block in range(3):
-        emit(block, dot(normed_t, d_t[block * feat : (block + 1) * feat, :], ((1,), (1,))))
-    emit(3, dot(attn_t[...], g_low[...]))
-
-
-def tokens_kernel(
-    q0, q1, q2, q3, gain, wqkv, wout, attn_t, d_t, o0, o1, o2, o3, wide, back
-):
+        at = slice(block * feat, (block + 1) * feat)
+        send[:, at] = dot(normed_t[pl.ds(theirs, rows), :], d_t[at, :], ((1,), (1,))).astype(BF16)
+        keep[:, at] = dot(normed_t[pl.ds(mine, rows), :], d_t[at, :], ((1,), (1,)))
+    at = slice(3 * feat, 4 * feat)
+    send[:, at] = dot(attn_t[pl.ds(theirs, rows), :], g_low[...]).astype(BF16)
+    keep[:, at] = dot(attn_t[pl.ds(mine, rows), :], g_low[...])
+    send[:, 4 * feat :] = split_low(gain_col[pl.ds(theirs, rows), :], 2)
+    keep[:, 4 * feat :] = gain_col[pl.ds(mine, rows), :]
+
+
+def tokens_kernel(q0, q1, q2, q3, gain, wout, attn_t, back, o0, o1, o2, o3, wide):
     quads, outs = (q0, q1, q2, q3), (o0, o1, o2, o3)
     rows = q0.shape[1]
     gather_quads(quads, 0, wide)
@@ -135,8 +151,7 @@
     for j, out in enumerate(outs):
         out[0] = mixed[j * rows : (j + 1) * rows].astype(BF16)
     xhat, inv = normalise(tok)
-    back[...] = dot(wqkv[...], d_t[...]).astype(BF16).astype(F32).T
-    scaled = back[...] * gain[...]
+    scaled = back[...].astype(F32) * gain[...]
     inner = (
         scaled
         - jnp.mean(scaled, -1, keepdims=True)
@@ -146,6 +161,48 @@
     grad = wide[...] + inv * inner
     for j, out in enumerate(outs):
         out[1] = grad[j * rows : (j + 1) * rows].astype(BF16)
+
+
+def gain_total(tile):
+    return jnp.where(lanes(tile.shape) == 0, jnp.sum(tile, -1, keepdims=True), 0.0)
+
+
+def pair_kernel(keep, other, out):
+    main = keep.shape[1] - 128
+    out[:, :main] = (keep[:, :main] + other[:, :main].astype(F32)).astype(BF16)
+    out[:, main:] = split_low(gain_total(keep[:, main:] + other[:, main:].astype(F32)), 2)
+
+
+def piece_kernel(pieces, out):
+    out[...] = jnp.sum(pieces[...].astype(F32), 0)
+
+
+def final_piece_kernel(factor, mine, p1, p2, p3, out):
+    main = mine.shape[1] - 128
+    total = (mine[...] + p1[...] + p2[...] + p3[...]) * factor
+    out[:, :main] = total[:, :main].astype(BF16)
+    out[:, main:] = split_low(gain_total(total[:, main:]), 3)
+
+
+def finish_kernel(ids, mine, theirs, grad_qkv, grad_out, gain_grad, sems):
+    rows = mine.shape[0]
+    wide = grad_qkv.shape[1]
+    main = wide + grad_out.shape[1]
+    copies = []
+    for n, ref in enumerate((mine, theirs)):
+        at = pl.multiple_of((ids[1] if n == 0 else 1 - ids[1]) * rows, rows)
+        for m, (dst, cols) in enumerate(
+            ((grad_qkv, slice(0, wide)), (grad_out, slice(wide, main)))
+        ):
+            copy = pltpu.make_async_copy(
+                ref.at[:, cols], dst.at[pl.ds(at, rows), :], sems.at[2 * n + m]
+            )
+            copy.start()
+            copies.append(copy)
+        column = ref[:, main:].astype(F32).T
+        gain_grad[:, pl.ds(at, rows)] = column[0:1] + column[1:2] + column[2:3]
+    for copy in copies:
+        copy.wait()
 
 
 def shards(tokens, layer_norm_gain, cotangent, w_qkv, w_out):
@@ -179,17 +236,19 @@
     ids = jnp.stack([(lax.axis_index(LAT) == lat_n - 1).astype(jnp.int32), core.astype(jnp.int32)])
     vmem = pl.BlockSpec(memory_space=pltpu.VMEM)
     smem = pl.BlockSpec(memory_space=pltpu.SMEM)
+    hbm = pl.BlockSpec(memory_space=pl.ANY)
     params = pltpu.CompilerParams(vmem_limit_bytes=40 * 1024 * 1024)
+    rows, width = feat // 2, 4 * feat + 128
     with jax.named_scope("window_grads"):
-        keep, send, attn_t, d_t = pl.pallas_call(
+        keep, send, attn_t, back = pl.pallas_call(
             grads_kernel,
             in_specs=[smem] + [vmem] * 8,
             out_specs=[vmem] * 4,
             out_shape=[
-                jax.ShapeDtypeStruct((2 * feat, feat), BF16),
-                jax.ShapeDtypeStruct((2 * feat, feat), BF16),
+                jax.ShapeDtypeStruct((rows, width), F32),
+                jax.ShapeDtypeStruct((rows, width), BF16),
                 jax.ShapeDtypeStruct((feat, n_tokens), BF16),
-                jax.ShapeDtypeStruct((3 * feat, n_tokens), BF16),
+                jax.ShapeDtypeStruct((n_tokens, feat), BF16),
             ],
             scratch_shapes=[
                 pltpu.VMEM((n_tokens, feat), F32),
@@ -198,6 +257,9 @@
                 pltpu.VMEM((3 * feat, n_tokens), BF16),
                 pltpu.VMEM((n_tokens, 2 * feat), BF16),
                 pltpu.VMEM((feat, n_tokens), BF16),
+                pltpu.VMEM((3 * feat, n_tokens), BF16),
+                pltpu.VMEM((feat, n_tokens), BF16),
+                pltpu.VMEM((feat, 128), F32),
             ],
             compiler_params=params,
         )(ids, *quads, gain_row, w_qkv, w_qkv.T, w_out)
@@ -207,47 +269,78 @@
     with jax.named_scope("window_tokens"):
         outs = pl.pallas_call(
             tokens_kernel,
-            in_specs=[vmem] * 9,
+            in_specs=[vmem] * 8,
             out_specs=[vmem] * 4,
             out_shape=[jax.ShapeDtypeStruct((2, quad_tokens, feat), BF16)] * 4,
-            scratch_shapes=[
-                pltpu.VMEM((n_tokens, feat), F32),
-                pltpu.VMEM((n_tokens, feat), F32),
-            ],
-            compiler_params=params,
-        )(*quads, gain_row, w_qkv, w_out, attn_t, d_t)
+            scratch_shapes=[pltpu.VMEM((n_tokens, feat), F32)],
+            compiler_params=params,
+        )(*quads, gain_row, w_out, attn_t, back)
+    with jax.named_scope("sum_cores"):
+        pair_sum = pl.pallas_call(
+            pair_kernel,
+            in_specs=[vmem] * 2,
+            out_specs=vmem,
+            out_shape=jax.ShapeDtypeStruct((rows, width), BF16),
+            compiler_params=params,
+        )(keep, other)
+    pair_sum, *outs = lax.optimization_barrier((pair_sum, *outs))
     with jax.named_scope("window_out"):
         outs = [
             q if s == (0, 0) else lax.ppermute(q, EVERY, pairs(s[0], s[1]))
             for q, s in zip(outs, shifts)
         ]
+    near, far = lax.axis_size(NEAR), lax.axis_size(FAR)
+    factor = 1.0 / math.sqrt(lat_n * lat_rows * lon_n * lon_cols * levels)
+    with jax.named_scope("sum_near"):
+        pieces = lax.all_to_all(pair_sum.reshape(near, rows // near, width), NEAR, 0, 0)
+        pieces, *outs = lax.optimization_barrier((pieces, *outs))
+        piece = pl.pallas_call(
+            piece_kernel,
+            in_specs=[vmem],
+            out_specs=vmem,
+            out_shape=jax.ShapeDtypeStruct((rows // near, width), F32),
+            compiler_params=params,
+        )(pieces)
+    with jax.named_scope("window_out"):
         blocks = [o.reshape(2, SHIFT, SHIFT, levels, feat) for o in outs]
         lower = jnp.concatenate([blocks[1], blocks[0]], 2)
         upper = jnp.concatenate([blocks[3], blocks[2]], 2)
         both = jnp.concatenate([upper, lower], 1)
         mixed, grad_tokens = both[0][None], both[1][None]
-    chips = lax.axis_size(CHIPS)
-    factor = 1.0 / math.sqrt(lat_n * lat_rows * lon_n * lon_cols * levels)
-    with jax.named_scope("sum_chips"):
-        pair_sum = (keep.astype(F32) + other.astype(F32)).astype(BF16)
-        pieces = lax.all_to_all(pair_sum.reshape(chips, -1, feat), CHIPS, 0, 0)
-        piece = (jnp.sum(pieces.astype(F32), 0) * factor).astype(BF16)
+    with jax.named_scope("sum_far"):
+        others = [
+            lax.ppermute(piece, FAR, [(i, (i + by) % far) for i in range(far)])
+            for by in range(1, far)
+        ]
+        piece = pl.pallas_call(
+            functools.partial(final_piece_kernel, factor),
+            in_specs=[vmem] * far,
+            out_specs=vmem,
+            out_shape=jax.ShapeDtypeStruct((rows // near, width), BF16),
+            compiler_params=params,
+        )(piece, *others)
     with jax.named_scope("share"):
-        mine = lax.all_to_all(jnp.broadcast_to(piece[None], (chips,) + piece.shape), CHIPS, 0, 0)
-        mine = mine.reshape(2, feat, feat)
+        mine = lax.all_to_all(jnp.broadcast_to(piece[None], (near,) + piece.shape), NEAR, 0, 0)
+        mine = mine.reshape(rows, width)
         theirs = lax.ppermute(mine, "core", swap)
-        first = jnp.where(core == 0, mine, theirs)
-        second = jnp.where(core == 0, theirs, mine)
-        grad_qkv = jnp.concatenate([first[0], first[1], second[0]], 1)
-        grad_out = second[1]
-    gain_gradient = (
-        jnp.sum(grad_qkv.astype(F32) * w_qkv.astype(F32), 1) / layer_norm_gain
-    )
-    return mixed, grad_tokens, gain_gradient, grad_qkv, grad_out
+    with jax.named_scope("finish"):
+        grad_qkv, grad_out, gain_gradient = pl.pallas_call(
+            finish_kernel,
+            in_specs=[smem, vmem, vmem],
+            out_specs=[hbm, hbm, vmem],
+            out_shape=[
+                jax.ShapeDtypeStruct((feat, 3 * feat), BF16),
+                jax.ShapeDtypeStruct((feat, feat), BF16),
+                jax.ShapeDtypeStruct((1, feat), F32),
+            ],
+            scratch_shapes=[pltpu.SemaphoreType.DMA((4,))],
+            compiler_params=params,
+        )(ids, mine, theirs)
+    return mixed, grad_tokens, gain_gradient[0], grad_qkv, grad_out
 
 
 def solution(mesh):
-    fine = Mesh(mesh.devices.reshape(2, 4, 8, 2, 2), EVERY)
+    fine = Mesh(mesh.devices.reshape(2, 4, 4, 2, 2, 2), EVERY)
     grid = P(None, LAT, LON, None, None)
     return jax.shard_map(
         shards,

time: 141 us -> 114 us (0.81)
  blocking collectives: 75.1 us -> 20.9 us
  waiting for transfers between devices: 12.4 us -> 29 us
  starting transfers between devices: 20.4 us -> 33.7 us
  other arithmetic: 6.06 us -> 1.75 us
  Pallas kernels: 16.4 us -> 19.9 us
    all_to_all x2 -> x1, blocking collectives: 75.1 us -> 20.9 us  [shards(): lax.all_to_all(jnp.broadcast_to(piece[None], (near,) + piece.shape), NEAR...]
    ppermute x3, waiting for transfers between devices: 8.76 us -> 20.2 us  [shards(): lax.ppermute(q, EVERY, pairs(s[0], s[1]))]
    ppermute x0 -> x3, waiting for transfers between devices: none -> 6.63 us  [shards(): lax.ppermute(piece, FAR, [(i, (i + by) % far) for i in range(far)])]
    all_to_all x0 -> x1, starting transfers between devices: none -> 6.35 us  [shards(): lax.all_to_all(pair_sum.reshape(near, rows // near, width), NEAR, 0, 0)]
    ppermute x0 -> x3, starting transfers between devices: none -> 6.15 us  [shards(): lax.ppermute(piece, FAR, [(i, (i + by) % far) for i in range(far)])]
    pallas_call x1 -> x5, Pallas kernels: 2.42 us -> 5.81 us  [the longest x1 2.46 us: shards(): pl.pallas_call(finish_kernel, in_specs=[smem, vmem, vmem], out_specs=[hbm...]
    ppermute x3, starting transfers between devices: 2.46 us -> 4.76 us  [shards(): lax.ppermute(q, EVERY, pairs(s[0], s[1]))]
    reduce_sum x2 -> x0, other arithmetic: 1.73 us -> none  [the longest x1 1.54 us: shards(): jnp.sum(grad_qkv.astype(F32) * w_qkv.astype(F32), 1) / layer_norm_gain]
  transfers between devices with their start and end apart: 8 -> 12, of which waited for: 3 -> 7; matrix products, arithmetic and copies ran while one was open for 4% -> 5% of each run, Pallas kernels for 2% -> 1%
where the time goes in v2:
time: 114 us; the launch traced here: 113 us
  starting transfers between devices  33.7 us (30%)
  waiting for transfers between devices  29 us (25%)
  blocking collectives  20.9 us (18%)
  Pallas kernels  19.9 us (17%)
  local copies, waits for them, and re-layouts  7.1 us (6%)
  other arithmetic  1.75 us (2%)
    all_to_all x1, blocking collectives, shards(): lax.all_to_all(jnp.broadcast_to(piece[None], (near,) + piece.shape), NEAR...  20.9 us
    ppermute x3, waiting for transfers between devices, shards(): lax.ppermute(q, EVERY, pairs(s[0], s[1]))  20.2 us
    pallas_call x1, Pallas kernels, shards(): pl.pallas_call(grads_kernel, in_specs=[smem] + [vmem] * 8, out_specs=[vme...  14.1 us
    ppermute x3, starting transfers between devices, shards(): lax.ppermute(q, EVERY, pairs(-s[0], -s[1]))  13 us
    ppermute x3, waiting for transfers between devices, shards(): lax.ppermute(piece, FAR, [(i, (i + by) % far) for i in range(far)])  6.63 us
    all_to_all x1, starting transfers between devices, shards(): lax.all_to_all(pair_sum.reshape(near, rows // near, width), NEAR, 0, 0)  6.35 us
    ppermute x3, starting transfers between devices, shards(): lax.ppermute(piece, FAR, [(i, (i + by) % far) for i in range(far)])  6.15 us
    ppermute x3, starting transfers between devices, shards(): lax.ppermute(q, EVERY, pairs(s[0], s[1]))  4.76 us
  transfers between devices with their start and end apart: 12, of which 7 were waited for; matrix products, arithmetic and copies ran while one was open for 5% of the time, Pallas kernels for 1%

profile of v2, /device:TPU:1, one launch (start us, length us, event | category | flops | bytes accessed | tf_op | source)
XLA Modules:
  0.0 113.4 jit_solution(12373083166891345009)
XLA Ops:
  0.6 1.6 %fusion.1 = (bf16[1,6,6,2,512]{4,3,2,1,0:T(2,128)(2,1)S(1)}, bf16[1,6,6,2,512]{4,3,2,1,0:T(2,128)(2,1)S(1)}, bf16[1,6,6,2,512]{4,3,2,1,0:T(2,128)(2,1)S(1)}, bf1...) fusion(bf16[1,12,12,2,512]{4,3,2,1,0:T(2,128)(2,1)} %param.5, ...), kind=kLoop, calls=%fused_computation.7 | loop fusion | bytes 1179648 | tf_op jit(solution)/shard_map/window_in/slice | solution.py:223
  2.2 0.2 pad_maximum_fusion.2
  2.4 0.0 copy-start
  2.4 0.7 reshape.43
  3.1 6.0 %collective-permute-start.1 = (bf16[2,72,512]{2,1,0:T(8,128)(2,1)}, bf16[2,72,512]{2,1,0:T(8,128)(2,1)S(1)}, u32[]{:S(2)}, u32[]{:S(2)}) collective-permute-start(bf16[2,72,512]{2,1,0:T(8,128)(2,1)} %reshape.43), channel_id=1, source_target_pairs={{0,224},{1,225},{2,226},{3,227},{4,228},{5,229},{6,230},{7,231},{8... | collective-permute-start | bytes 442376 | tf_op jit(solution)/shard_map/window_in/ppermute | solution.py:231
  9.2 0.2 pad_maximum_fusion.1
  9.4 0.7 reshape.42
  10.1 1.0 collective-permute-start
  11.1 0.2 pad_maximum_fusion.3
  11.3 0.7 reshape.44
  12.0 6.0 %collective-permute-start.2 = (bf16[2,72,512]{2,1,0:T(8,128)(2,1)}, bf16[2,72,512]{2,1,0:T(8,128)(2,1)}, u32[]{:S(2)}, u32[]{:S(2)}) collective-permute-start(bf16[2,72,512]{2,1,0:T(8,128)(2,1)} %reshape.44), channel_id=1, source_target_pairs={{0,255},{1,224},{2,225},{3,226},{4,227},{5,228},{6,229},{7,230},{8... | collective-permute-start | bytes 442376 | tf_op jit(solution)/shard_map/window_in/ppermute | solution.py:231
  18.0 0.2 pad_maximum_fusion
  18.2 0.1 reshape.41.q0
  18.3 0.0 copy-start.3
  18.3 0.7 copy.10
  19.0 0.1 pad_add_fusion.ids
  19.1 1.3 %collective-permute-done.2.q3 = bf16[2,72,512]{2,1,0:T(8,128)(2,1)} collective-permute-done((bf16[2,72,512]{2,1,0:T(8,128)(2,1)}, bf16[2,72,512]{2,1,0:T(8,128)(2,1)}, u32[]{:S(2)}, u32[]{:S(2)}) %collective-permute-start.2) | collective-permute-done | bytes 147488 | tf_op jit(solution)/shard_map/window_in/ppermute | solution.py:231
  20.4 1.0 copy-done.1
  21.5 14.1 %window_grads.1 = (f32[256,2176]{1,0:T(8,128)S(1)}, bf16[256,2176]{1,0:T(8,128)(2,1)S(1)}, bf16[512,288]{1,0:T(8,128)(2,1)S(1)}, bf16[288,512]{1,0:T(8,128)(2,1)S(1)}) custom-call(s32[2]{0:T(128)S(1)} %pad_add_fusion.ids, bf16[2,72,512]{2,1,0:T(8,128)(2,1)S(1)} %reshape.41.q0, bf16[2,72,512]{2,1,0:T(8,128)(2,1)} %collective-permute-done.q1, ...), custom_call_target="tpu_custom_call" | custom-call | tf_op jit(solution)/shard_map/window_grads/pallas_call | solution.py:243
  35.5 1.6 %collective-permute-start.3 = (bf16[256,2176]{1,0:T(8,128)(2,1)S(1)}, bf16[256,2176]{1,0:T(8,128)(2,1)S(1)}, u32[]{:S(2)}, u32[]{:S(2)}) collective-permute-start(bf16[256,2176]{1,0:T(8,128)(2,1)S(1)} %get-tuple-element.27), channel_id=1, source_target_pairs={{0,1},{1,0},{2,3},{3,2},{4,5},{5,4},{6,7},{7,6},{8,9},{9,8},{10,11... | collective-permute-start | bytes 3342344 | tf_op jit(solution)/shard_map/sum_cores/ppermute | solution.py:268
  37.1 1.6 %window_tokens.1 = (bf16[2,72,512]{2,1,0:T(8,128)(2,1)S(1)}, bf16[2,72,512]{2,1,0:T(8,128)(2,1)S(1)}, bf16[2,72,512]{2,1,0:T(8,128)(2,1)S(1)}, bf16[2,72,512]{2,1,0:T(8,128)(2,1)S(1)}) custom-call(bf16[2,72,512]{2,1,0:T(8,128)(2,1)S(1)} %reshape.41.q0, bf16[2,72,512]{2,1,0:T(8,128)(2,1)} %collective-permute-done.q1, ...), custom_call_target="tpu_custom_call" | custom-call | tf_op jit(solution)/shard_map/window_tokens/pallas_call | solution.py:270
  38.7 0.8 collective-permute-done.3.other
  39.5 1.5 %sum_cores.1 = bf16[256,2176]{1,0:T(8,128)(2,1)} custom-call(f32[256,2176]{1,0:T(8,128)S(1)} %get-tuple-element.26.keep, bf16[256,2176]{1,0:T(8,128)(2,1)S(1)} %collective-permute-done.3.other), custom_call_target="tpu_custom_call" | custom-call | tf_op jit(solution)/shard_map/sum_cores/pallas_call | solution.py:279
  41.0 6.4 %all-to-all-start = ((bf16[32,8,2176]{2,1,0:T(8,128)(2,1)}), bf16[32,8,2176]{2,1,0:T(8,128)(2,1)S(1)}, u32[]{:S(2)}, u32[]{:S(2)}) async-start(bf16[32,8,2176]{2,1,0:T(8,128)(2,1)} %bitcast.4), calls=%async_computation | async-start | bytes 2228224 | tf_op jit(solution)/shard_map/sum_near/all_to_all | solution.py:295
  47.4 2.3 %collective-permute-start.4 = (bf16[2,72,512]{2,1,0:T(8,128)(2,1)S(1)}, bf16[2,72,512]{2,1,0:T(8,128)(2,1)S(1)}, u32[]{:S(2)}, u32[]{:S(2)}) collective-permute-start(bf16[2,72,512]{2,1,0:T(8,128)(2,1)S(1)} %get-tuple-element.36), channel_id=1, source_target_pairs={{0,1},{1,2},{2,3},{3,4},{4,5},{5,6},{6,7},{7,8},{8,9},{9,10},{10,1... | collective-permute-start | bytes 442376 | tf_op jit(solution)/shard_map/window_out/ppermute | solution.py:289
  49.7 1.2 %collective-permute-start.5 = (bf16[2,72,512]{2,1,0:T(8,128)(2,1)S(1)}, bf16[2,72,512]{2,1,0:T(8,128)(2,1)S(1)}, u32[]{:S(2)}, u32[]{:S(2)}) collective-permute-start(bf16[2,72,512]{2,1,0:T(8,128)(2,1)S(1)} %get-tuple-element.37), channel_id=1, source_target_pairs={{0,32},{1,33},{2,34},{3,35},{4,36},{5,37},{6,38},{7,39},{8,40},{9,... | collective-permute-start | bytes 442376 | tf_op jit(solution)/shard_map/window_out/ppermute | solution.py:289
  50.9 1.3 %collective-permute-start.6 = (bf16[2,72,512]{2,1,0:T(8,128)(2,1)S(1)}, bf16[2,72,512]{2,1,0:T(8,128)(2,1)S(1)}, u32[]{:S(2)}, u32[]{:S(2)}) collective-permute-start(bf16[2,72,512]{2,1,0:T(8,128)(2,1)S(1)} %get-tuple-element.38), channel_id=1, source_target_pairs={{0,33},{1,34},{2,35},{3,36},{4,37},{5,38},{6,39},{7,40},{8,41},{9,... | collective-permute-start | bytes 442376 | tf_op jit(solution)/shard_map/window_out/ppermute | solution.py:289
  52.1 9.2 %collective-permute-done.4 = bf16[2,72,512]{2,1,0:T(8,128)(2,1)S(1)} collective-permute-done((bf16[2,72,512]{2,1,0:T(8,128)(2,1)S(1)}, bf16[2,72,512]{2,1,0:T(8,128)(2,1)S(1)}, u32[]{:S(2)}, u32[]{:S(2)}) %collective-permute-start.4) | collective-permute-done | bytes 147488 | tf_op jit(solution)/shard_map/window_out/ppermute | solution.py:289
  61.4 9.9 %collective-permute-done.5 = bf16[2,72,512]{2,1,0:T(8,128)(2,1)S(1)} collective-permute-done((bf16[2,72,512]{2,1,0:T(8,128)(2,1)S(1)}, bf16[2,72,512]{2,1,0:T(8,128)(2,1)S(1)}, u32[]{:S(2)}, u32[]{:S(2)}) %collective-permute-start.5) | collective-permute-done | bytes 147488 | tf_op jit(solution)/shard_map/window_out/ppermute | solution.py:289
  71.2 1.1 collective-permute-done.6
  72.4 0.2 sum_near.1.mine
  72.5 3.3 %collective-permute-start.9 = (f32[8,2176]{1,0:T(8,128)S(1)}, f32[8,2176]{1,0:T(8,128)S(1)}, u32[]{:S(2)}, u32[]{:S(2)}) collective-permute-start(f32[8,2176]{1,0:T(8,128)S(1)} %sum_near.1.mine), channel_id=1, source_target_pairs={{0,24},{8,0},{16,8},{24,16},{1,25},{9,1},{17,9},{25,17},{2,26},{10... | collective-permute-start | bytes 208904 | tf_op jit(solution)/shard_map/sum_far/ppermute | solution.py:312
  75.8 1.4 %collective-permute-start.8 = (f32[8,2176]{1,0:T(8,128)S(1)}, f32[8,2176]{1,0:T(8,128)S(1)}, u32[]{:S(2)}, u32[]{:S(2)}) collective-permute-start(f32[8,2176]{1,0:T(8,128)S(1)} %sum_near.1.mine), channel_id=1, source_target_pairs={{0,16},{8,24},{16,0},{24,8},{1,17},{9,25},{17,1},{25,9},{2,18},{10... | collective-permute-start | bytes 208904 | tf_op jit(solution)/shard_map/sum_far/ppermute | solution.py:312
  77.2 1.4 %collective-permute-start.7 = (f32[8,2176]{1,0:T(8,128)S(1)}, f32[8,2176]{1,0:T(8,128)S(1)}, u32[]{:S(2)}, u32[]{:S(2)}) collective-permute-start(f32[8,2176]{1,0:T(8,128)S(1)} %sum_near.1.mine), channel_id=1, source_target_pairs={{0,8},{8,16},{16,24},{24,0},{1,9},{9,17},{17,25},{25,1},{2,10},{10... | collective-permute-start | bytes 208904 | tf_op jit(solution)/shard_map/sum_far/ppermute | solution.py:312
  78.7 2.9 %collective-permute-done.9.p3 = f32[8,2176]{1,0:T(8,128)S(1)} collective-permute-done((f32[8,2176]{1,0:T(8,128)S(1)}, f32[8,2176]{1,0:T(8,128)S(1)}, u32[]{:S(2)}, u32[]{:S(2)}) %collective-permute-start.9) | collective-permute-done | bytes 69664 | tf_op jit(solution)/shard_map/sum_far/ppermute | solution.py:312
  81.5 3.8 %collective-permute-done.8.p2 = f32[8,2176]{1,0:T(8,128)S(1)} collective-permute-done((f32[8,2176]{1,0:T(8,128)S(1)}, f32[8,2176]{1,0:T(8,128)S(1)}, u32[]{:S(2)}, u32[]{:S(2)}) %collective-permute-start.8) | collective-permute-done | bytes 69664 | tf_op jit(solution)/shard_map/sum_far/ppermute | solution.py:312
  85.3 0.1 sum_far.1
  85.4 0.1 broadcast_in_dim.10
  85.5 20.9 %all_to_all.10 = bf16[32,8,2176]{2,1,0:T(8,128)(2,1)S(1)} all-to-all(bf16[32,8,2176]{2,1,0:T(8,128)(2,1)S(1)} %broadcast_in_dim.10), channel_id=1, replica_groups=mesh['xh'=2,'y'=4,'zh'=4,'zl'=2,'xl'=2,'core'=2] {'xh','y','zl','xl'}, dimensions={0} | all-to-all | bytes 2228224 | tf_op jit(solution)/shard_map/share/all_to_all | solution.py:323
  106.4 1.9 %collective-permute-start.10 = (bf16[256,2176]{1,0:T(8,128)(2,1)S(1)}, bf16[256,2176]{1,0:T(8,128)(2,1)S(1)}, u32[]{:S(2)}, u32[]{:S(2)}) collective-permute-start(bf16[256,2176]{1,0:T(8,128)(2,1)S(1)} %bitcast.8), channel_id=1, source_target_pairs={{0,1},{1,0},{2,3},{3,2},{4,5},{5,4},{6,7},{7,6},{8,9},{9,8},{10,11... | collective-permute-start | bytes 3342344 | tf_op jit(solution)/shard_map/share/ppermute | solution.py:325
  108.3 0.1 reshape.46
  108.4 0.1 reshape.47
  108.5 0.1 reshape.48
  108.5 0.1 reshape.49
  108.6 0.8 maximum_maximum_fusion
  109.5 1.2 %fusion = (bf16[1,12,12,2,512]{4,3,2,1,0:T(2,128)(2,1)}, bf16[1,12,12,2,512]{4,3,2,1,0:T(2,128)(2,1)}) fusion(bf16[2,12,12,2,512]{4,3,2,1,0:T(2,128)(2,1)S(1)} %maximum_maximum_fusion), kind=kLoop, calls=%fused_computation.6 | loop fusion | bytes 1179648 | tf_op jit(solution)/shard_map/window_out/slice | solution.py:309
  110.7 0.0 collective-permute-done.10.theirs
  110.7 2.5 %finish.1 = (bf16[512,1536]{1,0:T(8,128)(2,1)}, bf16[512,512]{1,0:T(8,128)(2,1)}, f32[1,512]{1,0:T(1,128)}) custom-call(s32[2]{0:T(128)S(1)} %pad_add_fusion.ids, bf16[256,2176]{1,0:T(8,128)(2,1)S(1)} %bitcast.9, bf16[256,2176]{1,0:T(8,128)(2,1)S(1)} %collective-permute-done.10.theirs), custom_call_target="tpu_custom_call" | custom-call | tf_op jit(solution)/shard_map/finish/pallas_call | solution.py:327
  (9 shorter events, 0.0 us)
Async XLA Ops:
  2.4 15.9 %copy-start = (bf16[512,1536]{1,0:T(8,128)(2,1)S(1)}, bf16[512,1536]{1,0:T(8,128)(2,1)}, u32[]{:S(2)}) copy-start(bf16[512,1536]{1,0:T(8,128)(2,1)} %wqkv.1) | copy-start | bytes 4718596
  3.1 16.0 %collective-permute-start.1 = (bf16[2,72,512]{2,1,0:T(8,128)(2,1)}, bf16[2,72,512]{2,1,0:T(8,128)(2,1)S(1)}, u32[]{:S(2)}, u32[]{:S(2)}) collective-permute-start(bf16[2,72,512]{2,1,0:T(8,128)(2,1)} %reshape.43), channel_id=1, source_target_pairs={{0,224},{1,225},{2,226},{3,227},{4,228},{5,229},{6,230},{7,231},{8... | collective-permute-start | bytes 442376 | tf_op jit(solution)/shard_map/window_in/ppermute | solution.py:231
  10.1 9.0 %collective-permute-start = (bf16[2,72,512]{2,1,0:T(8,128)(2,1)}, bf16[2,72,512]{2,1,0:T(8,128)(2,1)}, u32[]{:S(2)}, u32[]{:S(2)}) collective-permute-start(bf16[2,72,512]{2,1,0:T(8,128)(2,1)} %reshape.42), channel_id=1, source_target_pairs={{0,31},{1,0},{2,1},{3,2},{4,3},{5,4},{6,5},{7,6},{8,7},{9,8},{10,9... | collective-permute-start | bytes 442376 | tf_op jit(solution)/shard_map/window_in/ppermute | solution.py:231
  12.0 8.4 %collective-permute-start.2 = (bf16[2,72,512]{2,1,0:T(8,128)(2,1)}, bf16[2,72,512]{2,1,0:T(8,128)(2,1)}, u32[]{:S(2)}, u32[]{:S(2)}) collective-permute-start(bf16[2,72,512]{2,1,0:T(8,128)(2,1)} %reshape.44), channel_id=1, source_target_pairs={{0,255},{1,224},{2,225},{3,226},{4,227},{5,228},{6,229},{7,230},{8... | collective-permute-start | bytes 442376 | tf_op jit(solution)/shard_map/window_in/ppermute | solution.py:231
  18.3 2.1 %copy-start.3 = (f32[512]{0:T(512)S(1)}, f32[512]{0:T(512)}, u32[]{:S(2)}) copy-start(f32[512]{0:T(512)} %param.6) | copy-start | bytes 6148
  20.4 1.0 copy-start.1
  21.5 15.7 %copy-start.2 = (bf16[512,512]{1,0:T(8,128)(2,1)S(1)}, bf16[512,512]{1,0:T(8,128)(2,1)}, u32[]{:S(2)}) copy-start(bf16[512,512]{1,0:T(8,128)(2,1)} %wout.3) | copy-start | bytes 1572868
  35.5 4.0 %collective-permute-start.3 = (bf16[256,2176]{1,0:T(8,128)(2,1)S(1)}, bf16[256,2176]{1,0:T(8,128)(2,1)S(1)}, u32[]{:S(2)}, u32[]{:S(2)}) collective-permute-start(bf16[256,2176]{1,0:T(8,128)(2,1)S(1)} %get-tuple-element.27), channel_id=1, source_target_pairs={{0,1},{1,0},{2,3},{3,2},{4,5},{5,4},{6,7},{7,6},{8,9},{9,8},{10,11... | collective-permute-start | bytes 3342344 | tf_op jit(solution)/shard_map/sum_cores/ppermute | solution.py:268
  41.0 31.4 %all-to-all-start = ((bf16[32,8,2176]{2,1,0:T(8,128)(2,1)}), bf16[32,8,2176]{2,1,0:T(8,128)(2,1)S(1)}, u32[]{:S(2)}, u32[]{:S(2)}) async-start(bf16[32,8,2176]{2,1,0:T(8,128)(2,1)} %bitcast.4), calls=%async_computation | async-start | bytes 2228224 | tf_op jit(solution)/shard_map/sum_near/all_to_all | solution.py:295
  47.4 14.0 %collective-permute-start.4 = (bf16[2,72,512]{2,1,0:T(8,128)(2,1)S(1)}, bf16[2,72,512]{2,1,0:T(8,128)(2,1)S(1)}, u32[]{:S(2)}, u32[]{:S(2)}) collective-permute-start(bf16[2,72,512]{2,1,0:T(8,128)(2,1)S(1)} %get-tuple-element.36), channel_id=1, source_target_pairs={{0,1},{1,2},{2,3},{3,4},{4,5},{5,6},{6,7},{7,8},{8,9},{9,10},{10,1... | collective-permute-start | bytes 442376 | tf_op jit(solution)/shard_map/window_out/ppermute | solution.py:289
  49.7 21.6 %collective-permute-start.5 = (bf16[2,72,512]{2,1,0:T(8,128)(2,1)S(1)}, bf16[2,72,512]{2,1,0:T(8,128)(2,1)S(1)}, u32[]{:S(2)}, u32[]{:S(2)}) collective-permute-start(bf16[2,72,512]{2,1,0:T(8,128)(2,1)S(1)} %get-tuple-element.37), channel_id=1, source_target_pairs={{0,32},{1,33},{2,34},{3,35},{4,36},{5,37},{6,38},{7,39},{8,40},{9,... | collective-permute-start | bytes 442376 | tf_op jit(solution)/shard_map/window_out/ppermute | solution.py:289
  50.9 21.5 %collective-permute-start.6 = (bf16[2,72,512]{2,1,0:T(8,128)(2,1)S(1)}, bf16[2,72,512]{2,1,0:T(8,128)(2,1)S(1)}, u32[]{:S(2)}, u32[]{:S(2)}) collective-permute-start(bf16[2,72,512]{2,1,0:T(8,128)(2,1)S(1)} %get-tuple-element.38), channel_id=1, source_target_pairs={{0,33},{1,34},{2,35},{3,36},{4,37},{5,38},{6,39},{7,40},{8,41},{9,... | collective-permute-start | bytes 442376 | tf_op jit(solution)/shard_map/window_out/ppermute | solution.py:289
  72.5 9.0 %collective-permute-start.9 = (f32[8,2176]{1,0:T(8,128)S(1)}, f32[8,2176]{1,0:T(8,128)S(1)}, u32[]{:S(2)}, u32[]{:S(2)}) collective-permute-start(f32[8,2176]{1,0:T(8,128)S(1)} %sum_near.1.mine), channel_id=1, source_target_pairs={{0,24},{8,0},{16,8},{24,16},{1,25},{9,1},{17,9},{25,17},{2,26},{10... | collective-permute-start | bytes 208904 | tf_op jit(solution)/shard_map/sum_far/ppermute | solution.py:312
  75.8 9.5 %collective-permute-start.8 = (f32[8,2176]{1,0:T(8,128)S(1)}, f32[8,2176]{1,0:T(8,128)S(1)}, u32[]{:S(2)}, u32[]{:S(2)}) collective-permute-start(f32[8,2176]{1,0:T(8,128)S(1)} %sum_near.1.mine), channel_id=1, source_target_pairs={{0,16},{8,24},{16,0},{24,8},{1,17},{9,25},{17,1},{25,9},{2,18},{10... | collective-permute-start | bytes 208904 | tf_op jit(solution)/shard_map/sum_far/ppermute | solution.py:312
  77.2 8.1 %collective-permute-start.7 = (f32[8,2176]{1,0:T(8,128)S(1)}, f32[8,2176]{1,0:T(8,128)S(1)}, u32[]{:S(2)}, u32[]{:S(2)}) collective-permute-start(f32[8,2176]{1,0:T(8,128)S(1)} %sum_near.1.mine), channel_id=1, source_target_pairs={{0,8},{8,16},{16,24},{24,0},{1,9},{9,17},{17,25},{25,1},{2,10},{10... | collective-permute-start | bytes 208904 | tf_op jit(solution)/shard_map/sum_far/ppermute | solution.py:312
  106.4 4.3 %collective-permute-start.10 = (bf16[256,2176]{1,0:T(8,128)(2,1)S(1)}, bf16[256,2176]{1,0:T(8,128)(2,1)S(1)}, u32[]{:S(2)}, u32[]{:S(2)}) collective-permute-start(bf16[256,2176]{1,0:T(8,128)(2,1)S(1)} %bitcast.8), channel_id=1, source_target_pairs={{0,1},{1,0},{2,3},{3,2},{4,5},{5,4},{6,7},{7,6},{8,9},{9,8},{10,11... | collective-permute-start | bytes 3342344 | tf_op jit(solution)/shard_map/share/ppermute | solution.py:325

commit v3 on v2

v3 whole, which is shorter than its diff:
```python
import functools
import math

import jax
import jax.numpy as jnp
from jax import lax
from jax.experimental import pallas as pl
from jax.experimental.pallas import tpu as pltpu
from jax.sharding import Mesh
from jax.sharding import PartitionSpec as P

HEADS = 16
WIN = 12
SHIFT = 6
EPS = 1e-05
MASKED = -1e30
F32 = jnp.float32
BF16 = jnp.bfloat16

LAT = ("xh", "y")
LON = ("zh", "zl", "xl", "core")
NEAR = ("xh", "y", "zl", "xl")
FAR = "zh"
EVERY = LAT + LON


def dot(a, b, dims=((1,), (0,))):
    return lax.dot_general(a, b, (dims, ((), ())), preferred_element_type=F32)


def normalise(tok):
    mean = jnp.mean(tok, -1, keepdims=True)
    centred = tok - mean
    inv = lax.rsqrt(jnp.mean(centred * centred, -1, keepdims=True) + EPS)
    return centred * inv, inv


def gather_quads(refs, which, out):
    rows = refs[0].shape[1]
    for j, ref in enumerate(refs):
        out[j * rows : (j + 1) * rows, :] = ref[which].astype(F32)


def lanes(shape):
    return lax.broadcasted_iota(jnp.int32, shape, len(shape) - 1)


def split_low(value, terms):
    lane = lanes(value.shape)
    out = jnp.zeros_like(value)
    rest = value
    for i in range(terms):
        part = rest.astype(BF16).astype(F32)
        out = jnp.where(lane == i, part, out)
        rest = rest - part
    return out.astype(BF16)


def weights_kernel(wqkv, wout, wqkv_t, wout_near):
    wqkv_t[...] = wqkv[...].T
    wout_near[...] = wout[...]


def grads_kernel(
    ids, q0, q1, q2, q3, gain, wqkv, wqkv_t, wout,
    keep, send, attn_t, back,
    wide, normed, normed_t, g_low, q_t, kv_t, kv, do_t, dq_t, dkv_t, gain_col,
    diag, side, bias, scores, d_probs, p_low, d_low, acc,
):
    quads = (q0, q1, q2, q3)
    tokens, feat = wide.shape
    main = tokens // 128 * 128
    left = tokens - main
    ext = normed.shape[0]
    size = feat // HEADS
    per = 128 // size
    half = tokens // 2
    inv_root = 1.0 / math.sqrt(size)
    to_exp2 = inv_root * math.log2(math.e)

    def repeat_left(ref):
        for j in range(1, per):
            ref[tokens + (j - 1) * left : tokens + j * left, :] = ref[main:tokens, :]

    gather_quads(quads, 1, wide)
    g_low[:tokens, :] = wide[...].astype(BF16)
    repeat_left(g_low)
    do_t[...] = dot(wout[...], g_low[...], ((1,), (1,))).astype(BF16)
    gather_quads(quads, 0, wide)
    xhat, _ = normalise(wide[...])
    wide[...] = xhat
    normed[:tokens, :] = (xhat * gain[...]).astype(BF16)
    repeat_left(normed)
    q_t[...] = dot(wqkv_t[:feat, :], normed[...], ((1,), (1,))).astype(BF16)
    kv_t[...] = dot(wqkv_t[feat:, :], normed[:tokens, :], ((1,), (1,))).astype(BF16)
    kv[...] = dot(normed[:tokens, :], wqkv[:, feat:]).astype(BF16)
    normed_t[...] = normed[...].T

    row_head = lax.broadcasted_iota(jnp.int32, (128, 128), 0) // size
    diag[...] = jnp.where(row_head == lanes((128, 128)) // left, 1.0, 0.0).astype(BF16)
    late_key = lax.broadcasted_iota(jnp.int32, (tokens, 128), 0) >= half
    lane = lanes((tokens, 128))
    side[...] = jnp.where(
        jnp.logical_or(
            jnp.logical_and(lane == 0, late_key),
            jnp.logical_and(lane == 1, jnp.logical_not(late_key)),
        ),
        1.0,
        0.0,
    ).astype(BF16)
    which = lax.broadcasted_iota(jnp.int32, (128, ext), 0)
    late_query = lanes((128, ext)) >= half
    blocked = jnp.logical_or(
        jnp.logical_and(which == 0, jnp.logical_not(late_query)),
        jnp.logical_and(which == 1, late_query),
    )
    bias[...] = jnp.where(jnp.logical_and(blocked, ids[0] == 1), MASKED, 0.0).astype(BF16)

    def spread(block, h):
        parts = []
        if h > 0:
            parts.append(jnp.zeros((h * size, block.shape[1]), BF16))
        parts.append(block)
        if h < per - 1:
            parts.append(jnp.zeros(((per - 1 - h) * size, block.shape[1]), BF16))
        return jnp.concatenate(parts, 0)

    def operand(ref, g, h):
        rows = slice(128 * g, 128 * (g + 1))
        if h is None:
            return ref[rows, main:ext] * diag[...]
        return spread(ref[128 * g + size * h : 128 * g + size * (h + 1), :main], h)

    def score(slot, g, h):
        cols = slice(128 * g, 128 * (g + 1))
        at, width = (slice(main, ext), ext - main) if h is None else (slice(0, main), main)
        keys = jnp.concatenate([kv[:, cols], side[...]], 1)
        queries = jnp.concatenate([operand(q_t, g, h), bias[:, at]], 0)
        scores[slot, :, :width] = dot(keys, queries)
        values = kv[:, feat + 128 * g : feat + 128 * (g + 1)]
        d_probs[slot, :, :width] = dot(values, operand(do_t, g, h))

    step = 32

    def soften(slot, h):
        width = ext - main if h is None else main
        chunks = [slice(c, c + step) for c in range(0, tokens, step)]

        def fold(value, op):
            return op(value.reshape(step // 8, 8, width), axis=0)

        top = None
        for c in chunks:
            part = fold(scores[slot, c, :width], jnp.max)
            top = part if top is None else jnp.maximum(top, part)
        top = jnp.max(top, 0, keepdims=True)
        total = jnp.zeros((8, width), F32)
        for c in chunks:
            e = jnp.exp2((scores[slot, c, :width] - top) * to_exp2)
            scores[slot, c, :width] = e
            total = total + fold(e, jnp.sum)
        scale = 1.0 / jnp.sum(total, 0, keepdims=True)
        delta = jnp.zeros((8, width), F32)
        for c in chunks:
            p = scores[slot, c, :width] * scale
            p_low[slot, c, :width] = p.astype(BF16)
            delta = delta + fold(d_probs[slot, c, :width] * p, jnp.sum)
        delta = jnp.sum(delta, 0, keepdims=True)
        scale = scale * inv_root
        for c in chunks:
            p = scores[slot, c, :width] * scale
            d_low[slot, c, :width] = (p * (d_probs[slot, c, :width] - delta)).astype(BF16)

    def collect(slot, g, h):
        nt = ((1,), (1,))
        if h is None:
            rows = slice(128 * g, 128 * (g + 1))
            later = slice(feat + 128 * g, feat + 128 * (g + 1))
            width = ext - main
            keep_own = diag[...].astype(F32)
            p, d = p_low[slot, :, :width], d_low[slot, :, :width]
            attn_t[rows, main:ext] = (dot(kv_t[later, :], p) * keep_own).astype(BF16)
            dq_t[rows, main:ext] = (dot(kv_t[rows, :], d) * keep_own).astype(BF16)
            acc[0] = dot(operand(q_t, g, h), d, nt)
            acc[1] = dot(operand(do_t, g, h), p, nt)
            return
        rows = slice(128 * g + size * h, 128 * g + size * (h + 1))
        later = slice(feat + rows.start, feat + rows.stop)
        own = slice(size * h, size * (h + 1))
        p, d = p_low[slot], d_low[slot]
        attn_t[rows, :main] = dot(kv_t[later, :], p).astype(BF16)
        dq_t[rows, :main] = dot(kv_t[rows, :], d).astype(BF16)
        dkv_t[rows, :] = (dot(q_t[rows, :main], d, nt) + acc[0, own, :]).astype(BF16)
        dkv_t[later, :] = (dot(do_t[rows, :main], p, nt) + acc[1, own, :]).astype(BF16)

    blocks = [(g, h) for g in range(HEADS // per) for h in (None, *range(per))]
    score(0, *blocks[0])
    for n, (g, h) in enumerate(blocks):
        if n + 1 < len(blocks):
            score((n + 1) % 2, *blocks[n + 1])
        soften(n % 2, h)
        if n > 0:
            collect((n - 1) % 2, *blocks[n - 1])
    collect((len(blocks) - 1) % 2, *blocks[-1])

    from_q = dot(wqkv[:, :feat], dq_t[...])
    from_kv = dot(wqkv[:, feat:], dkv_t[...])
    back[:main, :] = (from_q[:, :main] + from_kv[:, :main]).T.astype(BF16)
    rest = from_q[:, main:].T
    last = from_kv[:, main:].T
    for j in range(per):
        last = last + rest[j * left : (j + 1) * left]
    back[main:, :] = last.astype(BF16)
    part_gain = jnp.sum(back[...].astype(F32) * wide[...], 0, keepdims=True)
    column = jnp.broadcast_to(part_gain, (128, feat)).T
    gain_col[...] = jnp.where(lanes(column.shape) < 2, column, 0.0)

    rows = feat // 2
    mine = pl.multiple_of(ids[1] * rows, rows)
    theirs = pl.multiple_of((1 - ids[1]) * rows, rows)

    def partial_sums(start):
        pick = pl.ds(start, rows)
        return (
            dot(normed_t[pick, :], dq_t[...], ((1,), (1,))),
            dot(normed_t[pick, :tokens], dkv_t[:feat, :], ((1,), (1,))),
            dot(normed_t[pick, :tokens], dkv_t[feat:, :], ((1,), (1,))),
            dot(attn_t[pick, :], g_low[...]),
        )

    for block, value in enumerate(partial_sums(theirs)):
        send[:, block * feat : (block + 1) * feat] = value.astype(BF16)
    for block, value in enumerate(partial_sums(mine)):
        keep[:, block * feat : (block + 1) * feat] = value
    send[:, 4 * feat :] = gain_col[pl.ds(theirs, rows), :].astype(BF16)
    keep[:, 4 * feat :] = gain_col[pl.ds(mine, rows), :]


def grads_scratch(tokens, feat):
    ext = tokens // 128 * 128 + 128
    return [
        pltpu.VMEM((tokens, feat), F32),
        pltpu.VMEM((ext, feat), BF16),
        pltpu.VMEM((feat, ext), BF16),
        pltpu.VMEM((ext, feat), BF16),
        pltpu.VMEM((feat, ext), BF16),
        pltpu.VMEM((2 * feat, tokens), BF16),
        pltpu.VMEM((tokens, 2 * feat), BF16),
        pltpu.VMEM((feat, ext), BF16),
        pltpu.VMEM((feat, ext), BF16),
        pltpu.VMEM((2 * feat, tokens), BF16),
        pltpu.VMEM((feat, 128), F32),
        pltpu.VMEM((128, 128), BF16),
        pltpu.VMEM((tokens, 128), BF16),
        pltpu.VMEM((128, ext), BF16),
        pltpu.VMEM((2, tokens, 256), F32),
        pltpu.VMEM((2, tokens, 256), F32),
        pltpu.VMEM((2, tokens, 256), BF16),
        pltpu.VMEM((2, tokens, 256), BF16),
        pltpu.VMEM((2, 128, tokens), F32),
    ]


def tokens_kernel(q0, q1, q2, q3, gain, wout, attn_t, back, o0, o1, o2, o3, wide):
    quads, outs = (q0, q1, q2, q3), (o0, o1, o2, o3)
    rows = q0.shape[1]
    gather_quads(quads, 0, wide)
    tok = wide[...]
    main = tok.shape[0] // 128 * 128
    left = tok.shape[0] - main
    added = dot(attn_t[...], wout[...], ((0,), (0,)))
    last = added[main : main + left]
    for at in range(main + left, added.shape[0], left):
        last = last + added[at : at + left]
    mixed = tok + jnp.concatenate([added[:main], last], 0)
    for j, out in enumerate(outs):
        out[0] = mixed[j * rows : (j + 1) * rows].astype(BF16)
    xhat, inv = normalise(tok)
    scaled = back[...].astype(F32) * gain[...]
    inner = (
        scaled
        - jnp.mean(scaled, -1, keepdims=True)
        - xhat * jnp.mean(scaled * xhat, -1, keepdims=True)
    )
    gather_quads(quads, 1, wide)
    grad = wide[...] + inv * inner
    for j, out in enumerate(outs):
        out[1] = grad[j * rows : (j + 1) * rows].astype(BF16)


def gain_total(tile):
    return jnp.where(lanes(tile.shape) == 0, jnp.sum(tile, -1, keepdims=True), 0.0)


def add_pair(keep, other):
    total = keep + other.astype(F32)
    rest = total - lax.reduce_precision(total, 8, 7)
    return jnp.where(lanes(total.shape) == total.shape[1] - 127, rest, total).astype(BF16)


def final_piece_kernel(factor, parts, _, out):
    main = parts.shape[2] - 128
    total = jnp.sum(parts[...], 0) * factor
    out[:, :main] = total[:, :main].astype(BF16)
    out[:, main:] = split_low(gain_total(total[:, main:]), 3)


def finish_kernel(ids, mine, theirs, grad_qkv, grad_out, gain_grad, tails, sems):
    rows = mine.shape[0]
    wide = grad_qkv.shape[1]
    main = wide + grad_out.shape[1]
    copies = []
    for n, half in enumerate((mine, theirs)):
        at = pl.multiple_of((ids[1] if n == 0 else 1 - ids[1]) * rows, rows)
        for m, (src, dst) in enumerate(
            (
                (half.at[:, main:], tails.at[n]),
                (half.at[:, :wide], grad_qkv.at[pl.ds(at, rows), :]),
                (half.at[:, wide:main], grad_out.at[pl.ds(at, rows), :]),
            )
        ):
            copy = pltpu.make_async_copy(src, dst, sems.at[3 * n + m])
            copy.start()
            copies.append((m, copy))
    for m, copy in copies:
        if m == 0:
            copy.wait()
    for n in range(2):
        at = pl.multiple_of((ids[1] if n == 0 else 1 - ids[1]) * rows, rows)
        column = tails[n].astype(F32).T
        gain_grad[:, pl.ds(at, rows)] = column[0:1] + column[1:2] + column[2:3]
    for m, copy in copies:
        if m > 0:
            copy.wait()


def shards(tokens, layer_norm_gain, cotangent, w_qkv, w_out):
    _, lat_rows, lon_cols, levels, feat = tokens.shape
    lat_n, lon_n = lax.axis_size(LAT), lax.axis_size(LON)
    quad_tokens = SHIFT * SHIFT * levels
    n_tokens = 4 * quad_tokens
    keep_part, go_part = slice(SHIFT, lat_rows), slice(0, SHIFT)

    def pairs(d_lat, d_lon):
        return [
            (a * lon_n + o, (a + d_lat) % lat_n * lon_n + (o + d_lon) % lon_n)
            for a in range(lat_n)
            for o in range(lon_n)
        ]

    def quad(rows, cols):
        both = jnp.stack([tokens[0, rows, cols], cotangent[0, rows, cols]])
        return both.reshape(2, quad_tokens, feat)

    shifts = ((0, 0), (0, 1), (1, 0), (1, 1))
    cuts = [(go_part if a else keep_part, go_part if o else keep_part) for a, o in shifts]
    with jax.named_scope("window_in"):
        quads = [quad(*cut) for cut in cuts]
        quads = [
            q if s == (0, 0) else lax.ppermute(q, EVERY, pairs(-s[0], -s[1]))
            for q, s in zip(quads, shifts)
        ]
    gain_row = layer_norm_gain[None, :]
    core = lax.axis_index("core")
    ids = jnp.stack([(lax.axis_index(LAT) == lat_n - 1).astype(jnp.int32), core.astype(jnp.int32)])
    vmem = pl.BlockSpec(memory_space=pltpu.VMEM)
    smem = pl.BlockSpec(memory_space=pltpu.SMEM)
    hbm = pl.BlockSpec(memory_space=pl.ANY)
    params = pltpu.CompilerParams(vmem_limit_bytes=40 * 1024 * 1024)
    rows, width = feat // 2, 4 * feat + 128
    with jax.named_scope("weights"):
        w_qkv_t, w_out_near = pl.pallas_call(
            weights_kernel,
            in_specs=[vmem] * 2,
            out_specs=[vmem] * 2,
            out_shape=[
                jax.ShapeDtypeStruct((3 * feat, feat), BF16),
                jax.ShapeDtypeStruct((feat, feat), BF16),
            ],
            compiler_params=params,
        )(w_qkv, w_out)
    with jax.named_scope("window_grads"):
        keep, send, attn_t, back = pl.pallas_call(
            grads_kernel,
            in_specs=[smem] + [vmem] * 8,
            out_specs=[vmem] * 4,
            out_shape=[
                jax.ShapeDtypeStruct((rows, width), F32),
                jax.ShapeDtypeStruct((rows, width), BF16),
                jax.ShapeDtypeStruct((feat, n_tokens // 128 * 128 + 128), BF16),
                jax.ShapeDtypeStruct((n_tokens, feat), BF16),
            ],
            scratch_shapes=grads_scratch(n_tokens, feat),
            compiler_params=params,
        )(ids, *quads, gain_row, w_qkv, w_qkv_t, w_out_near)
    swap = [(0, 1), (1, 0)]
    with jax.named_scope("sum_cores"):
        other = lax.ppermute(send, "core", swap)
    with jax.named_scope("window_tokens"):
        outs = pl.pallas_call(
            tokens_kernel,
            in_specs=[vmem] * 8,
            out_specs=[vmem] * 4,
            out_shape=[jax.ShapeDtypeStruct((2, quad_tokens, feat), BF16)] * 4,
            scratch_shapes=[pltpu.VMEM((n_tokens, feat), F32)],
            compiler_params=params,
        )(*quads, gain_row, w_out, attn_t, back)
    with jax.named_scope("sum_cores"):
        pair_sum = add_pair(keep, other)
    near, far = lax.axis_size(NEAR), lax.axis_size(FAR)
    factor = 1.0 / math.sqrt(lat_n * lat_rows * lon_n * lon_cols * levels)
    chunk = rows // near
    with jax.named_scope("sum_near"):
        pieces = lax.all_to_all(pair_sum.reshape(near, chunk, width), NEAR, 0, 0)
        piece = jnp.sum(pieces.astype(F32), 0)
        piece = jnp.broadcast_to(piece[None], (far, chunk, width))
    after, *outs = lax.optimization_barrier((piece, *outs))
    with jax.named_scope("sum_far"):
        parts = lax.all_to_all(piece, FAR, 0, 0)
    with jax.named_scope("window_out"):
        outs = [
            q if s == (0, 0) else lax.ppermute(q, EVERY, pairs(s[0], s[1]))
            for q, s in zip(outs, shifts)
        ]
    with jax.named_scope("sum_far"):
        piece = pl.pallas_call(
            functools.partial(final_piece_kernel, factor),
            in_specs=[vmem, hbm],
            out_specs=vmem,
            out_shape=jax.ShapeDtypeStruct((chunk, width), BF16),
            compiler_params=params,
        )(parts, after)
    piece, *outs = lax.optimization_barrier((piece, *outs))
    with jax.named_scope("share"):
        mine = lax.all_to_all(jnp.broadcast_to(piece[None], (near,) + piece.shape), NEAR, 0, 0)
        mine = mine.reshape(rows, width)
        theirs = lax.ppermute(mine, "core", swap)
    outs = lax.optimization_barrier((mine, *outs))[1:]
    with jax.named_scope("window_out"):
        blocks = [o.reshape(2, SHIFT, SHIFT, levels, feat) for o in outs]
        lower = jnp.concatenate([blocks[1], blocks[0]], 2)
        upper = jnp.concatenate([blocks[3], blocks[2]], 2)
        both = jnp.concatenate([upper, lower], 1)
        mixed, grad_tokens = both[0][None], both[1][None]
    final = [
        jax.ShapeDtypeStruct((feat, 3 * feat), BF16),
        jax.ShapeDtypeStruct((feat, feat), BF16),
        jax.ShapeDtypeStruct((1, feat), F32),
    ]
    with jax.named_scope("finish"):
        grad_qkv, grad_out, gain_gradient = pl.pallas_call(
            finish_kernel,
            in_specs=[smem, hbm, hbm],
            out_specs=[hbm, hbm, vmem],
            out_shape=final,
            scratch_shapes=[pltpu.VMEM((2, rows, 128), BF16), pltpu.SemaphoreType.DMA((6,))],
            compiler_params=params,
        )(ids, mine, theirs)
    return mixed, grad_tokens, gain_gradient[0], grad_qkv, grad_out


def solution(mesh):
    fine = Mesh(mesh.devices.reshape(2, 4, 4, 2, 2, 2), EVERY)
    grid = P(None, LAT, LON, None, None)
    return jax.shard_map(
        shards,
        mesh=fine,
        in_specs=(grid, P(), grid, P(), P()),
        out_specs=(grid, grid, P(), P(), P()),
        check_vma=False,
    )
```

time: 114 us -> 108 us (0.947)
  blocking collectives: 20.9 us -> 43 us
  waiting for transfers between devices: 29 us -> 13.8 us
  Pallas kernels: 19.9 us -> 13.1 us
  starting transfers between devices: 33.7 us -> 28.5 us
  local copies, waits for them, and re-layouts: 7.1 us -> 4.89 us
  other arithmetic: 1.75 us -> 3.26 us
    all_to_all x0 -> x1, blocking collectives: none -> 22.3 us  [shards(): pieces = lax.all_to_all(pair_sum.reshape(near, chunk, width), NEAR, 0, 0)]
    ppermute x3, waiting for transfers between devices: 20.2 us -> 6.84 us  [shards(): lax.ppermute(q, EVERY, pairs(s[0], s[1]))]
    ppermute x3 -> x0, waiting for transfers between devices: 6.63 us -> none  [shards(): lax.ppermute(piece, FAR, [(i, (i + by) % far) for i in range(far)])]
    ppermute x3 -> x0, starting transfers between devices: 6.15 us -> none  [shards(): lax.ppermute(piece, FAR, [(i, (i + by) % far) for i in range(far)])]
    pallas_call x1, Pallas kernels: 14.1 us -> 9.42 us  [shards(): pl.pallas_call(grads_kernel, in_specs=[smem] + [vmem] * 8, out_specs=[vme...]
    all_to_all x1, waiting for transfers between devices: 0.01 us -> 4.15 us  [shards(): parts = lax.all_to_all(piece, FAR, 0, 0)]
    reshape x4, local copies, waits for them, and re-layouts: 2.23 us -> 0.25 us  [quad(): return both.reshape(2, quad_tokens, feat)]
    unnamed x9 -> x6, local copies, waits for them, and re-layouts: 1.77 us -> 0.01 us
  transfers between devices with their start and end apart: 12 -> 9, of which waited for: 7 -> 5; matrix products, arithmetic and copies ran while one was open for 5% -> 4% of each run, Pallas kernels for 1% -> 1%
where the time goes in v3:
time: 108 us; the launch traced here: 107 us
  blocking collectives  43 us (40%)
  starting transfers between devices  28.5 us (26%)
  waiting for transfers between devices  13.8 us (13%)
  Pallas kernels  13.1 us (12%)
  local copies, waits for them, and re-layouts  4.89 us (5%)
  other arithmetic  3.26 us (3%)
    all_to_all x1, blocking collectives, shards(): pieces = lax.all_to_all(pair_sum.reshape(near, chunk, width), NEAR, 0, 0)  22.3 us
    all_to_all x1, blocking collectives, shards(): lax.all_to_all(jnp.broadcast_to(piece[None], (near,) + piece.shape), NEAR...  20.6 us
    ppermute x3, starting transfers between devices, shards(): lax.ppermute(q, EVERY, pairs(-s[0], -s[1]))  12.3 us
    pallas_call x1, Pallas kernels, shards(): pl.pallas_call(grads_kernel, in_specs=[smem] + [vmem] * 8, out_specs=[vme...  9.42 us
    all_to_all x1, starting transfers between devices, shards(): parts = lax.all_to_all(piece, FAR, 0, 0)  7.59 us
    ppermute x3, waiting for transfers between devices, shards(): lax.ppermute(q, EVERY, pairs(s[0], s[1]))  6.84 us
    all_to_all x1, waiting for transfers between devices, shards(): parts = lax.all_to_all(piece, FAR, 0, 0)  4.15 us
    ppermute x3, starting transfers between devices, shards(): lax.ppermute(q, EVERY, pairs(s[0], s[1]))  3.48 us
  transfers between devices with their start and end apart: 9, of which 5 were waited for; matrix products, arithmetic and copies ran while one was open for 4% of the time, Pallas kernels for 1%

profile of v3, /device:TPU:1, one launch (start us, length us, event | category | flops | bytes accessed | tf_op | source)
XLA Modules:
  0.0 107.4 jit_solution(2789761085189527518)
XLA Ops:
  0.6 0.0 copy-start
  0.7 1.7 %fusion.3 = (bf16[1,6,6,2,512]{4,3,2,1,0:T(2,128)(2,1)S(1)}, bf16[1,6,6,2,512]{4,3,2,1,0:T(2,128)(2,1)S(1)}, bf16[1,6,6,2,512]{4,3,2,1,0:T(2,128)(2,1)S(1)}, bf1...) fusion(bf16[1,12,12,2,512]{4,3,2,1,0:T(2,128)(2,1)} %param.5, ...), kind=kLoop, calls=%fused_computation.12 | loop fusion | bytes 1179648 | tf_op jit(solution)/shard_map/window_in/slice | solution.py:352
  2.4 0.2 pad_maximum_fusion.2
  2.6 0.1 reshape.44
  2.6 6.1 %collective-permute-start.1 = (bf16[2,72,512]{2,1,0:T(8,128)(2,1)S(1)}, bf16[2,72,512]{2,1,0:T(8,128)(2,1)S(1)}, u32[]{:S(2)}, u32[]{:S(2)}) collective-permute-start(bf16[2,72,512]{2,1,0:T(8,128)(2,1)S(1)} %reshape.44), channel_id=1, source_target_pairs={{0,224},{1,225},{2,226},{3,227},{4,228},{5,229},{6,230},{7,231},{8... | collective-permute-start | bytes 442376 | tf_op jit(solution)/shard_map/window_in/ppermute | solution.py:360
  8.7 0.2 pad_maximum_fusion.3
  8.9 0.1 reshape.45
  9.0 1.4 %collective-permute-start.2 = (bf16[2,72,512]{2,1,0:T(8,128)(2,1)S(1)}, bf16[2,72,512]{2,1,0:T(8,128)(2,1)S(1)}, u32[]{:S(2)}, u32[]{:S(2)}) collective-permute-start(bf16[2,72,512]{2,1,0:T(8,128)(2,1)S(1)} %reshape.45), channel_id=1, source_target_pairs={{0,255},{1,224},{2,225},{3,226},{4,227},{5,228},{6,229},{7,230},{8... | collective-permute-start | bytes 442376 | tf_op jit(solution)/shard_map/window_in/ppermute | solution.py:360
  10.4 0.2 pad_maximum_fusion.1
  10.6 0.0 copy-start.2
  10.6 0.1 reshape.43
  10.7 4.8 %collective-permute-start = (bf16[2,72,512]{2,1,0:T(8,128)(2,1)S(1)}, bf16[2,72,512]{2,1,0:T(8,128)(2,1)S(1)}, u32[]{:S(2)}, u32[]{:S(2)}) collective-permute-start(bf16[2,72,512]{2,1,0:T(8,128)(2,1)S(1)} %reshape.43), channel_id=1, source_target_pairs={{0,31},{1,0},{2,1},{3,2},{4,3},{5,4},{6,5},{7,6},{8,7},{9,8},{10,9... | collective-permute-start | bytes 442376 | tf_op jit(solution)/shard_map/window_in/ppermute | solution.py:360
  15.5 0.2 pad_maximum_fusion
  15.7 0.1 reshape.42.q0
  15.8 0.5 weights.1
  16.3 0.1 pad_add_fusion.ids
  16.4 0.0 collective-permute-done.1.q2
  16.4 0.0 collective-permute-done.2.q3
  16.4 0.4 collective-permute-done.q1
  16.8 0.0 copy-done.2
  16.8 9.4 %window_grads.1 = (f32[256,2176]{1,0:T(8,128)S(1)}, bf16[256,2176]{1,0:T(8,128)(2,1)S(1)}, bf16[512,384]{1,0:T(8,128)(2,1)S(1)}, bf16[288,512]{1,0:T(8,128)(2,1)S(1)}) custom-call(s32[2]{0:T(128)S(1)} %pad_add_fusion.ids, bf16[2,72,512]{2,1,0:T(8,128)(2,1)S(1)} %reshape.42.q0, bf16[2,72,512]{2,1,0:T(8,128)(2,1)S(1)} %collective-permute-done.q1, ...), custom_call_target="tpu_custom_call" | custom-call | tf_op jit(solution)/shard_map/window_grads/pallas_call | solution.py:383
  26.2 2.9 %collective-permute-start.3 = (bf16[256,2176]{1,0:T(8,128)(2,1)S(1)}, bf16[256,2176]{1,0:T(8,128)(2,1)S(1)}, u32[]{:S(2)}, u32[]{:S(2)}) collective-permute-start(bf16[256,2176]{1,0:T(8,128)(2,1)S(1)} %get-tuple-element.35), channel_id=1, source_target_pairs={{0,1},{1,0},{2,3},{3,2},{4,5},{5,4},{6,7},{7,6},{8,9},{9,8},{10,11... | collective-permute-start | bytes 3342344 | tf_op jit(solution)/shard_map/sum_cores/ppermute | solution.py:398
  29.1 2.4 %collective-permute-done.3 = bf16[256,2176]{1,0:T(8,128)(2,1)S(1)} collective-permute-done((bf16[256,2176]{1,0:T(8,128)(2,1)S(1)}, bf16[256,2176]{1,0:T(8,128)(2,1)S(1)}, u32[]{:S(2)}, u32[]{:S(2)}) %collective-permute-start.3) | collective-permute-done | bytes 1114144 | tf_op jit(solution)/shard_map/sum_cores/ppermute | solution.py:398
  31.5 0.4 fusion.1
  31.9 22.3 %all_to_all.15 = bf16[32,8,2176]{2,1,0:T(8,128)(2,1)S(1)} all-to-all(bf16[32,8,2176]{2,1,0:T(8,128)(2,1)S(1)} %fusion.1), channel_id=1, replica_groups=mesh['xh'=2,'y'=4,'zh'=4,'zl'=2,'xl'=2,'core'=2] {'xh','y','zl','xl'}, dimensions={0} | all-to-all | bytes 2228224 | tf_op jit(solution)/shard_map/sum_near/all_to_all | solution.py:414
  54.3 0.2 convert_reduce_fusion
  54.4 0.7 broadcast_in_dim.7._
  55.2 7.6 %all-to-all-start.1 = ((f32[4,8,2176]{2,1,0:T(8,128)}), f32[4,8,2176]{2,1,0:T(8,128)S(1)}, u32[]{:S(2)}, u32[]{:S(2)}) async-start(f32[4,8,2176]{2,1,0:T(8,128)} %broadcast_in_dim.7._), calls=%async_computation.1 | async-start | bytes 557056 | tf_op jit(solution)/shard_map/sum_far/all_to_all | solution.py:419
  62.8 0.6 window_tokens.1
  63.4 2.4 %collective-permute-start.4 = (bf16[2,72,512]{2,1,0:T(8,128)(2,1)S(1)}, bf16[2,72,512]{2,1,0:T(8,128)(2,1)S(1)}, u32[]{:S(2)}, u32[]{:S(2)}) collective-permute-start(bf16[2,72,512]{2,1,0:T(8,128)(2,1)S(1)} %get-tuple-element.44), channel_id=1, source_target_pairs={{0,1},{1,2},{2,3},{3,4},{4,5},{5,6},{6,7},{7,8},{8,9},{9,10},{10,1... | collective-permute-start | bytes 442376 | tf_op jit(solution)/shard_map/window_out/ppermute | solution.py:422
  65.8 0.3 collective-permute-start.5
  66.1 0.8 collective-permute-start.6
  66.8 4.2 %all-to-all-done.1.parts = f32[4,8,2176]{2,1,0:T(8,128)S(1)} async-done(((f32[4,8,2176]{2,1,0:T(8,128)}), f32[4,8,2176]{2,1,0:T(8,128)S(1)}, u32[]{:S(2)}, u32[]{:S(2)}) %all-to-all-start.1) | async-done | bytes 278560 | tf_op jit(solution)/shard_map/sum_far/all_to_all | solution.py:419
  71.0 0.1 sum_far.1
  71.1 0.0 collective-permute-done.4
  71.1 3.7 %collective-permute-done.5 = bf16[2,72,512]{2,1,0:T(8,128)(2,1)S(1)} collective-permute-done((bf16[2,72,512]{2,1,0:T(8,128)(2,1)S(1)}, bf16[2,72,512]{2,1,0:T(8,128)(2,1)S(1)}, u32[]{:S(2)}, u32[]{:S(2)}) %collective-permute-start.5) | collective-permute-done | bytes 147488 | tf_op jit(solution)/shard_map/window_out/ppermute | solution.py:422
  74.8 3.1 %collective-permute-done.6 = bf16[2,72,512]{2,1,0:T(8,128)(2,1)S(1)} collective-permute-done((bf16[2,72,512]{2,1,0:T(8,128)(2,1)S(1)}, bf16[2,72,512]{2,1,0:T(8,128)(2,1)S(1)}, u32[]{:S(2)}, u32[]{:S(2)}) %collective-permute-start.6) | collective-permute-done | bytes 147488 | tf_op jit(solution)/shard_map/window_out/ppermute | solution.py:422
  77.9 0.1 broadcast_in_dim.8
  78.0 20.6 %all_to_all.16 = bf16[32,8,2176]{2,1,0:T(8,128)(2,1)S(1)} all-to-all(bf16[32,8,2176]{2,1,0:T(8,128)(2,1)S(1)} %broadcast_in_dim.8), channel_id=1, replica_groups=mesh['xh'=2,'y'=4,'zh'=4,'zl'=2,'xl'=2,'core'=2] {'xh','y','zl','xl'}, dimensions={0} | all-to-all | bytes 2228224 | tf_op jit(solution)/shard_map/share/all_to_all | solution.py:435
  98.6 2.2 %collective-permute-start.7 = (bf16[256,2176]{1,0:T(8,128)(2,1)S(1)}, bf16[256,2176]{1,0:T(8,128)(2,1)S(1)}, u32[]{:S(2)}, u32[]{:S(2)}) collective-permute-start(bf16[256,2176]{1,0:T(8,128)(2,1)S(1)} %bitcast.7), channel_id=1, source_target_pairs={{0,1},{1,0},{2,3},{3,2},{4,5},{5,4},{6,7},{7,6},{8,9},{9,8},{10,11... | collective-permute-start | bytes 3342344 | tf_op jit(solution)/shard_map/share/ppermute | solution.py:437
  100.8 0.1 reshape.48
  100.9 0.1 reshape.49
  101.0 0.1 reshape.50
  101.0 0.7 reshape.51
  101.8 1.7 %maximum_maximum_fusion = bf16[2,12,12,2,512]{4,3,2,1,0:T(2,128)(2,1)S(1)} fusion(bf16[2,6,6,2,512]{4,3,2,1,0:T(2,128)(2,1)} %reshape.51, bf16[2,6,6,2,512]{4,3,2,1,0:T(2,128)(2,1)S(1)} %reshape.50, bf16[2,6,6,2,512]{4,3,2,1,0:T(2,128)(2,1)S(1)} %reshape.49, bf16[2,6,6,2,512]{4,3,2,1,0:T(2,128)(2,1)S(1)} %reshape.48), kind=kLoop, calls=%fused_computation.4 | loop fusion | flops 884736 | bytes 1179648 | tf_op jit(solution)/shard_map/window_out/concatenate | solution.py:443
  103.5 1.2 %fusion.2 = (bf16[1,12,12,2,512]{4,3,2,1,0:T(2,128)(2,1)}, bf16[1,12,12,2,512]{4,3,2,1,0:T(2,128)(2,1)}) fusion(bf16[2,12,12,2,512]{4,3,2,1,0:T(2,128)(2,1)S(1)} %maximum_maximum_fusion), kind=kLoop, calls=%fused_computation.11 | loop fusion | bytes 1179648 | tf_op jit(solution)/shard_map/window_out/slice | solution.py:444
  104.7 0.0 collective-permute-done.7.theirs
  104.7 2.5 %finish.1 = (bf16[512,1536]{1,0:T(8,128)(2,1)}, bf16[512,512]{1,0:T(8,128)(2,1)}, f32[1,512]{1,0:T(1,128)}) custom-call(s32[2]{0:T(128)S(1)} %pad_add_fusion.ids, bf16[256,2176]{1,0:T(8,128)(2,1)S(1)} %bitcast.8, bf16[256,2176]{1,0:T(8,128)(2,1)S(1)} %collective-permute-done.7.theirs), custom_call_target="tpu_custom_call" | custom-call | tf_op jit(solution)/shard_map/finish/pallas_call | solution.py:451
  (4 shorter events, 0.0 us)
Async XLA Ops:
  0.6 15.2 %copy-start = (bf16[512,1536]{1,0:T(8,128)(2,1)S(1)}, bf16[512,1536]{1,0:T(8,128)(2,1)}, u32[]{:S(2)}) copy-start(bf16[512,1536]{1,0:T(8,128)(2,1)} %wqkv.3) | copy-start | bytes 4718596
  0.6 15.2 %copy-start.1 = (bf16[512,512]{1,0:T(8,128)(2,1)S(1)}, bf16[512,512]{1,0:T(8,128)(2,1)}, u32[]{:S(2)}) copy-start(bf16[512,512]{1,0:T(8,128)(2,1)} %wout.3) | copy-start | bytes 1572868
  2.6 13.8 %collective-permute-start.1 = (bf16[2,72,512]{2,1,0:T(8,128)(2,1)S(1)}, bf16[2,72,512]{2,1,0:T(8,128)(2,1)S(1)}, u32[]{:S(2)}, u32[]{:S(2)}) collective-permute-start(bf16[2,72,512]{2,1,0:T(8,128)(2,1)S(1)} %reshape.44), channel_id=1, source_target_pairs={{0,224},{1,225},{2,226},{3,227},{4,228},{5,229},{6,230},{7,231},{8... | collective-permute-start | bytes 442376 | tf_op jit(solution)/shard_map/window_in/ppermute | solution.py:360
  9.0 7.4 %collective-permute-start.2 = (bf16[2,72,512]{2,1,0:T(8,128)(2,1)S(1)}, bf16[2,72,512]{2,1,0:T(8,128)(2,1)S(1)}, u32[]{:S(2)}, u32[]{:S(2)}) collective-permute-start(bf16[2,72,512]{2,1,0:T(8,128)(2,1)S(1)} %reshape.45), channel_id=1, source_target_pairs={{0,255},{1,224},{2,225},{3,226},{4,227},{5,228},{6,229},{7,230},{8... | collective-permute-start | bytes 442376 | tf_op jit(solution)/shard_map/window_in/ppermute | solution.py:360
  10.6 6.2 %copy-start.2 = (f32[512]{0:T(512)S(1)}, f32[512]{0:T(512)}, u32[]{:S(2)}) copy-start(f32[512]{0:T(512)} %param.6) | copy-start | bytes 6148
  10.7 6.1 %collective-permute-start = (bf16[2,72,512]{2,1,0:T(8,128)(2,1)S(1)}, bf16[2,72,512]{2,1,0:T(8,128)(2,1)S(1)}, u32[]{:S(2)}, u32[]{:S(2)}) collective-permute-start(bf16[2,72,512]{2,1,0:T(8,128)(2,1)S(1)} %reshape.43), channel_id=1, source_target_pairs={{0,31},{1,0},{2,1},{3,2},{4,3},{5,4},{6,5},{7,6},{8,7},{9,8},{10,9... | collective-permute-start | bytes 442376 | tf_op jit(solution)/shard_map/window_in/ppermute | solution.py:360
  26.2 5.3 %collective-permute-start.3 = (bf16[256,2176]{1,0:T(8,128)(2,1)S(1)}, bf16[256,2176]{1,0:T(8,128)(2,1)S(1)}, u32[]{:S(2)}, u32[]{:S(2)}) collective-permute-start(bf16[256,2176]{1,0:T(8,128)(2,1)S(1)} %get-tuple-element.35), channel_id=1, source_target_pairs={{0,1},{1,0},{2,3},{3,2},{4,5},{5,4},{6,7},{7,6},{8,9},{9,8},{10,11... | collective-permute-start | bytes 3342344 | tf_op jit(solution)/shard_map/sum_cores/ppermute | solution.py:398
  55.2 15.8 %all-to-all-start.1 = ((f32[4,8,2176]{2,1,0:T(8,128)}), f32[4,8,2176]{2,1,0:T(8,128)S(1)}, u32[]{:S(2)}, u32[]{:S(2)}) async-start(f32[4,8,2176]{2,1,0:T(8,128)} %broadcast_in_dim.7._), calls=%async_computation.1 | async-start | bytes 557056 | tf_op jit(solution)/shard_map/sum_far/all_to_all | solution.py:419
  63.4 7.7 %collective-permute-start.4 = (bf16[2,72,512]{2,1,0:T(8,128)(2,1)S(1)}, bf16[2,72,512]{2,1,0:T(8,128)(2,1)S(1)}, u32[]{:S(2)}, u32[]{:S(2)}) collective-permute-start(bf16[2,72,512]{2,1,0:T(8,128)(2,1)S(1)} %get-tuple-element.44), channel_id=1, source_target_pairs={{0,1},{1,2},{2,3},{3,4},{4,5},{5,6},{6,7},{7,8},{8,9},{9,10},{10,1... | collective-permute-start | bytes 442376 | tf_op jit(solution)/shard_map/window_out/ppermute | solution.py:422
  65.8 9.0 %collective-permute-start.5 = (bf16[2,72,512]{2,1,0:T(8,128)(2,1)S(1)}, bf16[2,72,512]{2,1,0:T(8,128)(2,1)S(1)}, u32[]{:S(2)}, u32[]{:S(2)}) collective-permute-start(bf16[2,72,512]{2,1,0:T(8,128)(2,1)S(1)} %get-tuple-element.45), channel_id=1, source_target_pairs={{0,32},{1,33},{2,34},{3,35},{4,36},{5,37},{6,38},{7,39},{8,40},{9,... | collective-permute-start | bytes 442376 | tf_op jit(solution)/shard_map/window_out/ppermute | solution.py:422
  66.1 11.9 %collective-permute-start.6 = (bf16[2,72,512]{2,1,0:T(8,128)(2,1)S(1)}, bf16[2,72,512]{2,1,0:T(8,128)(2,1)S(1)}, u32[]{:S(2)}, u32[]{:S(2)}) collective-permute-start(bf16[2,72,512]{2,1,0:T(8,128)(2,1)S(1)} %get-tuple-element.46), channel_id=1, source_target_pairs={{0,33},{1,34},{2,35},{3,36},{4,37},{5,38},{6,39},{7,40},{8,41},{9,... | collective-permute-start | bytes 442376 | tf_op jit(solution)/shard_map/window_out/ppermute | solution.py:422
  98.6 6.1 %collective-permute-start.7 = (bf16[256,2176]{1,0:T(8,128)(2,1)S(1)}, bf16[256,2176]{1,0:T(8,128)(2,1)S(1)}, u32[]{:S(2)}, u32[]{:S(2)}) collective-permute-start(bf16[256,2176]{1,0:T(8,128)(2,1)S(1)} %bitcast.7), channel_id=1, source_target_pairs={{0,1},{1,0},{2,3},{3,2},{4,5},{5,4},{6,7},{7,6},{8,9},{9,8},{10,11... | collective-permute-start | bytes 3342344 | tf_op jit(solution)/shard_map/share/ppermute | solution.py:437

commit v4 on v3

--- a/solution.py
+++ b/solution.py
@@ -62,7 +62,7 @@
 
 
 def grads_kernel(
-    ids, q0, q1, q2, q3, gain, wqkv, wqkv_t, wout,
+    q0, q1, q2, q3, gain, wqkv, wqkv_t, wout,
     keep, send, attn_t, back,
     wide, normed, normed_t, g_low, q_t, kv_t, kv, do_t, dq_t, dkv_t, gain_col,
     diag, side, bias, scores, d_probs, p_low, d_low, acc,
@@ -75,6 +75,8 @@
     size = feat // HEADS
     per = 128 // size
     half = tokens // 2
+    edge = lax.axis_index(LAT) == lax.axis_size(LAT) - 1
+    core = lax.axis_index("core")
     inv_root = 1.0 / math.sqrt(size)
     to_exp2 = inv_root * math.log2(math.e)
 
@@ -114,7 +116,7 @@
         jnp.logical_and(which == 0, jnp.logical_not(late_query)),
         jnp.logical_and(which == 1, late_query),
     )
-    bias[...] = jnp.where(jnp.logical_and(blocked, ids[0] == 1), MASKED, 0.0).astype(BF16)
+    bias[...] = jnp.where(jnp.logical_and(blocked, edge), MASKED, 0.0).astype(BF16)
 
     def spread(block, h):
         parts = []
@@ -216,8 +218,8 @@
     gain_col[...] = jnp.where(lanes(column.shape) < 2, column, 0.0)
 
     rows = feat // 2
-    mine = pl.multiple_of(ids[1] * rows, rows)
-    theirs = pl.multiple_of((1 - ids[1]) * rows, rows)
+    mine = pl.multiple_of(core * rows, rows)
+    theirs = pl.multiple_of((1 - core) * rows, rows)
 
     def partial_sums(start):
         pick = pl.ds(start, rows)
@@ -274,7 +276,7 @@
         last = last + added[at : at + left]
     mixed = tok + jnp.concatenate([added[:main], last], 0)
     for j, out in enumerate(outs):
-        out[0] = mixed[j * rows : (j + 1) * rows].astype(BF16)
+        out[0] = mixed[j * rows : (j + 1) * rows].astype(BF16).reshape(out.shape[1:])
     xhat, inv = normalise(tok)
     scaled = back[...].astype(F32) * gain[...]
     inner = (
@@ -285,53 +287,58 @@
     gather_quads(quads, 1, wide)
     grad = wide[...] + inv * inner
     for j, out in enumerate(outs):
-        out[1] = grad[j * rows : (j + 1) * rows].astype(BF16)
+        out[1] = grad[j * rows : (j + 1) * rows].astype(BF16).reshape(out.shape[1:])
 
 
 def gain_total(tile):
     return jnp.where(lanes(tile.shape) == 0, jnp.sum(tile, -1, keepdims=True), 0.0)
 
 
-def add_pair(keep, other):
-    total = keep + other.astype(F32)
-    rest = total - lax.reduce_precision(total, 8, 7)
-    return jnp.where(lanes(total.shape) == total.shape[1] - 127, rest, total).astype(BF16)
-
-
-def final_piece_kernel(factor, parts, _, out):
+def pair_kernel(keep, other, out):
+    main = keep.shape[1] - 128
+    for at in range(0, keep.shape[0], 16):
+        rows = slice(at, at + 16)
+        out[rows, :main] = (keep[rows, :main] + other[rows, :main].astype(F32)).astype(BF16)
+        total = keep[rows, main:] + other[rows, main:].astype(F32)
+        rest = total - total.astype(BF16).astype(F32)
+        out[rows, main:] = jnp.where(lanes(total.shape) == 1, rest, total).astype(BF16)
+
+
+def final_piece_kernel(factor, parts, out):
     main = parts.shape[2] - 128
     total = jnp.sum(parts[...], 0) * factor
     out[:, :main] = total[:, :main].astype(BF16)
     out[:, main:] = split_low(gain_total(total[:, main:]), 3)
 
 
-def finish_kernel(ids, mine, theirs, grad_qkv, grad_out, gain_grad, tails, sems):
+def finish_kernel(
+    mine, theirs, o0, o1, o2, o3, mixed, grad_tokens, grad_qkv, grad_out, gain_grad, gains, sems
+):
     rows = mine.shape[0]
     wide = grad_qkv.shape[1]
     main = wide + grad_out.shape[1]
+    core = lax.axis_index("core")
     copies = []
+
+    def copy(src, dst):
+        item = pltpu.make_async_copy(src, dst, sems.at[len(copies)])
+        item.start()
+        copies.append(item)
+
     for n, half in enumerate((mine, theirs)):
-        at = pl.multiple_of((ids[1] if n == 0 else 1 - ids[1]) * rows, rows)
-        for m, (src, dst) in enumerate(
-            (
-                (half.at[:, main:], tails.at[n]),
-                (half.at[:, :wide], grad_qkv.at[pl.ds(at, rows), :]),
-                (half.at[:, wide:main], grad_out.at[pl.ds(at, rows), :]),
-            )
-        ):
-            copy = pltpu.make_async_copy(src, dst, sems.at[3 * n + m])
-            copy.start()
-            copies.append((m, copy))
-    for m, copy in copies:
-        if m == 0:
-            copy.wait()
-    for n in range(2):
-        at = pl.multiple_of((ids[1] if n == 0 else 1 - ids[1]) * rows, rows)
-        column = tails[n].astype(F32).T
-        gain_grad[:, pl.ds(at, rows)] = column[0:1] + column[1:2] + column[2:3]
-    for m, copy in copies:
-        if m > 0:
-            copy.wait()
+        at = pl.multiple_of((core if n == 0 else 1 - core) * rows, rows)
+        copy(half.at[:, :wide], grad_qkv.at[pl.ds(at, rows), :])
+        copy(half.at[:, wide:main], grad_out.at[pl.ds(at, rows), :])
+        column = half[:, main:].astype(F32).T
+        gains[:, pl.ds(at, rows)] = column[0:1] + column[1:2] + column[2:3]
+    copy(gains, gain_grad)
+    for n, quad in enumerate((o0, o1, o2, o3)):
+        lat = slice(0, SHIFT) if n // 2 else slice(SHIFT, 2 * SHIFT)
+        lon = slice(0, SHIFT) if n % 2 else slice(SHIFT, 2 * SHIFT)
+        copy(quad.at[0], mixed.at[0, lat, lon])
+        copy(quad.at[1], grad_tokens.at[0, lat, lon])
+    for item in copies:
+        item.wait()
 
 
 def shards(tokens, layer_norm_gain, cotangent, w_qkv, w_out):
@@ -361,10 +368,7 @@
             for q, s in zip(quads, shifts)
         ]
     gain_row = layer_norm_gain[None, :]
-    core = lax.axis_index("core")
-    ids = jnp.stack([(lax.axis_index(LAT) == lat_n - 1).astype(jnp.int32), core.astype(jnp.int32)])
     vmem = pl.BlockSpec(memory_space=pltpu.VMEM)
-    smem = pl.BlockSpec(memory_space=pltpu.SMEM)
     hbm = pl.BlockSpec(memory_space=pl.ANY)
     params = pltpu.CompilerParams(vmem_limit_bytes=40 * 1024 * 1024)
     rows, width = feat // 2, 4 * feat + 128
@@ -382,7 +386,7 @@
     with jax.named_scope("window_grads"):
         keep, send, attn_t, back = pl.pallas_call(
             grads_kernel,
-            in_specs=[smem] + [vmem] * 8,
+            in_specs=[vmem] * 8,
             out_specs=[vmem] * 4,
             out_shape=[
                 jax.ShapeDtypeStruct((rows, width), F32),
@@ -392,7 +396,7 @@
             ],
             scratch_shapes=grads_scratch(n_tokens, feat),
             compiler_params=params,
-        )(ids, *quads, gain_row, w_qkv, w_qkv_t, w_out_near)
+        )(*quads, gain_row, w_qkv, w_qkv_t, w_out_near)
     swap = [(0, 1), (1, 0)]
     with jax.named_scope("sum_cores"):
         other = lax.ppermute(send, "core", swap)
@@ -401,61 +405,62 @@
             tokens_kernel,
             in_specs=[vmem] * 8,
             out_specs=[vmem] * 4,
-            out_shape=[jax.ShapeDtypeStruct((2, quad_tokens, feat), BF16)] * 4,
+            out_shape=[jax.ShapeDtypeStruct((2, SHIFT, SHIFT, levels, feat), BF16)] * 4,
             scratch_shapes=[pltpu.VMEM((n_tokens, feat), F32)],
             compiler_params=params,
         )(*quads, gain_row, w_out, attn_t, back)
     with jax.named_scope("sum_cores"):
-        pair_sum = add_pair(keep, other)
+        pair_sum = pl.pallas_call(
+            pair_kernel,
+            in_specs=[vmem] * 2,
+            out_specs=vmem,
+            out_shape=jax.ShapeDtypeStruct((rows, width), BF16),
+            compiler_params=params,
+        )(keep, other)
+    pair_sum, *outs = lax.optimization_barrier((pair_sum, *outs))
+    with jax.named_scope("window_out"):
+        outs = [
+            q if s == (0, 0) else lax.ppermute(q, EVERY, pairs(s[0], s[1]))
+            for q, s in zip(outs, shifts)
+        ]
     near, far = lax.axis_size(NEAR), lax.axis_size(FAR)
     factor = 1.0 / math.sqrt(lat_n * lat_rows * lon_n * lon_cols * levels)
     chunk = rows // near
     with jax.named_scope("sum_near"):
         pieces = lax.all_to_all(pair_sum.reshape(near, chunk, width), NEAR, 0, 0)
+        pieces, *outs = lax.optimization_barrier((pieces, *outs))
         piece = jnp.sum(pieces.astype(F32), 0)
         piece = jnp.broadcast_to(piece[None], (far, chunk, width))
-    after, *outs = lax.optimization_barrier((piece, *outs))
     with jax.named_scope("sum_far"):
         parts = lax.all_to_all(piece, FAR, 0, 0)
-    with jax.named_scope("window_out"):
-        outs = [
-            q if s == (0, 0) else lax.ppermute(q, EVERY, pairs(s[0], s[1]))
-            for q, s in zip(outs, shifts)
-        ]
     with jax.named_scope("sum_far"):
         piece = pl.pallas_call(
             functools.partial(final_piece_kernel, factor),
-            in_specs=[vmem, hbm],
+            in_specs=[vmem],
             out_specs=vmem,
             out_shape=jax.ShapeDtypeStruct((chunk, width), BF16),
             compiler_params=params,
-        )(parts, after)
-    piece, *outs = lax.optimization_barrier((piece, *outs))
+        )(parts)
     with jax.named_scope("share"):
         mine = lax.all_to_all(jnp.broadcast_to(piece[None], (near,) + piece.shape), NEAR, 0, 0)
         mine = mine.reshape(rows, width)
         theirs = lax.ppermute(mine, "core", swap)
-    outs = lax.optimization_barrier((mine, *outs))[1:]
-    with jax.named_scope("window_out"):
-        blocks = [o.reshape(2, SHIFT, SHIFT, levels, feat) for o in outs]
-        lower = jnp.concatenate([blocks[1], blocks[0]], 2)
-        upper = jnp.concatenate([blocks[3], blocks[2]], 2)
-        both = jnp.concatenate([upper, lower], 1)
-        mixed, grad_tokens = both[0][None], both[1][None]
-    final = [
-        jax.ShapeDtypeStruct((feat, 3 * feat), BF16),
-        jax.ShapeDtypeStruct((feat, feat), BF16),
-        jax.ShapeDtypeStruct((1, feat), F32),
-    ]
     with jax.named_scope("finish"):
-        grad_qkv, grad_out, gain_gradient = pl.pallas_call(
+        shape = (1, 2 * SHIFT, 2 * SHIFT, levels, feat)
+        mixed, grad_tokens, grad_qkv, grad_out, gain_gradient = pl.pallas_call(
             finish_kernel,
-            in_specs=[smem, hbm, hbm],
-            out_specs=[hbm, hbm, vmem],
-            out_shape=final,
-            scratch_shapes=[pltpu.VMEM((2, rows, 128), BF16), pltpu.SemaphoreType.DMA((6,))],
-            compiler_params=params,
-        )(ids, mine, theirs)
+            in_specs=[vmem] * 2 + [hbm] * 4,
+            out_specs=[hbm] * 5,
+            out_shape=[
+                jax.ShapeDtypeStruct(shape, BF16),
+                jax.ShapeDtypeStruct(shape, BF16),
+                jax.ShapeDtypeStruct((feat, 3 * feat), BF16),
+                jax.ShapeDtypeStruct((feat, feat), BF16),
+                jax.ShapeDtypeStruct((1, feat), F32),
+            ],
+            scratch_shapes=[pltpu.VMEM((1, feat), F32), pltpu.SemaphoreType.DMA((13,))],
+            compiler_params=params,
+        )(mine, theirs, *outs)
     return mixed, grad_tokens, gain_gradient[0], grad_qkv, grad_out
 
 

time: 108 us -> 109 us (level)
  waiting for transfers between devices: 13.8 us -> 26 us
  blocking collectives: 43 us -> 38.2 us
  local copies, waits for them, and re-layouts: 4.89 us -> 1.92 us
  other arithmetic: 3.26 us -> 0.99 us
  starting transfers between devices: 28.5 us -> 27.2 us
    ppermute x3, waiting for transfers between devices: 6.84 us -> 20.6 us  [shards(): lax.ppermute(q, EVERY, pairs(s[0], s[1]))]
    all_to_all x1, blocking collectives: 22.3 us -> 17 us  [shards(): parts = lax.all_to_all(piece, FAR, 0, 0)]
    all_to_all x1, waiting for transfers between devices: 4.15 us -> 0.01 us  [shards(): pieces = lax.all_to_all(pair_sum.reshape(near, chunk, width), NEAR, 0, 0)]
    ppermute x1, waiting for transfers between devices: 0.01 us -> 2.38 us  [shards(): theirs = lax.ppermute(mine, 'core', swap)]
    concatenate x1 -> x0, other arithmetic: 1.75 us -> none  [shards(): both = jnp.concatenate([upper, lower], 1)]
    ppermute x1, starting transfers between devices: 2.91 us -> 1.61 us  [shards(): other = lax.ppermute(send, 'core', swap)]
    all_to_all x1, starting transfers between devices: 7.59 us -> 6.34 us  [shards(): pieces = lax.all_to_all(pair_sum.reshape(near, chunk, width), NEAR, 0, 0)]
    slice x1 -> x0, local copies, waits for them, and re-layouts: 1.22 us -> none  [shards(): mixed, grad_tokens = (both[0][None], both[1][None])]
  transfers between devices with their start and end apart: 9 -> 9, of which waited for: 5 -> 6; matrix products, arithmetic and copies ran while one was open for 4% -> 1% of each run, Pallas kernels for 1% -> 1%
where the time goes in v4:
time: 109 us; the launch traced here: 108 us
  blocking collectives  38.2 us (35%)
  starting transfers between devices  27.2 us (25%)
  waiting for transfers between devices  26 us (24%)
  Pallas kernels  13 us (12%)
  local copies, waits for them, and re-layouts  1.92 us (2%)
    all_to_all x1, blocking collectives, shards(): lax.all_to_all(jnp.broadcast_to(piece[None], (near,) + piece.shape), NEAR...  21.2 us
    ppermute x3, waiting for transfers between devices, shards(): lax.ppermute(q, EVERY, pairs(s[0], s[1]))  20.6 us
    all_to_all x1, blocking collectives, shards(): parts = lax.all_to_all(piece, FAR, 0, 0)  17 us
    ppermute x3, starting transfers between devices, shards(): lax.ppermute(q, EVERY, pairs(-s[0], -s[1]))  13.4 us
    pallas_call x1, Pallas kernels, shards(): pl.pallas_call(grads_kernel, in_specs=[vmem] * 8, out_specs=[vmem] * 4, o...  8.9 us
    all_to_all x1, starting transfers between devices, shards(): pieces = lax.all_to_all(pair_sum.reshape(near, chunk, width), NEAR, 0, 0)  6.34 us
    ppermute x3, starting transfers between devices, shards(): lax.ppermute(q, EVERY, pairs(s[0], s[1]))  4.58 us
    ppermute x1, waiting for transfers between devices, shards(): theirs = lax.ppermute(mine, 'core', swap)  2.38 us
  transfers between devices with their start and end apart: 9, of which 6 were waited for; matrix products, arithmetic and copies ran while one was open for 1% of the time, Pallas kernels for 1%

profile of v4, /device:TPU:1, one launch (start us, length us, event | category | flops | bytes accessed | tf_op | source)
XLA Modules:
  0.0 108.2 jit_solution(4905431250916044947)
XLA Ops:
  0.6 1.6 %fusion = (bf16[1,6,6,2,512]{4,3,2,1,0:T(2,128)(2,1)S(1)}, bf16[1,6,6,2,512]{4,3,2,1,0:T(2,128)(2,1)S(1)}, bf16[1,6,6,2,512]{4,3,2,1,0:T(2,128)(2,1)S(1)}, bf16[...) fusion(bf16[1,12,12,2,512]{4,3,2,1,0:T(2,128)(2,1)} %param.5, ...), kind=kLoop, calls=%fused_computation.5 | loop fusion | bytes 1179648 | tf_op jit(solution)/shard_map/window_in/slice | solution.py:359
  2.2 0.0 copy-start
  2.2 0.0 copy-start.1
  2.2 0.2 pad_maximum_fusion.2
  2.4 0.1 reshape.32
  2.5 6.1 %collective-permute-start.1 = (bf16[2,72,512]{2,1,0:T(8,128)(2,1)S(1)}, bf16[2,72,512]{2,1,0:T(8,128)(2,1)S(1)}, u32[]{:S(2)}, u32[]{:S(2)}) collective-permute-start(bf16[2,72,512]{2,1,0:T(8,128)(2,1)S(1)} %reshape.32), channel_id=1, source_target_pairs={{0,224},{1,225},{2,226},{3,227},{4,228},{5,229},{6,230},{7,231},{8... | collective-permute-start | bytes 442376 | tf_op jit(solution)/shard_map/window_in/ppermute | solution.py:367
  8.6 0.2 pad_maximum_fusion.1
  8.8 0.1 reshape.31
  8.9 1.0 collective-permute-start
  9.9 0.2 pad_maximum_fusion.3
  10.1 0.1 reshape.33
  10.2 6.3 %collective-permute-start.2 = (bf16[2,72,512]{2,1,0:T(8,128)(2,1)S(1)}, bf16[2,72,512]{2,1,0:T(8,128)(2,1)S(1)}, u32[]{:S(2)}, u32[]{:S(2)}) collective-permute-start(bf16[2,72,512]{2,1,0:T(8,128)(2,1)S(1)} %reshape.33), channel_id=1, source_target_pairs={{0,255},{1,224},{2,225},{3,226},{4,227},{5,228},{6,229},{7,230},{8... | collective-permute-start | bytes 442376 | tf_op jit(solution)/shard_map/window_in/ppermute | solution.py:367
  16.4 0.2 pad_maximum_fusion
  16.7 0.1 reshape.30.q0
  16.7 0.0 copy-done
  16.7 0.0 copy-done.1
  16.7 0.0 copy-start.2
  16.8 0.5 weights.1
  17.2 0.0 collective-permute-done.1.q2
  17.2 0.0 collective-permute-done.q1
  17.2 1.3 %collective-permute-done.2.q3 = bf16[2,72,512]{2,1,0:T(8,128)(2,1)S(1)} collective-permute-done((bf16[2,72,512]{2,1,0:T(8,128)(2,1)S(1)}, bf16[2,72,512]{2,1,0:T(8,128)(2,1)S(1)}, u32[]{:S(2)}, u32[]{:S(2)}) %collective-permute-start.2) | collective-permute-done | bytes 147488 | tf_op jit(solution)/shard_map/window_in/ppermute | solution.py:367
  18.5 0.0 copy-done.2
  18.6 8.9 %window_grads.1 = (f32[256,2176]{1,0:T(8,128)S(1)}, bf16[256,2176]{1,0:T(8,128)(2,1)S(1)}, bf16[512,384]{1,0:T(8,128)(2,1)S(1)}, bf16[288,512]{1,0:T(8,128)(2,1)S(1)}) custom-call(bf16[2,72,512]{2,1,0:T(8,128)(2,1)S(1)} %reshape.30.q0, bf16[2,72,512]{2,1,0:T(8,128)(2,1)S(1)} %collective-permute-done.q1, bf16[2,72,512]{2,1,0:T(8,128)(2,1)S(1)} %collective-permute-done.1.q2, ...), custom_call_target="tpu_custom_call" | custom-call | tf_op jit(solution)/shard_map/window_grads/pallas_call | solution.py:387
  27.5 1.6 %collective-permute-start.3 = (bf16[256,2176]{1,0:T(8,128)(2,1)S(1)}, bf16[256,2176]{1,0:T(8,128)(2,1)S(1)}, u32[]{:S(2)}, u32[]{:S(2)}) collective-permute-start(bf16[256,2176]{1,0:T(8,128)(2,1)S(1)} %get-tuple-element.33), channel_id=1, source_target_pairs={{0,1},{1,0},{2,3},{3,2},{4,5},{5,4},{6,7},{7,6},{8,9},{9,8},{10,11... | collective-permute-start | bytes 3342344 | tf_op jit(solution)/shard_map/sum_cores/ppermute | solution.py:402
  29.1 0.7 window_tokens.1
  29.8 1.7 %collective-permute-done.3.other = bf16[256,2176]{1,0:T(8,128)(2,1)S(1)} collective-permute-done((bf16[256,2176]{1,0:T(8,128)(2,1)S(1)}, bf16[256,2176]{1,0:T(8,128)(2,1)S(1)}, u32[]{:S(2)}, u32[]{:S(2)}) %collective-permute-start.3) | collective-permute-done | bytes 1114144 | tf_op jit(solution)/shard_map/sum_cores/ppermute | solution.py:402
  31.4 1.2 %sum_cores.1 = bf16[256,2176]{1,0:T(8,128)(2,1)} custom-call(f32[256,2176]{1,0:T(8,128)S(1)} %get-tuple-element.32.keep, bf16[256,2176]{1,0:T(8,128)(2,1)S(1)} %collective-permute-done.3.other), custom_call_target="tpu_custom_call" | custom-call | tf_op jit(solution)/shard_map/sum_cores/pallas_call | solution.py:413
  32.7 6.3 %all-to-all-start = ((bf16[32,8,2176]{2,1,0:T(8,128)(2,1)}), bf16[32,8,2176]{2,1,0:T(8,128)(2,1)S(1)}, u32[]{:S(2)}, u32[]{:S(2)}) async-start(bf16[32,8,2176]{2,1,0:T(8,128)(2,1)} %bitcast.1), calls=%async_computation | async-start | bytes 2228224 | tf_op jit(solution)/shard_map/sum_near/all_to_all | solution.py:430
  39.0 2.1 %collective-permute-start.4 = (bf16[2,6,6,2,512]{4,3,2,1,0:T(2,128)(2,1)S(1)}, bf16[2,6,6,2,512]{4,3,2,1,0:T(2,128)(2,1)S(1)}, u32[]{:S(2)}, u32[]{:S(2)}) collective-permute-start(bf16[2,6,6,2,512]{4,3,2,1,0:T(2,128)(2,1)S(1)} %get-tuple-element.42), channel_id=1, source_target_pairs={{0,1},{1,2},{2,3},{3,4},{4,5},{5,6},{6,7},{7,8},{8,9},{9,10},{10,1... | collective-permute-start | bytes 442376 | tf_op jit(solution)/shard_map/window_out/ppermute | solution.py:423
  41.2 1.2 %collective-permute-start.5 = (bf16[2,6,6,2,512]{4,3,2,1,0:T(2,128)(2,1)S(1)}, bf16[2,6,6,2,512]{4,3,2,1,0:T(2,128)(2,1)S(1)}, u32[]{:S(2)}, u32[]{:S(2)}) collective-permute-start(bf16[2,6,6,2,512]{4,3,2,1,0:T(2,128)(2,1)S(1)} %get-tuple-element.43), channel_id=1, source_target_pairs={{0,32},{1,33},{2,34},{3,35},{4,36},{5,37},{6,38},{7,39},{8,40},{9,... | collective-permute-start | bytes 442376 | tf_op jit(solution)/shard_map/window_out/ppermute | solution.py:423
  42.3 1.3 %collective-permute-start.6 = (bf16[2,6,6,2,512]{4,3,2,1,0:T(2,128)(2,1)S(1)}, bf16[2,6,6,2,512]{4,3,2,1,0:T(2,128)(2,1)S(1)}, u32[]{:S(2)}, u32[]{:S(2)}) collective-permute-start(bf16[2,6,6,2,512]{4,3,2,1,0:T(2,128)(2,1)S(1)} %get-tuple-element.44), channel_id=1, source_target_pairs={{0,33},{1,34},{2,35},{3,36},{4,37},{5,38},{6,39},{7,40},{8,41},{9,... | collective-permute-start | bytes 442376 | tf_op jit(solution)/shard_map/window_out/ppermute | solution.py:423
  43.6 9.4 %collective-permute-done.4.o1 = bf16[2,6,6,2,512]{4,3,2,1,0:T(2,128)(2,1)S(1)} collective-permute-done((bf16[2,6,6,2,512]{4,3,2,1,0:T(2,128)(2,1)S(1)}, bf16[2,6,6,2,512]{4,3,2,1,0:T(2,128)(2,1)S(1)}, u32[]{:S(2)}, u32[]{:S(2)}) %collective-permute-start.4) | collective-permute-done | bytes 147488 | tf_op jit(solution)/shard_map/window_out/ppermute | solution.py:423
  53.0 10.0 %collective-permute-done.5.o2 = bf16[2,6,6,2,512]{4,3,2,1,0:T(2,128)(2,1)S(1)} collective-permute-done((bf16[2,6,6,2,512]{4,3,2,1,0:T(2,128)(2,1)S(1)}, bf16[2,6,6,2,512]{4,3,2,1,0:T(2,128)(2,1)S(1)}, u32[]{:S(2)}, u32[]{:S(2)}) %collective-permute-start.5) | collective-permute-done | bytes 147488 | tf_op jit(solution)/shard_map/window_out/ppermute | solution.py:423
  63.1 1.1 %collective-permute-done.6.o3 = bf16[2,6,6,2,512]{4,3,2,1,0:T(2,128)(2,1)S(1)} collective-permute-done((bf16[2,6,6,2,512]{4,3,2,1,0:T(2,128)(2,1)S(1)}, bf16[2,6,6,2,512]{4,3,2,1,0:T(2,128)(2,1)S(1)}, u32[]{:S(2)}, u32[]{:S(2)}) %collective-permute-start.6) | collective-permute-done | bytes 147488 | tf_op jit(solution)/shard_map/window_out/ppermute | solution.py:423
  64.2 0.0 all-to-all-done
  64.2 0.2 convert_reduce_fusion
  64.4 17.0 %all_to_all.15.parts = f32[4,8,2176]{2,1,0:T(8,128)S(1)} all-to-all(f32[4,8,2176]{2,1,0:T(8,128)S(1)} %broadcast_in_dim.7), channel_id=1, replica_groups=mesh['xh'=2,'y'=4,'zh'=4,'zl'=2,'xl'=2,'core'=2] {'zh'}, dimensions={0} | all-to-all | bytes 557056 | tf_op jit(solution)/shard_map/sum_far/all_to_all | solution.py:435
  81.3 0.1 sum_far.1
  81.5 0.1 broadcast_in_dim.8
  81.5 21.2 %all_to_all.16 = bf16[32,8,2176]{2,1,0:T(8,128)(2,1)S(1)} all-to-all(bf16[32,8,2176]{2,1,0:T(8,128)(2,1)S(1)} %broadcast_in_dim.8), channel_id=1, replica_groups=mesh['xh'=2,'y'=4,'zh'=4,'zl'=2,'xl'=2,'core'=2] {'xh','y','zl','xl'}, dimensions={0} | all-to-all | bytes 2228224 | tf_op jit(solution)/shard_map/share/all_to_all | solution.py:445
  102.7 1.3 %collective-permute-start.7 = (bf16[256,2176]{1,0:T(8,128)(2,1)S(1)}, bf16[256,2176]{1,0:T(8,128)(2,1)S(1)}, u32[]{:S(2)}, u32[]{:S(2)}) collective-permute-start(bf16[256,2176]{1,0:T(8,128)(2,1)S(1)} %bitcast.4), channel_id=1, source_target_pairs={{0,1},{1,0},{2,3},{3,2},{4,5},{5,4},{6,7},{7,6},{8,9},{9,8},{10,11... | collective-permute-start | bytes 3342344 | tf_op jit(solution)/shard_map/share/ppermute | solution.py:447
  104.1 2.4 %collective-permute-done.7.theirs = bf16[256,2176]{1,0:T(8,128)(2,1)S(1)} collective-permute-done((bf16[256,2176]{1,0:T(8,128)(2,1)S(1)}, bf16[256,2176]{1,0:T(8,128)(2,1)S(1)}, u32[]{:S(2)}, u32[]{:S(2)}) %collective-permute-start.7) | collective-permute-done | bytes 1114144 | tf_op jit(solution)/shard_map/share/ppermute | solution.py:447
  106.4 1.6 %finish.1 = (bf16[1,12,12,2,512]{4,3,2,1,0:T(2,128)(2,1)}, bf16[1,12,12,2,512]{4,3,2,1,0:T(2,128)(2,1)}, bf16[512,1536]{1,0:T(8,128)(2,1)}, bf16[512,512]{1,0:T(8,128)(2,1)}, f32[1,512]{1,0:T(1,128)}) custom-call(bf16[256,2176]{1,0:T(8,128)(2,1)S(1)} %bitcast.5, bf16[256,2176]{1,0:T(8,128)(2,1)S(1)} %collective-permute-done.7.theirs, ...), custom_call_target="tpu_custom_call" | custom-call | tf_op jit(solution)/shard_map/finish/pallas_call | solution.py:450
  (1 shorter events, 0.0 us)
Async XLA Ops:
  2.2 14.5 %copy-start = (bf16[512,1536]{1,0:T(8,128)(2,1)S(1)}, bf16[512,1536]{1,0:T(8,128)(2,1)}, u32[]{:S(2)}) copy-start(bf16[512,1536]{1,0:T(8,128)(2,1)} %wqkv.3) | copy-start | bytes 4718596
  2.2 14.5 %copy-start.1 = (bf16[512,512]{1,0:T(8,128)(2,1)S(1)}, bf16[512,512]{1,0:T(8,128)(2,1)}, u32[]{:S(2)}) copy-start(bf16[512,512]{1,0:T(8,128)(2,1)} %wout.3) | copy-start | bytes 1572868
  2.5 14.7 %collective-permute-start.1 = (bf16[2,72,512]{2,1,0:T(8,128)(2,1)S(1)}, bf16[2,72,512]{2,1,0:T(8,128)(2,1)S(1)}, u32[]{:S(2)}, u32[]{:S(2)}) collective-permute-start(bf16[2,72,512]{2,1,0:T(8,128)(2,1)S(1)} %reshape.32), channel_id=1, source_target_pairs={{0,224},{1,225},{2,226},{3,227},{4,228},{5,229},{6,230},{7,231},{8... | collective-permute-start | bytes 442376 | tf_op jit(solution)/shard_map/window_in/ppermute | solution.py:367
  8.9 8.4 %collective-permute-start = (bf16[2,72,512]{2,1,0:T(8,128)(2,1)S(1)}, bf16[2,72,512]{2,1,0:T(8,128)(2,1)S(1)}, u32[]{:S(2)}, u32[]{:S(2)}) collective-permute-start(bf16[2,72,512]{2,1,0:T(8,128)(2,1)S(1)} %reshape.31), channel_id=1, source_target_pairs={{0,31},{1,0},{2,1},{3,2},{4,3},{5,4},{6,5},{7,6},{8,7},{9,8},{10,9... | collective-permute-start | bytes 442376 | tf_op jit(solution)/shard_map/window_in/ppermute | solution.py:367
  10.2 8.4 %collective-permute-start.2 = (bf16[2,72,512]{2,1,0:T(8,128)(2,1)S(1)}, bf16[2,72,512]{2,1,0:T(8,128)(2,1)S(1)}, u32[]{:S(2)}, u32[]{:S(2)}) collective-permute-start(bf16[2,72,512]{2,1,0:T(8,128)(2,1)S(1)} %reshape.33), channel_id=1, source_target_pairs={{0,255},{1,224},{2,225},{3,226},{4,227},{5,228},{6,229},{7,230},{8... | collective-permute-start | bytes 442376 | tf_op jit(solution)/shard_map/window_in/ppermute | solution.py:367
  16.7 1.8 %copy-start.2 = (f32[512]{0:T(512)S(1)}, f32[512]{0:T(512)}, u32[]{:S(2)}) copy-start(f32[512]{0:T(512)} %param.6) | copy-start | bytes 6148
  27.5 4.0 %collective-permute-start.3 = (bf16[256,2176]{1,0:T(8,128)(2,1)S(1)}, bf16[256,2176]{1,0:T(8,128)(2,1)S(1)}, u32[]{:S(2)}, u32[]{:S(2)}) collective-permute-start(bf16[256,2176]{1,0:T(8,128)(2,1)S(1)} %get-tuple-element.33), channel_id=1, source_target_pairs={{0,1},{1,0},{2,3},{3,2},{4,5},{5,4},{6,7},{7,6},{8,9},{9,8},{10,11... | collective-permute-start | bytes 3342344 | tf_op jit(solution)/shard_map/sum_cores/ppermute | solution.py:402
  32.7 31.5 %all-to-all-start = ((bf16[32,8,2176]{2,1,0:T(8,128)(2,1)}), bf16[32,8,2176]{2,1,0:T(8,128)(2,1)S(1)}, u32[]{:S(2)}, u32[]{:S(2)}) async-start(bf16[32,8,2176]{2,1,0:T(8,128)(2,1)} %bitcast.1), calls=%async_computation | async-start | bytes 2228224 | tf_op jit(solution)/shard_map/sum_near/all_to_all | solution.py:430
  39.0 14.0 %collective-permute-start.4 = (bf16[2,6,6,2,512]{4,3,2,1,0:T(2,128)(2,1)S(1)}, bf16[2,6,6,2,512]{4,3,2,1,0:T(2,128)(2,1)S(1)}, u32[]{:S(2)}, u32[]{:S(2)}) collective-permute-start(bf16[2,6,6,2,512]{4,3,2,1,0:T(2,128)(2,1)S(1)} %get-tuple-element.42), channel_id=1, source_target_pairs={{0,1},{1,2},{2,3},{3,4},{4,5},{5,6},{6,7},{7,8},{8,9},{9,10},{10,1... | collective-permute-start | bytes 442376 | tf_op jit(solution)/shard_map/window_out/ppermute | solution.py:423
  41.2 21.9 %collective-permute-start.5 = (bf16[2,6,6,2,512]{4,3,2,1,0:T(2,128)(2,1)S(1)}, bf16[2,6,6,2,512]{4,3,2,1,0:T(2,128)(2,1)S(1)}, u32[]{:S(2)}, u32[]{:S(2)}) collective-permute-start(bf16[2,6,6,2,512]{4,3,2,1,0:T(2,128)(2,1)S(1)} %get-tuple-element.43), channel_id=1, source_target_pairs={{0,32},{1,33},{2,34},{3,35},{4,36},{5,37},{6,38},{7,39},{8,40},{9,... | collective-permute-start | bytes 442376 | tf_op jit(solution)/shard_map/window_out/ppermute | solution.py:423
  42.3 21.9 %collective-permute-start.6 = (bf16[2,6,6,2,512]{4,3,2,1,0:T(2,128)(2,1)S(1)}, bf16[2,6,6,2,512]{4,3,2,1,0:T(2,128)(2,1)S(1)}, u32[]{:S(2)}, u32[]{:S(2)}) collective-permute-start(bf16[2,6,6,2,512]{4,3,2,1,0:T(2,128)(2,1)S(1)} %get-tuple-element.44), channel_id=1, source_target_pairs={{0,33},{1,34},{2,35},{3,36},{4,37},{5,38},{6,39},{7,40},{8,41},{9,... | collective-permute-start | bytes 442376 | tf_op jit(solution)/shard_map/window_out/ppermute | solution.py:423
  102.7 3.7 %collective-permute-start.7 = (bf16[256,2176]{1,0:T(8,128)(2,1)S(1)}, bf16[256,2176]{1,0:T(8,128)(2,1)S(1)}, u32[]{:S(2)}, u32[]{:S(2)}) collective-permute-start(bf16[256,2176]{1,0:T(8,128)(2,1)S(1)} %bitcast.4), channel_id=1, source_target_pairs={{0,1},{1,0},{2,3},{3,2},{4,5},{5,4},{6,7},{7,6},{8,9},{9,8},{10,11... | collective-permute-start | bytes 3342344 | tf_op jit(solution)/shard_map/share/ppermute | solution.py:447

commit v5 on v4

--- a/solution.py
+++ b/solution.py
@@ -294,19 +294,15 @@
     return jnp.where(lanes(tile.shape) == 0, jnp.sum(tile, -1, keepdims=True), 0.0)
 
 
-def pair_kernel(keep, other, out):
-    main = keep.shape[1] - 128
-    for at in range(0, keep.shape[0], 16):
-        rows = slice(at, at + 16)
-        out[rows, :main] = (keep[rows, :main] + other[rows, :main].astype(F32)).astype(BF16)
-        total = keep[rows, main:] + other[rows, main:].astype(F32)
-        rest = total - total.astype(BF16).astype(F32)
-        out[rows, main:] = jnp.where(lanes(total.shape) == 1, rest, total).astype(BF16)
-
-
-def final_piece_kernel(factor, parts, out):
-    main = parts.shape[2] - 128
-    total = jnp.sum(parts[...], 0) * factor
+def add_pair(keep, other):
+    total = keep + other.astype(F32)
+    rest = total - lax.reduce_precision(total, 8, 7)
+    return jnp.where(lanes(total.shape) == total.shape[1] - 127, rest, total).astype(BF16)
+
+
+def final_piece_kernel(factor, mine, next1, next2, next3, _, out):
+    main = mine.shape[1] - 128
+    total = ((mine[...] + next2[...]) + (next1[...] + next3[...])) * factor
     out[:, :main] = total[:, :main].astype(BF16)
     out[:, main:] = split_low(gain_total(total[:, main:]), 3)
 
@@ -410,37 +406,34 @@
             compiler_params=params,
         )(*quads, gain_row, w_out, attn_t, back)
     with jax.named_scope("sum_cores"):
-        pair_sum = pl.pallas_call(
-            pair_kernel,
-            in_specs=[vmem] * 2,
-            out_specs=vmem,
-            out_shape=jax.ShapeDtypeStruct((rows, width), BF16),
-            compiler_params=params,
-        )(keep, other)
+        pair_sum = add_pair(keep, other)
     pair_sum, *outs = lax.optimization_barrier((pair_sum, *outs))
+    near, far = lax.axis_size(NEAR), lax.axis_size(FAR)
+    factor = 1.0 / math.sqrt(lat_n * lat_rows * lon_n * lon_cols * levels)
+    chunk = rows // near
+    with jax.named_scope("sum_near"):
+        pieces = lax.all_to_all(pair_sum.reshape(near, chunk, width), NEAR, 0, 0)
+        piece = jnp.sum(pieces.astype(F32), 0)
+    with jax.named_scope("sum_far"):
+        others = [
+            lax.ppermute(piece, FAR, [(i, (i + by) % far) for i in range(far)])
+            for by in range(1, far)
+        ]
+    after, *outs = lax.optimization_barrier((piece, *outs))
     with jax.named_scope("window_out"):
         outs = [
             q if s == (0, 0) else lax.ppermute(q, EVERY, pairs(s[0], s[1]))
             for q, s in zip(outs, shifts)
         ]
-    near, far = lax.axis_size(NEAR), lax.axis_size(FAR)
-    factor = 1.0 / math.sqrt(lat_n * lat_rows * lon_n * lon_cols * levels)
-    chunk = rows // near
-    with jax.named_scope("sum_near"):
-        pieces = lax.all_to_all(pair_sum.reshape(near, chunk, width), NEAR, 0, 0)
-        pieces, *outs = lax.optimization_barrier((pieces, *outs))
-        piece = jnp.sum(pieces.astype(F32), 0)
-        piece = jnp.broadcast_to(piece[None], (far, chunk, width))
-    with jax.named_scope("sum_far"):
-        parts = lax.all_to_all(piece, FAR, 0, 0)
     with jax.named_scope("sum_far"):
         piece = pl.pallas_call(
             functools.partial(final_piece_kernel, factor),
-            in_specs=[vmem],
+            in_specs=[vmem] * far + [hbm],
             out_specs=vmem,
             out_shape=jax.ShapeDtypeStruct((chunk, width), BF16),
             compiler_params=params,
-        )(parts)
+        )(piece, *others, after)
+    piece, *outs = lax.optimization_barrier((piece, *outs))
     with jax.named_scope("share"):
         mine = lax.all_to_all(jnp.broadcast_to(piece[None], (near,) + piece.shape), NEAR, 0, 0)
         mine = mine.reshape(rows, width)

time: 109 us -> 106 us (0.972)
  waiting for transfers between devices: 26 us -> 10.2 us
  blocking collectives: 38.2 us -> 50.3 us
  starting transfers between devices: 27.2 us -> 29 us
  Pallas kernels: 13 us -> 11.8 us
    ppermute x3, waiting for transfers between devices: 20.6 us -> 0.01 us  [shards(): lax.ppermute(q, EVERY, pairs(s[0], s[1]))]
    ppermute x0 -> x3, starting transfers between devices: none -> 8.43 us  [shards(): lax.ppermute(piece, FAR, [(i, (i + by) % far) for i in range(far)])]
    all_to_all x1, blocking collectives: 21.2 us -> 28 us  [shards(): lax.all_to_all(jnp.broadcast_to(piece[None], (near,) + piece.shape), NEAR...]
    all_to_all x1 -> x0, starting transfers between devices: 6.34 us -> none  [shards(): pieces = lax.all_to_all(pair_sum.reshape(near, chunk, width), NEAR, 0, 0)]
    ppermute x0 -> x3, waiting for transfers between devices: none -> 5.66 us  [shards(): lax.ppermute(piece, FAR, [(i, (i + by) % far) for i in range(far)])]
    all_to_all x1, blocking collectives: 17 us -> 22.3 us  [shards(): pieces = lax.all_to_all(pair_sum.reshape(near, chunk, width), NEAR, 0, 0)]
    ppermute x3, starting transfers between devices: 4.58 us -> 3.19 us  [shards(): lax.ppermute(q, EVERY, pairs(s[0], s[1]))]
    ppermute x1, starting transfers between devices: 1.61 us -> 2.9 us  [shards(): other = lax.ppermute(send, 'core', swap)]
  transfers between devices with their start and end apart: 9 -> 11, of which waited for: 6 -> 6; matrix products, arithmetic and copies ran while one was open for 1% -> 1% of each run, Pallas kernels for 1% -> 1%
where the time goes in v5:
time: 106 us
  blocking collectives  50.3 us (47%)
  starting transfers between devices  29 us (27%)
  Pallas kernels  11.8 us (11%)
  waiting for transfers between devices  10.2 us (10%)
  local copies, waits for them, and re-layouts  2.04 us (2%)
  other arithmetic  1.43 us (1%)
    all_to_all x1, blocking collectives, shards(): lax.all_to_all(jnp.broadcast_to(piece[None], (near,) + piece.shape), NEAR...  28 us
    all_to_all x1, blocking collectives, shards(): pieces = lax.all_to_all(pair_sum.reshape(near, chunk, width), NEAR, 0, 0)  22.3 us
    ppermute x3, starting transfers between devices, shards(): lax.ppermute(q, EVERY, pairs(-s[0], -s[1]))  12.3 us
    pallas_call x1, Pallas kernels, shards(): pl.pallas_call(grads_kernel, in_specs=[vmem] * 8, out_specs=[vmem] * 4, o...  8.88 us
    ppermute x3, starting transfers between devices, shards(): lax.ppermute(piece, FAR, [(i, (i + by) % far) for i in range(far)])  8.43 us
    ppermute x3, waiting for transfers between devices, shards(): lax.ppermute(piece, FAR, [(i, (i + by) % far) for i in range(far)])  5.66 us
    ppermute x3, starting transfers between devices, shards(): lax.ppermute(q, EVERY, pairs(s[0], s[1]))  3.19 us
    ppermute x1, starting transfers between devices, shards(): other = lax.ppermute(send, 'core', swap)  2.9 us
  transfers between devices with their start and end apart: 11, of which 6 were waited for; matrix products, arithmetic and copies ran while one was open for 1% of the time, Pallas kernels for 1%

profile of v5, /device:TPU:1, one launch (start us, length us, event | category | flops | bytes accessed | tf_op | source)
XLA Modules:
  0.0 105.7 jit_solution(14922784822234448664)
XLA Ops:
  0.6 0.0 copy-start
  0.6 0.0 copy-start.1
  0.7 1.7 %fusion.1 = (bf16[1,6,6,2,512]{4,3,2,1,0:T(2,128)(2,1)S(1)}, bf16[1,6,6,2,512]{4,3,2,1,0:T(2,128)(2,1)S(1)}, bf16[1,6,6,2,512]{4,3,2,1,0:T(2,128)(2,1)S(1)}, bf1...) fusion(bf16[1,12,12,2,512]{4,3,2,1,0:T(2,128)(2,1)} %param.5, ...), kind=kLoop, calls=%fused_computation.8 | loop fusion | bytes 1179648 | tf_op jit(solution)/shard_map/window_in/slice | solution.py:355
  2.4 0.2 pad_maximum_fusion.2
  2.6 0.1 reshape.31
  2.6 6.1 %collective-permute-start.1 = (bf16[2,72,512]{2,1,0:T(8,128)(2,1)S(1)}, bf16[2,72,512]{2,1,0:T(8,128)(2,1)S(1)}, u32[]{:S(2)}, u32[]{:S(2)}) collective-permute-start(bf16[2,72,512]{2,1,0:T(8,128)(2,1)S(1)} %reshape.31), channel_id=1, source_target_pairs={{0,224},{1,225},{2,226},{3,227},{4,228},{5,229},{6,230},{7,231},{8... | collective-permute-start | bytes 442376 | tf_op jit(solution)/shard_map/window_in/ppermute | solution.py:363
  8.7 0.2 pad_maximum_fusion.3
  8.9 0.1 reshape.32
  9.0 1.4 %collective-permute-start.2 = (bf16[2,72,512]{2,1,0:T(8,128)(2,1)S(1)}, bf16[2,72,512]{2,1,0:T(8,128)(2,1)S(1)}, u32[]{:S(2)}, u32[]{:S(2)}) collective-permute-start(bf16[2,72,512]{2,1,0:T(8,128)(2,1)S(1)} %reshape.32), channel_id=1, source_target_pairs={{0,255},{1,224},{2,225},{3,226},{4,227},{5,228},{6,229},{7,230},{8... | collective-permute-start | bytes 442376 | tf_op jit(solution)/shard_map/window_in/ppermute | solution.py:363
  10.4 0.0 copy-start.2
  10.4 0.2 pad_maximum_fusion.1
  10.6 0.1 reshape.30
  10.7 4.8 %collective-permute-start = (bf16[2,72,512]{2,1,0:T(8,128)(2,1)S(1)}, bf16[2,72,512]{2,1,0:T(8,128)(2,1)S(1)}, u32[]{:S(2)}, u32[]{:S(2)}) collective-permute-start(bf16[2,72,512]{2,1,0:T(8,128)(2,1)S(1)} %reshape.30), channel_id=1, source_target_pairs={{0,31},{1,0},{2,1},{3,2},{4,3},{5,4},{6,5},{7,6},{8,7},{9,8},{10,9... | collective-permute-start | bytes 442376 | tf_op jit(solution)/shard_map/window_in/ppermute | solution.py:363
  15.5 0.2 pad_maximum_fusion
  15.7 0.1 reshape.29.q0
  15.8 0.0 copy-done
  15.8 0.0 copy-done.1
  15.8 0.5 weights.1
  16.3 0.0 collective-permute-done.1.q2
  16.3 0.0 collective-permute-done.2.q3
  16.3 0.5 collective-permute-done.q1
  16.8 0.0 copy-done.2
  16.8 8.9 %window_grads.1 = (f32[256,2176]{1,0:T(8,128)S(1)}, bf16[256,2176]{1,0:T(8,128)(2,1)S(1)}, bf16[512,384]{1,0:T(8,128)(2,1)S(1)}, bf16[288,512]{1,0:T(8,128)(2,1)S(1)}) custom-call(bf16[2,72,512]{2,1,0:T(8,128)(2,1)S(1)} %reshape.29.q0, bf16[2,72,512]{2,1,0:T(8,128)(2,1)S(1)} %collective-permute-done.q1, bf16[2,72,512]{2,1,0:T(8,128)(2,1)S(1)} %collective-permute-done.1.q2, ...), custom_call_target="tpu_custom_call" | custom-call | tf_op jit(solution)/shard_map/window_grads/pallas_call | solution.py:383
  25.7 2.9 %collective-permute-start.3 = (bf16[256,2176]{1,0:T(8,128)(2,1)S(1)}, bf16[256,2176]{1,0:T(8,128)(2,1)S(1)}, u32[]{:S(2)}, u32[]{:S(2)}) collective-permute-start(bf16[256,2176]{1,0:T(8,128)(2,1)S(1)} %get-tuple-element.38), channel_id=1, source_target_pairs={{0,1},{1,0},{2,3},{3,2},{4,5},{5,4},{6,7},{7,6},{8,9},{9,8},{10,11... | collective-permute-start | bytes 3342344 | tf_op jit(solution)/shard_map/sum_cores/ppermute | solution.py:398
  28.6 0.7 window_tokens.1
  29.3 1.7 %collective-permute-done.3 = bf16[256,2176]{1,0:T(8,128)(2,1)S(1)} collective-permute-done((bf16[256,2176]{1,0:T(8,128)(2,1)S(1)}, bf16[256,2176]{1,0:T(8,128)(2,1)S(1)}, u32[]{:S(2)}, u32[]{:S(2)}) %collective-permute-start.3) | collective-permute-done | bytes 1114144 | tf_op jit(solution)/shard_map/sum_cores/ppermute | solution.py:398
  31.0 0.4 fusion
  31.4 22.3 %all_to_all.10 = bf16[32,8,2176]{2,1,0:T(8,128)(2,1)S(1)} all-to-all(bf16[32,8,2176]{2,1,0:T(8,128)(2,1)S(1)} %bitcast.8), channel_id=1, replica_groups=mesh['xh'=2,'y'=4,'zh'=4,'zl'=2,'xl'=2,'core'=2] {'xh','y','zl','xl'}, dimensions={0} | all-to-all | bytes 2228224 | tf_op jit(solution)/shard_map/sum_near/all_to_all | solution.py:415
  53.7 0.2 convert_reduce_fusion.mine._
  53.9 2.1 %collective-permute-start.7 = (bf16[2,6,6,2,512]{4,3,2,1,0:T(2,128)(2,1)S(1)}, bf16[2,6,6,2,512]{4,3,2,1,0:T(2,128)(2,1)S(1)}, u32[]{:S(2)}, u32[]{:S(2)}) collective-permute-start(bf16[2,6,6,2,512]{4,3,2,1,0:T(2,128)(2,1)S(1)} %get-tuple-element.52), channel_id=1, source_target_pairs={{0,1},{1,2},{2,3},{3,4},{4,5},{5,6},{6,7},{7,8},{8,9},{9,10},{10,1... | collective-permute-start | bytes 442376 | tf_op jit(solution)/shard_map/window_out/ppermute | solution.py:425
  56.0 0.3 collective-permute-start.8
  56.3 0.8 collective-permute-start.9
  57.1 3.0 %collective-permute-start.4 = (f32[8,2176]{1,0:T(8,128)S(1)}, f32[8,2176]{1,0:T(8,128)S(1)}, u32[]{:S(2)}, u32[]{:S(2)}) collective-permute-start(f32[8,2176]{1,0:T(8,128)S(1)} %convert_reduce_fusion.mine._), channel_id=1, source_target_pairs={{0,8},{8,16},{16,24},{24,0},{1,9},{9,17},{17,25},{25,1},{2,10},{10... | collective-permute-start | bytes 208904 | tf_op jit(solution)/shard_map/sum_far/ppermute | solution.py:419
  60.1 4.3 %collective-permute-start.5 = (f32[8,2176]{1,0:T(8,128)S(1)}, f32[8,2176]{1,0:T(8,128)S(1)}, u32[]{:S(2)}, u32[]{:S(2)}) collective-permute-start(f32[8,2176]{1,0:T(8,128)S(1)} %convert_reduce_fusion.mine._), channel_id=1, source_target_pairs={{0,16},{8,24},{16,0},{24,8},{1,17},{9,25},{17,1},{25,9},{2,18},{10... | collective-permute-start | bytes 208904 | tf_op jit(solution)/shard_map/sum_far/ppermute | solution.py:419
  64.3 1.5 %collective-permute-done.4.next1 = f32[8,2176]{1,0:T(8,128)S(1)} collective-permute-done((f32[8,2176]{1,0:T(8,128)S(1)}, f32[8,2176]{1,0:T(8,128)S(1)}, u32[]{:S(2)}, u32[]{:S(2)}) %collective-permute-start.4) | collective-permute-done | bytes 69664 | tf_op jit(solution)/shard_map/sum_far/ppermute | solution.py:419
  65.8 1.2 %collective-permute-start.6 = (f32[8,2176]{1,0:T(8,128)S(1)}, f32[8,2176]{1,0:T(8,128)S(1)}, u32[]{:S(2)}, u32[]{:S(2)}) collective-permute-start(f32[8,2176]{1,0:T(8,128)S(1)} %convert_reduce_fusion.mine._), channel_id=1, source_target_pairs={{0,24},{8,0},{16,8},{24,16},{1,25},{9,1},{17,9},{25,17},{2,26},{10... | collective-permute-start | bytes 208904 | tf_op jit(solution)/shard_map/sum_far/ppermute | solution.py:419
  67.0 2.4 %collective-permute-done.5.next2 = f32[8,2176]{1,0:T(8,128)S(1)} collective-permute-done((f32[8,2176]{1,0:T(8,128)S(1)}, f32[8,2176]{1,0:T(8,128)S(1)}, u32[]{:S(2)}, u32[]{:S(2)}) %collective-permute-start.5) | collective-permute-done | bytes 69664 | tf_op jit(solution)/shard_map/sum_far/ppermute | solution.py:419
  69.4 1.8 %collective-permute-done.6.next3 = f32[8,2176]{1,0:T(8,128)S(1)} collective-permute-done((f32[8,2176]{1,0:T(8,128)S(1)}, f32[8,2176]{1,0:T(8,128)S(1)}, u32[]{:S(2)}, u32[]{:S(2)}) %collective-permute-start.6) | collective-permute-done | bytes 69664 | tf_op jit(solution)/shard_map/sum_far/ppermute | solution.py:419
  71.2 0.1 sum_far.1
  71.3 0.0 collective-permute-done.7.o1
  71.3 0.0 collective-permute-done.8.o2
  71.3 0.0 collective-permute-done.9.o3
  71.3 0.1 broadcast_in_dim.10
  71.4 28.0 %all_to_all.11 = bf16[32,8,2176]{2,1,0:T(8,128)(2,1)S(1)} all-to-all(bf16[32,8,2176]{2,1,0:T(8,128)(2,1)S(1)} %broadcast_in_dim.10), channel_id=1, replica_groups=mesh['xh'=2,'y'=4,'zh'=4,'zl'=2,'xl'=2,'core'=2] {'xh','y','zl','xl'}, dimensions={0} | all-to-all | bytes 2228224 | tf_op jit(solution)/shard_map/share/all_to_all | solution.py:438
  99.4 2.1 %collective-permute-start.10 = (bf16[256,2176]{1,0:T(8,128)(2,1)S(1)}, bf16[256,2176]{1,0:T(8,128)(2,1)S(1)}, u32[]{:S(2)}, u32[]{:S(2)}) collective-permute-start(bf16[256,2176]{1,0:T(8,128)(2,1)S(1)} %bitcast.4), channel_id=1, source_target_pairs={{0,1},{1,0},{2,3},{3,2},{4,5},{5,4},{6,7},{7,6},{8,9},{9,8},{10,11... | collective-permute-start | bytes 3342344 | tf_op jit(solution)/shard_map/share/ppermute | solution.py:440
  101.5 2.4 %collective-permute-done.10.theirs = bf16[256,2176]{1,0:T(8,128)(2,1)S(1)} collective-permute-done((bf16[256,2176]{1,0:T(8,128)(2,1)S(1)}, bf16[256,2176]{1,0:T(8,128)(2,1)S(1)}, u32[]{:S(2)}, u32[]{:S(2)}) %collective-permute-start.10) | collective-permute-done | bytes 1114144 | tf_op jit(solution)/shard_map/share/ppermute | solution.py:440
  103.9 1.6 %finish.1 = (bf16[1,12,12,2,512]{4,3,2,1,0:T(2,128)(2,1)}, bf16[1,12,12,2,512]{4,3,2,1,0:T(2,128)(2,1)}, bf16[512,1536]{1,0:T(8,128)(2,1)}, bf16[512,512]{1,0:T(8,128)(2,1)}, f32[1,512]{1,0:T(1,128)}) custom-call(bf16[256,2176]{1,0:T(8,128)(2,1)S(1)} %bitcast.5, bf16[256,2176]{1,0:T(8,128)(2,1)S(1)} %collective-permute-done.10.theirs, ...), custom_call_target="tpu_custom_call" | custom-call | tf_op jit(solution)/shard_map/finish/pallas_call | solution.py:443
  (1 shorter events, 0.0 us)
Async XLA Ops:
  0.6 15.2 %copy-start = (bf16[512,1536]{1,0:T(8,128)(2,1)S(1)}, bf16[512,1536]{1,0:T(8,128)(2,1)}, u32[]{:S(2)}) copy-start(bf16[512,1536]{1,0:T(8,128)(2,1)} %wqkv.3) | copy-start | bytes 4718596
  0.6 15.2 %copy-start.1 = (bf16[512,512]{1,0:T(8,128)(2,1)S(1)}, bf16[512,512]{1,0:T(8,128)(2,1)}, u32[]{:S(2)}) copy-start(bf16[512,512]{1,0:T(8,128)(2,1)} %wout.3) | copy-start | bytes 1572868
  2.6 13.7 %collective-permute-start.1 = (bf16[2,72,512]{2,1,0:T(8,128)(2,1)S(1)}, bf16[2,72,512]{2,1,0:T(8,128)(2,1)S(1)}, u32[]{:S(2)}, u32[]{:S(2)}) collective-permute-start(bf16[2,72,512]{2,1,0:T(8,128)(2,1)S(1)} %reshape.31), channel_id=1, source_target_pairs={{0,224},{1,225},{2,226},{3,227},{4,228},{5,229},{6,230},{7,231},{8... | collective-permute-start | bytes 442376 | tf_op jit(solution)/shard_map/window_in/ppermute | solution.py:363
  9.0 7.3 %collective-permute-start.2 = (bf16[2,72,512]{2,1,0:T(8,128)(2,1)S(1)}, bf16[2,72,512]{2,1,0:T(8,128)(2,1)S(1)}, u32[]{:S(2)}, u32[]{:S(2)}) collective-permute-start(bf16[2,72,512]{2,1,0:T(8,128)(2,1)S(1)} %reshape.32), channel_id=1, source_target_pairs={{0,255},{1,224},{2,225},{3,226},{4,227},{5,228},{6,229},{7,230},{8... | collective-permute-start | bytes 442376 | tf_op jit(solution)/shard_map/window_in/ppermute | solution.py:363
  10.4 6.4 %copy-start.2 = (f32[512]{0:T(512)S(1)}, f32[512]{0:T(512)}, u32[]{:S(2)}) copy-start(f32[512]{0:T(512)} %param.6) | copy-start | bytes 6148
  10.7 6.1 %collective-permute-start = (bf16[2,72,512]{2,1,0:T(8,128)(2,1)S(1)}, bf16[2,72,512]{2,1,0:T(8,128)(2,1)S(1)}, u32[]{:S(2)}, u32[]{:S(2)}) collective-permute-start(bf16[2,72,512]{2,1,0:T(8,128)(2,1)S(1)} %reshape.30), channel_id=1, source_target_pairs={{0,31},{1,0},{2,1},{3,2},{4,3},{5,4},{6,5},{7,6},{8,7},{9,8},{10,9... | collective-permute-start | bytes 442376 | tf_op jit(solution)/shard_map/window_in/ppermute | solution.py:363
  25.7 5.3 %collective-permute-start.3 = (bf16[256,2176]{1,0:T(8,128)(2,1)S(1)}, bf16[256,2176]{1,0:T(8,128)(2,1)S(1)}, u32[]{:S(2)}, u32[]{:S(2)}) collective-permute-start(bf16[256,2176]{1,0:T(8,128)(2,1)S(1)} %get-tuple-element.38), channel_id=1, source_target_pairs={{0,1},{1,0},{2,3},{3,2},{4,5},{5,4},{6,7},{7,6},{8,9},{9,8},{10,11... | collective-permute-start | bytes 3342344 | tf_op jit(solution)/shard_map/sum_cores/ppermute | solution.py:398
  53.9 17.4 %collective-permute-start.7 = (bf16[2,6,6,2,512]{4,3,2,1,0:T(2,128)(2,1)S(1)}, bf16[2,6,6,2,512]{4,3,2,1,0:T(2,128)(2,1)S(1)}, u32[]{:S(2)}, u32[]{:S(2)}) collective-permute-start(bf16[2,6,6,2,512]{4,3,2,1,0:T(2,128)(2,1)S(1)} %get-tuple-element.52), channel_id=1, source_target_pairs={{0,1},{1,2},{2,3},{3,4},{4,5},{5,6},{6,7},{7,8},{8,9},{9,10},{10,1... | collective-permute-start | bytes 442376 | tf_op jit(solution)/shard_map/window_out/ppermute | solution.py:425
  56.0 15.3 %collective-permute-start.8 = (bf16[2,6,6,2,512]{4,3,2,1,0:T(2,128)(2,1)S(1)}, bf16[2,6,6,2,512]{4,3,2,1,0:T(2,128)(2,1)S(1)}, u32[]{:S(2)}, u32[]{:S(2)}) collective-permute-start(bf16[2,6,6,2,512]{4,3,2,1,0:T(2,128)(2,1)S(1)} %get-tuple-element.53), channel_id=1, source_target_pairs={{0,32},{1,33},{2,34},{3,35},{4,36},{5,37},{6,38},{7,39},{8,40},{9,... | collective-permute-start | bytes 442376 | tf_op jit(solution)/shard_map/window_out/ppermute | solution.py:425
  56.3 15.0 %collective-permute-start.9 = (bf16[2,6,6,2,512]{4,3,2,1,0:T(2,128)(2,1)S(1)}, bf16[2,6,6,2,512]{4,3,2,1,0:T(2,128)(2,1)S(1)}, u32[]{:S(2)}, u32[]{:S(2)}) collective-permute-start(bf16[2,6,6,2,512]{4,3,2,1,0:T(2,128)(2,1)S(1)} %get-tuple-element.54), channel_id=1, source_target_pairs={{0,33},{1,34},{2,35},{3,36},{4,37},{5,38},{6,39},{7,40},{8,41},{9,... | collective-permute-start | bytes 442376 | tf_op jit(solution)/shard_map/window_out/ppermute | solution.py:425
  57.1 8.7 %collective-permute-start.4 = (f32[8,2176]{1,0:T(8,128)S(1)}, f32[8,2176]{1,0:T(8,128)S(1)}, u32[]{:S(2)}, u32[]{:S(2)}) collective-permute-start(f32[8,2176]{1,0:T(8,128)S(1)} %convert_reduce_fusion.mine._), channel_id=1, source_target_pairs={{0,8},{8,16},{16,24},{24,0},{1,9},{9,17},{17,25},{25,1},{2,10},{10... | collective-permute-start | bytes 208904 | tf_op jit(solution)/shard_map/sum_far/ppermute | solution.py:419
  60.1 9.3 %collective-permute-start.5 = (f32[8,2176]{1,0:T(8,128)S(1)}, f32[8,2176]{1,0:T(8,128)S(1)}, u32[]{:S(2)}, u32[]{:S(2)}) collective-permute-start(f32[8,2176]{1,0:T(8,128)S(1)} %convert_reduce_fusion.mine._), channel_id=1, source_target_pairs={{0,16},{8,24},{16,0},{24,8},{1,17},{9,25},{17,1},{25,9},{2,18},{10... | collective-permute-start | bytes 208904 | tf_op jit(solution)/shard_map/sum_far/ppermute | solution.py:419
  65.8 5.4 %collective-permute-start.6 = (f32[8,2176]{1,0:T(8,128)S(1)}, f32[8,2176]{1,0:T(8,128)S(1)}, u32[]{:S(2)}, u32[]{:S(2)}) collective-permute-start(f32[8,2176]{1,0:T(8,128)S(1)} %convert_reduce_fusion.mine._), channel_id=1, source_target_pairs={{0,24},{8,0},{16,8},{24,16},{1,25},{9,1},{17,9},{25,17},{2,26},{10... | collective-permute-start | bytes 208904 | tf_op jit(solution)/shard_map/sum_far/ppermute | solution.py:419
  99.4 4.5 %collective-permute-start.10 = (bf16[256,2176]{1,0:T(8,128)(2,1)S(1)}, bf16[256,2176]{1,0:T(8,128)(2,1)S(1)}, u32[]{:S(2)}, u32[]{:S(2)}) collective-permute-start(bf16[256,2176]{1,0:T(8,128)(2,1)S(1)} %bitcast.4), channel_id=1, source_target_pairs={{0,1},{1,0},{2,3},{3,2},{4,5},{5,4},{6,7},{7,6},{8,9},{9,8},{10,11... | collective-permute-start | bytes 3342344 | tf_op jit(solution)/shard_map/share/ppermute | solution.py:440

commit v6 on v5

--- a/solution.py
+++ b/solution.py
@@ -75,8 +75,8 @@
     size = feat // HEADS
     per = 128 // size
     half = tokens // 2
-    edge = lax.axis_index(LAT) == lax.axis_size(LAT) - 1
     core = lax.axis_index("core")
+    edge = lax.axis_index(LAT) == jnp.where(core == 0, lax.axis_size(LAT) - 1, 0)
     inv_root = 1.0 / math.sqrt(size)
     to_exp2 = inv_root * math.log2(math.e)
 
@@ -263,8 +263,8 @@
     ]
 
 
-def tokens_kernel(q0, q1, q2, q3, gain, wout, attn_t, back, o0, o1, o2, o3, wide):
-    quads, outs = (q0, q1, q2, q3), (o0, o1, o2, o3)
+def tokens_kernel(q0, q1, q2, q3, gain, wout, attn_t, back, own, east, north, wide):
+    quads, outs = (q0, q1, q2, q3), (own, east, north.at[0], north.at[1])
     rows = q0.shape[1]
     gather_quads(quads, 0, wide)
     tok = wide[...]
@@ -307,8 +307,14 @@
     out[:, main:] = split_low(gain_total(total[:, main:]), 3)
 
 
+def half_rows(core):
+    first = jnp.where(core == 0, SHIFT, 0)
+    return first, SHIFT - first
+
+
 def finish_kernel(
-    mine, theirs, o0, o1, o2, o3, mixed, grad_tokens, grad_qkv, grad_out, gain_grad, gains, sems
+    mine, theirs, own, north, east,
+    mixed, grad_tokens, grad_qkv, grad_out, gain_grad, gains, sems,
 ):
     rows = mine.shape[0]
     wide = grad_qkv.shape[1]
@@ -328,11 +334,16 @@
         column = half[:, main:].astype(F32).T
         gains[:, pl.ds(at, rows)] = column[0:1] + column[1:2] + column[2:3]
     copy(gains, gain_grad)
-    for n, quad in enumerate((o0, o1, o2, o3)):
-        lat = slice(0, SHIFT) if n // 2 else slice(SHIFT, 2 * SHIFT)
-        lon = slice(0, SHIFT) if n % 2 else slice(SHIFT, 2 * SHIFT)
-        copy(quad.at[0], mixed.at[0, lat, lon])
-        copy(quad.at[1], grad_tokens.at[0, lat, lon])
+    own_rows, other_rows = half_rows(core)
+    for quad, at, lon in (
+        (own, own_rows, SHIFT),
+        (north.at[0], other_rows, SHIFT),
+        (east.at[0], other_rows, 0),
+        (east.at[1], own_rows, 0),
+    ):
+        block = (0, pl.ds(at, SHIFT), pl.ds(lon, SHIFT))
+        copy(quad.at[0], mixed.at[block])
+        copy(quad.at[1], grad_tokens.at[block])
     for item in copies:
         item.wait()
 
@@ -342,26 +353,36 @@
     lat_n, lon_n = lax.axis_size(LAT), lax.axis_size(LON)
     quad_tokens = SHIFT * SHIFT * levels
     n_tokens = 4 * quad_tokens
-    keep_part, go_part = slice(SHIFT, lat_rows), slice(0, SHIFT)
-
-    def pairs(d_lat, d_lon):
+    own_rows, other_rows = half_rows(lax.axis_index("core"))
+
+    def towards(lon):
+        return 1 if lon % 2 == 0 else -1
+
+    def pairs(target):
         return [
-            (a * lon_n + o, (a + d_lat) % lat_n * lon_n + (o + d_lon) % lon_n)
+            (a * lon_n + o, target(a, o)[0] % lat_n * lon_n + target(a, o)[1] % lon_n)
             for a in range(lat_n)
             for o in range(lon_n)
         ]
 
-    def quad(rows, cols):
-        both = jnp.stack([tokens[0, rows, cols], cotangent[0, rows, cols]])
-        return both.reshape(2, quad_tokens, feat)
-
-    shifts = ((0, 0), (0, 1), (1, 0), (1, 1))
-    cuts = [(go_part if a else keep_part, go_part if o else keep_part) for a, o in shifts]
+    def quad(first, cols):
+        both = [
+            lax.dynamic_slice_in_dim(full[0, :, cols], first, SHIFT, 0)
+            for full in (tokens, cotangent)
+        ]
+        return jnp.stack(both).reshape(2, quad_tokens, feat)
+
+    near_cols, far_cols = slice(SHIFT, lon_cols), slice(0, SHIFT)
     with jax.named_scope("window_in"):
-        quads = [quad(*cut) for cut in cuts]
         quads = [
-            q if s == (0, 0) else lax.ppermute(q, EVERY, pairs(-s[0], -s[1]))
-            for q, s in zip(quads, shifts)
+            quad(own_rows, near_cols),
+            lax.ppermute(quad(other_rows, far_cols), EVERY, pairs(lambda a, o: (a, o - 1))),
+            lax.ppermute(
+                quad(other_rows, near_cols), EVERY, pairs(lambda a, o: (a - towards(o), o))
+            ),
+            lax.ppermute(
+                quad(own_rows, far_cols), EVERY, pairs(lambda a, o: (a - towards(o - 1), o - 1))
+            ),
         ]
     gain_row = layer_norm_gain[None, :]
     vmem = pl.BlockSpec(memory_space=pltpu.VMEM)
@@ -397,17 +418,20 @@
     with jax.named_scope("sum_cores"):
         other = lax.ppermute(send, "core", swap)
     with jax.named_scope("window_tokens"):
-        outs = pl.pallas_call(
+        own, east, north = pl.pallas_call(
             tokens_kernel,
             in_specs=[vmem] * 8,
-            out_specs=[vmem] * 4,
-            out_shape=[jax.ShapeDtypeStruct((2, SHIFT, SHIFT, levels, feat), BF16)] * 4,
+            out_specs=[vmem] * 3,
+            out_shape=[
+                jax.ShapeDtypeStruct(lead + (2, SHIFT, SHIFT, levels, feat), BF16)
+                for lead in ((), (), (2,))
+            ],
             scratch_shapes=[pltpu.VMEM((n_tokens, feat), F32)],
             compiler_params=params,
         )(*quads, gain_row, w_out, attn_t, back)
     with jax.named_scope("sum_cores"):
         pair_sum = add_pair(keep, other)
-    pair_sum, *outs = lax.optimization_barrier((pair_sum, *outs))
+    pair_sum, north = lax.optimization_barrier((pair_sum, north))
     near, far = lax.axis_size(NEAR), lax.axis_size(FAR)
     factor = 1.0 / math.sqrt(lat_n * lat_rows * lon_n * lon_cols * levels)
     chunk = rows // near
@@ -419,12 +443,9 @@
             lax.ppermute(piece, FAR, [(i, (i + by) % far) for i in range(far)])
             for by in range(1, far)
         ]
-    after, *outs = lax.optimization_barrier((piece, *outs))
+    after, north = lax.optimization_barrier((piece, north))
     with jax.named_scope("window_out"):
-        outs = [
-            q if s == (0, 0) else lax.ppermute(q, EVERY, pairs(s[0], s[1]))
-            for q, s in zip(outs, shifts)
-        ]
+        north = lax.ppermute(north, EVERY, pairs(lambda a, o: (a + towards(o), o)))
     with jax.named_scope("sum_far"):
         piece = pl.pallas_call(
             functools.partial(final_piece_kernel, factor),
@@ -433,7 +454,10 @@
             out_shape=jax.ShapeDtypeStruct((chunk, width), BF16),
             compiler_params=params,
         )(piece, *others, after)
-    piece, *outs = lax.optimization_barrier((piece, *outs))
+    piece, north = lax.optimization_barrier((piece, north))
+    with jax.named_scope("window_out"):
+        east = jnp.stack([east, north[1]])
+        east = lax.ppermute(east, EVERY, pairs(lambda a, o: (a, o + 1)))
     with jax.named_scope("share"):
         mine = lax.all_to_all(jnp.broadcast_to(piece[None], (near,) + piece.shape), NEAR, 0, 0)
         mine = mine.reshape(rows, width)
@@ -442,7 +466,7 @@
         shape = (1, 2 * SHIFT, 2 * SHIFT, levels, feat)
         mixed, grad_tokens, grad_qkv, grad_out, gain_gradient = pl.pallas_call(
             finish_kernel,
-            in_specs=[vmem] * 2 + [hbm] * 4,
+            in_specs=[vmem] * 2 + [hbm] * 3,
             out_specs=[hbm] * 5,
             out_shape=[
                 jax.ShapeDtypeStruct(shape, BF16),
@@ -453,7 +477,7 @@
             ],
             scratch_shapes=[pltpu.VMEM((1, feat), F32), pltpu.SemaphoreType.DMA((13,))],
             compiler_params=params,
-        )(mine, theirs, *outs)
+        )(mine, theirs, own, north, east)
     return mixed, grad_tokens, gain_gradient[0], grad_qkv, grad_out
 
 

time: 106 us -> 104 us (0.981)
  the two profiles are of different devices: /device:TPU:1 before, /device:TPU:8 now
where the time goes in v6:
time: 104 us
  blocking collectives  49.8 us (48%)
  starting transfers between devices  20.8 us (20%)
  waiting for transfers between devices  16.3 us (16%)
  Pallas kernels  11.8 us (11%)
  local copies, waits for them, and re-layouts  3.46 us (3%)
  other arithmetic  1.07 us (1%)
    all_to_all x1, blocking collectives, shards(): pieces = lax.all_to_all(pair_sum.reshape(near, chunk, width), NEAR, 0, 0)  27 us
    all_to_all x1, blocking collectives, shards(): lax.all_to_all(jnp.broadcast_to(piece[None], (near,) + piece.shape), NEAR...  22.8 us
    pallas_call x1, Pallas kernels, shards(): pl.pallas_call(grads_kernel, in_specs=[vmem] * 8, out_specs=[vmem] * 4, o...  8.89 us
    ppermute x3, starting transfers between devices, shards(): lax.ppermute(piece, FAR, [(i, (i + by) % far) for i in range(far)])  8.51 us
    ppermute x1, waiting for transfers between devices, shards(): east = lax.ppermute(east, EVERY, pairs(lambda a, o: (a, o + 1)))  7.75 us
    ppermute x1, starting transfers between devices, shards(): lax.ppermute(quad(other_rows, far_cols), EVERY, pairs(lambda a, o: (a, o...  6.3 us
    ppermute x3, waiting for transfers between devices, shards(): lax.ppermute(piece, FAR, [(i, (i + by) % far) for i in range(far)])  3.82 us
    ppermute x1, waiting for transfers between devices, shards(): lax.ppermute(quad(other_rows, near_cols), EVERY, pairs(lambda a, o: (a -...  2.8 us
  transfers between devices with their start and end apart: 10, of which 6 were waited for; matrix products, arithmetic and copies ran while one was open for 1% of the time, Pallas kernels for 1%

profile of v6, /device:TPU:8, one launch (start us, length us, event | category | flops | bytes accessed | tf_op | source)
XLA Modules:
  0.0 104.2 jit_solution(16384023957184656151)
XLA Ops:
  0.6 1.2 %fusion.2 = (bf16[1,12,6,2,512]{4,3,2,1,0:T(2,128)(2,1)S(1)}, bf16[1,12,6,2,512]{4,3,2,1,0:T(2,128)(2,1)S(1)}) fusion(bf16[1,12,12,2,512]{4,3,2,1,0:T(2,128)(2,1)} %param.7), kind=kLoop, calls=%fused_computation.19 | loop fusion | bytes 589824 | tf_op jit(solution)/shard_map/window_in/slice | solution.py:370
  1.8 0.2 constant_dynamic-slice_fusion
  2.1 0.0 copy-start
  2.1 0.0 copy-start.1
  2.1 1.3 %fusion.1 = (bf16[1,12,6,2,512]{4,3,2,1,0:T(2,128)(2,1)S(1)}, bf16[1,12,6,2,512]{4,3,2,1,0:T(2,128)(2,1)S(1)}) fusion(bf16[1,12,12,2,512]{4,3,2,1,0:T(2,128)(2,1)} %param.5), kind=kLoop, calls=%fused_computation.18 | loop fusion | bytes 589824 | tf_op jit(solution)/shard_map/window_in/slice | solution.py:370
  3.5 0.2 constant_dynamic-slice_fusion.1
  3.8 6.3 %collective-permute-start = (bf16[2,72,512]{2,1,0:T(8,128)(2,1)S(1)}, bf16[2,72,512]{2,1,0:T(8,128)(2,1)S(1)}, u32[]{:S(2)}, u32[]{:S(2)}) collective-permute-start(bf16[2,72,512]{2,1,0:T(8,128)(2,1)S(1)} %pad_maximum_fusion.1), channel_id=1, source_target_pairs={{0,31},{1,0},{2,1},{3,2},{4,3},{5,4},{6,5},{7,6},{8,7},{9,8},{10,9... | collective-permute-start | bytes 442376 | tf_op jit(solution)/shard_map/window_in/ppermute | solution.py:379
  10.2 0.5 collective-permute-start.1
  10.7 0.0 copy-start.2
  10.8 2.5 %collective-permute-start.2 = (bf16[2,72,512]{2,1,0:T(8,128)(2,1)S(1)}, bf16[2,72,512]{2,1,0:T(8,128)(2,1)S(1)}, u32[]{:S(2)}, u32[]{:S(2)}) collective-permute-start(bf16[2,72,512]{2,1,0:T(8,128)(2,1)S(1)} %pad_maximum_fusion.3), channel_id=1, source_target_pairs={{0,63},{1,224},{2,33},{3,226},{4,35},{5,228},{6,37},{7,230},{8,39}... | collective-permute-start | bytes 442376 | tf_op jit(solution)/shard_map/window_in/ppermute | solution.py:383
  13.4 0.0 copy-done
  13.4 0.0 copy-done.1
  13.4 0.5 weights.1
  13.9 0.0 collective-permute-done.q1
  13.9 2.8 %collective-permute-done.1.q2 = bf16[2,72,512]{2,1,0:T(8,128)(2,1)S(1)} collective-permute-done((bf16[2,72,512]{2,1,0:T(8,128)(2,1)S(1)}, bf16[2,72,512]{2,1,0:T(8,128)(2,1)S(1)}, u32[]{:S(2)}, u32[]{:S(2)}) %collective-permute-start.1) | collective-permute-done | bytes 147488 | tf_op jit(solution)/shard_map/window_in/ppermute | solution.py:380
  16.7 0.3 collective-permute-done.2.q3
  17.0 0.0 copy-done.2
  17.0 8.9 %window_grads.1 = (f32[256,2176]{1,0:T(8,128)S(1)}, bf16[256,2176]{1,0:T(8,128)(2,1)S(1)}, bf16[512,384]{1,0:T(8,128)(2,1)S(1)}, bf16[288,512]{1,0:T(8,128)(2,1)S(1)}) custom-call(bf16[2,72,512]{2,1,0:T(8,128)(2,1)S(1)} %constant_dynamic-update-slice_fusion.q0, bf16[2,72,512]{2,1,0:T(8,128)(2,1)S(1)} %collective-permute-done.q1, ...), custom_call_target="tpu_custom_call" | custom-call | tf_op jit(solution)/shard_map/window_grads/pallas_call | solution.py:404
  25.9 1.6 %collective-permute-start.3 = (bf16[256,2176]{1,0:T(8,128)(2,1)S(1)}, bf16[256,2176]{1,0:T(8,128)(2,1)S(1)}, u32[]{:S(2)}, u32[]{:S(2)}) collective-permute-start(bf16[256,2176]{1,0:T(8,128)(2,1)S(1)} %get-tuple-element.28), channel_id=1, source_target_pairs={{0,1},{1,0},{2,3},{3,2},{4,5},{5,4},{6,7},{7,6},{8,9},{9,8},{10,11... | collective-permute-start | bytes 3342344 | tf_op jit(solution)/shard_map/sum_cores/ppermute | solution.py:419
  27.4 0.7 window_tokens.1
  28.1 1.7 %collective-permute-done.3 = bf16[256,2176]{1,0:T(8,128)(2,1)S(1)} collective-permute-done((bf16[256,2176]{1,0:T(8,128)(2,1)S(1)}, bf16[256,2176]{1,0:T(8,128)(2,1)S(1)}, u32[]{:S(2)}, u32[]{:S(2)}) %collective-permute-start.3) | collective-permute-done | bytes 1114144 | tf_op jit(solution)/shard_map/sum_cores/ppermute | solution.py:419
  29.8 0.4 fusion
  30.3 27.0 %all_to_all.10 = bf16[32,8,2176]{2,1,0:T(8,128)(2,1)S(1)} all-to-all(bf16[32,8,2176]{2,1,0:T(8,128)(2,1)S(1)} %bitcast.10), channel_id=1, replica_groups=mesh['xh'=2,'y'=4,'zh'=4,'zl'=2,'xl'=2,'core'=2] {'xh','y','zl','xl'}, dimensions={0} | all-to-all | bytes 2228224 | tf_op jit(solution)/shard_map/sum_near/all_to_all | solution.py:439
  57.2 0.2 convert_reduce_fusion.mine._
  57.4 0.8 collective-permute-start.7
  58.2 0.5 collective-permute-start.4
  58.7 5.4 %collective-permute-start.5 = (f32[8,2176]{1,0:T(8,128)S(1)}, f32[8,2176]{1,0:T(8,128)S(1)}, u32[]{:S(2)}, u32[]{:S(2)}) collective-permute-start(f32[8,2176]{1,0:T(8,128)S(1)} %convert_reduce_fusion.mine._), channel_id=1, source_target_pairs={{0,16},{8,24},{16,0},{24,8},{1,17},{9,25},{17,1},{25,9},{2,18},{10... | collective-permute-start | bytes 208904 | tf_op jit(solution)/shard_map/sum_far/ppermute | solution.py:443
  64.1 2.7 %collective-permute-start.6 = (f32[8,2176]{1,0:T(8,128)S(1)}, f32[8,2176]{1,0:T(8,128)S(1)}, u32[]{:S(2)}, u32[]{:S(2)}) collective-permute-start(f32[8,2176]{1,0:T(8,128)S(1)} %convert_reduce_fusion.mine._), channel_id=1, source_target_pairs={{0,24},{8,0},{16,8},{24,16},{1,25},{9,1},{17,9},{25,17},{2,26},{10... | collective-permute-start | bytes 208904 | tf_op jit(solution)/shard_map/sum_far/ppermute | solution.py:443
  66.7 0.0 collective-permute-done.4.next1
  66.7 1.9 %collective-permute-done.5.next2 = f32[8,2176]{1,0:T(8,128)S(1)} collective-permute-done((f32[8,2176]{1,0:T(8,128)S(1)}, f32[8,2176]{1,0:T(8,128)S(1)}, u32[]{:S(2)}, u32[]{:S(2)}) %collective-permute-start.5) | collective-permute-done | bytes 69664 | tf_op jit(solution)/shard_map/sum_far/ppermute | solution.py:443
  68.6 2.0 %collective-permute-done.6.next3 = f32[8,2176]{1,0:T(8,128)S(1)} collective-permute-done((f32[8,2176]{1,0:T(8,128)S(1)}, f32[8,2176]{1,0:T(8,128)S(1)}, u32[]{:S(2)}, u32[]{:S(2)}) %collective-permute-start.6) | collective-permute-done | bytes 69664 | tf_op jit(solution)/shard_map/sum_far/ppermute | solution.py:443
  70.6 0.1 sum_far.1
  70.7 0.0 collective-permute-done.7.north
  70.7 0.1 broadcast_in_dim.10
  70.7 22.8 %all_to_all.11 = bf16[32,8,2176]{2,1,0:T(8,128)(2,1)S(1)} all-to-all(bf16[32,8,2176]{2,1,0:T(8,128)(2,1)S(1)} %broadcast_in_dim.10), channel_id=1, replica_groups=mesh['xh'=2,'y'=4,'zh'=4,'zl'=2,'xl'=2,'core'=2] {'xh','y','zl','xl'}, dimensions={0} | all-to-all | bytes 2228224 | tf_op jit(solution)/shard_map/share/all_to_all | solution.py:462
  93.5 0.0 collective-permute-start.8
  93.5 0.1 slice.23
  93.6 0.4 pad_maximum_fusion
  94.1 0.6 collective-permute-start.9
  94.6 7.8 %collective-permute-done.9.east = bf16[2,2,6,6,2,512]{5,4,3,2,1,0:T(2,128)(2,1)S(1)} collective-permute-done((bf16[2,2,6,6,2,512]{5,4,3,2,1,0:T(2,128)(2,1)S(1)}, bf16[2,2,6,6,2,512]{5,4,3,2,1,0:T(2,128)(2,1)S(1)}, u32[]{:S(2)}, u32[]{:S(2)}) %collective-permute-start.9) | collective-permute-done | bytes 294944 | tf_op jit(solution)/shard_map/window_out/ppermute | solution.py:460
  102.4 0.0 collective-permute-done.8.theirs
  102.4 1.6 %finish.1 = (bf16[1,12,12,2,512]{4,3,2,1,0:T(2,128)(2,1)}, bf16[1,12,12,2,512]{4,3,2,1,0:T(2,128)(2,1)}, bf16[512,1536]{1,0:T(8,128)(2,1)}, bf16[512,512]{1,0:T(8,128)(2,1)}, f32[1,512]{1,0:T(1,128)}) custom-call(bf16[256,2176]{1,0:T(8,128)(2,1)S(1)} %bitcast.6, bf16[256,2176]{1,0:T(8,128)(2,1)S(1)} %collective-permute-done.8.theirs, ...), custom_call_target="tpu_custom_call" | custom-call | tf_op jit(solution)/shard_map/finish/pallas_call | solution.py:467
  (14 shorter events, 0.4 us)
Async XLA Ops:
  2.1 11.3 %copy-start = (bf16[512,1536]{1,0:T(8,128)(2,1)S(1)}, bf16[512,1536]{1,0:T(8,128)(2,1)}, u32[]{:S(2)}) copy-start(bf16[512,1536]{1,0:T(8,128)(2,1)} %wqkv.3) | copy-start | bytes 4718596
  2.1 11.3 %copy-start.1 = (bf16[512,512]{1,0:T(8,128)(2,1)S(1)}, bf16[512,512]{1,0:T(8,128)(2,1)}, u32[]{:S(2)}) copy-start(bf16[512,512]{1,0:T(8,128)(2,1)} %wout.3) | copy-start | bytes 1572868
  3.8 10.1 %collective-permute-start = (bf16[2,72,512]{2,1,0:T(8,128)(2,1)S(1)}, bf16[2,72,512]{2,1,0:T(8,128)(2,1)S(1)}, u32[]{:S(2)}, u32[]{:S(2)}) collective-permute-start(bf16[2,72,512]{2,1,0:T(8,128)(2,1)S(1)} %pad_maximum_fusion.1), channel_id=1, source_target_pairs={{0,31},{1,0},{2,1},{3,2},{4,3},{5,4},{6,5},{7,6},{8,7},{9,8},{10,9... | collective-permute-start | bytes 442376 | tf_op jit(solution)/shard_map/window_in/ppermute | solution.py:379
  10.2 6.5 %collective-permute-start.1 = (bf16[2,72,512]{2,1,0:T(8,128)(2,1)S(1)}, bf16[2,72,512]{2,1,0:T(8,128)(2,1)S(1)}, u32[]{:S(2)}, u32[]{:S(2)}) collective-permute-start(bf16[2,72,512]{2,1,0:T(8,128)(2,1)S(1)} %pad_maximum_fusion.2), channel_id=1, source_target_pairs={{0,224},{1,33},{2,226},{3,35},{4,228},{5,37},{6,230},{7,39},{8,232... | collective-permute-start | bytes 442376 | tf_op jit(solution)/shard_map/window_in/ppermute | solution.py:380
  10.7 6.2 %copy-start.2 = (f32[512]{0:T(512)S(1)}, f32[512]{0:T(512)}, u32[]{:S(2)}) copy-start(f32[512]{0:T(512)} %param.6) | copy-start | bytes 6148
  10.8 6.2 %collective-permute-start.2 = (bf16[2,72,512]{2,1,0:T(8,128)(2,1)S(1)}, bf16[2,72,512]{2,1,0:T(8,128)(2,1)S(1)}, u32[]{:S(2)}, u32[]{:S(2)}) collective-permute-start(bf16[2,72,512]{2,1,0:T(8,128)(2,1)S(1)} %pad_maximum_fusion.3), channel_id=1, source_target_pairs={{0,63},{1,224},{2,33},{3,226},{4,35},{5,228},{6,37},{7,230},{8,39}... | collective-permute-start | bytes 442376 | tf_op jit(solution)/shard_map/window_in/ppermute | solution.py:383
  25.9 4.0 %collective-permute-start.3 = (bf16[256,2176]{1,0:T(8,128)(2,1)S(1)}, bf16[256,2176]{1,0:T(8,128)(2,1)S(1)}, u32[]{:S(2)}, u32[]{:S(2)}) collective-permute-start(bf16[256,2176]{1,0:T(8,128)(2,1)S(1)} %get-tuple-element.28), channel_id=1, source_target_pairs={{0,1},{1,0},{2,3},{3,2},{4,5},{5,4},{6,7},{7,6},{8,9},{9,8},{10,11... | collective-permute-start | bytes 3342344 | tf_op jit(solution)/shard_map/sum_cores/ppermute | solution.py:419
  57.4 13.3 %collective-permute-start.7 = (bf16[2,2,6,6,2,512]{5,4,3,2,1,0:T(2,128)(2,1)S(1)}, bf16[2,2,6,6,2,512]{5,4,3,2,1,0:T(2,128)(2,1)S(1)}, u32[]{:S(2)}, u32[]{:S(2)}) collective-permute-start(bf16[2,2,6,6,2,512]{5,4,3,2,1,0:T(2,128)(2,1)S(1)} %get-tuple-element.35), channel_id=1, source_target_pairs={{0,32},{1,225},{2,34},{3,227},{4,36},{5,229},{6,38},{7,231},{8,40}... | collective-permute-start | bytes 884744 | tf_op jit(solution)/shard_map/window_out/ppermute | solution.py:448
  58.2 8.5 %collective-permute-start.4 = (f32[8,2176]{1,0:T(8,128)S(1)}, f32[8,2176]{1,0:T(8,128)S(1)}, u32[]{:S(2)}, u32[]{:S(2)}) collective-permute-start(f32[8,2176]{1,0:T(8,128)S(1)} %convert_reduce_fusion.mine._), channel_id=1, source_target_pairs={{0,8},{8,16},{16,24},{24,0},{1,9},{9,17},{17,25},{25,1},{2,10},{10... | collective-permute-start | bytes 208904 | tf_op jit(solution)/shard_map/sum_far/ppermute | solution.py:443
  58.7 9.9 %collective-permute-start.5 = (f32[8,2176]{1,0:T(8,128)S(1)}, f32[8,2176]{1,0:T(8,128)S(1)}, u32[]{:S(2)}, u32[]{:S(2)}) collective-permute-start(f32[8,2176]{1,0:T(8,128)S(1)} %convert_reduce_fusion.mine._), channel_id=1, source_target_pairs={{0,16},{8,24},{16,0},{24,8},{1,17},{9,25},{17,1},{25,9},{2,18},{10... | collective-permute-start | bytes 208904 | tf_op jit(solution)/shard_map/sum_far/ppermute | solution.py:443
  64.1 6.5 %collective-permute-start.6 = (f32[8,2176]{1,0:T(8,128)S(1)}, f32[8,2176]{1,0:T(8,128)S(1)}, u32[]{:S(2)}, u32[]{:S(2)}) collective-permute-start(f32[8,2176]{1,0:T(8,128)S(1)} %convert_reduce_fusion.mine._), channel_id=1, source_target_pairs={{0,24},{8,0},{16,8},{24,16},{1,25},{9,1},{17,9},{25,17},{2,26},{10... | collective-permute-start | bytes 208904 | tf_op jit(solution)/shard_map/sum_far/ppermute | solution.py:443
  93.5 8.9 %collective-permute-start.8 = (bf16[256,2176]{1,0:T(8,128)(2,1)S(1)}, bf16[256,2176]{1,0:T(8,128)(2,1)S(1)}, u32[]{:S(2)}, u32[]{:S(2)}) collective-permute-start(bf16[256,2176]{1,0:T(8,128)(2,1)S(1)} %bitcast.5), channel_id=1, source_target_pairs={{0,1},{1,0},{2,3},{3,2},{4,5},{5,4},{6,7},{7,6},{8,9},{9,8},{10,11... | collective-permute-start | bytes 3342344 | tf_op jit(solution)/shard_map/share/ppermute | solution.py:464
  94.1 8.3 %collective-permute-start.9 = (bf16[2,2,6,6,2,512]{5,4,3,2,1,0:T(2,128)(2,1)S(1)}, bf16[2,2,6,6,2,512]{5,4,3,2,1,0:T(2,128)(2,1)S(1)}, u32[]{:S(2)}, u32[]{:S(2)}) collective-permute-start(bf16[2,2,6,6,2,512]{5,4,3,2,1,0:T(2,128)(2,1)S(1)} %pad_maximum_fusion), channel_id=1, source_target_pairs={{0,1},{1,2},{2,3},{3,4},{4,5},{5,6},{6,7},{7,8},{8,9},{9,10},{10,1... | collective-permute-start | bytes 884744 | tf_op jit(solution)/shard_map/window_out/ppermute | solution.py:460

commit v7 on v6

--- a/solution.py
+++ b/solution.py
@@ -365,25 +365,26 @@
             for o in range(lon_n)
         ]
 
-    def quad(first, cols):
-        both = [
-            lax.dynamic_slice_in_dim(full[0, :, cols], first, SHIFT, 0)
-            for full in (tokens, cotangent)
-        ]
-        return jnp.stack(both).reshape(2, quad_tokens, feat)
+    low_first = own_rows == 0
+
+    def quad(own, cols):
+        low, high = (
+            jnp.stack([full[0, rows, cols] for full in (tokens, cotangent)])
+            for rows in (slice(0, SHIFT), slice(SHIFT, lat_rows))
+        )
+        both = jnp.where(low_first == own, low, high)
+        return both.reshape(2, quad_tokens, feat)
 
     near_cols, far_cols = slice(SHIFT, lon_cols), slice(0, SHIFT)
     with jax.named_scope("window_in"):
-        quads = [
-            quad(own_rows, near_cols),
-            lax.ppermute(quad(other_rows, far_cols), EVERY, pairs(lambda a, o: (a, o - 1))),
-            lax.ppermute(
-                quad(other_rows, near_cols), EVERY, pairs(lambda a, o: (a - towards(o), o))
-            ),
-            lax.ppermute(
-                quad(own_rows, far_cols), EVERY, pairs(lambda a, o: (a - towards(o - 1), o - 1))
-            ),
-        ]
+        north = lax.ppermute(
+            quad(False, near_cols), EVERY, pairs(lambda a, o: (a - towards(o), o))
+        )
+        corner = lax.ppermute(
+            quad(True, far_cols), EVERY, pairs(lambda a, o: (a - towards(o - 1), o - 1))
+        )
+        east = lax.ppermute(quad(False, far_cols), EVERY, pairs(lambda a, o: (a, o - 1)))
+        quads = [quad(True, near_cols), east, north, corner]
     gain_row = layer_norm_gain[None, :]
     vmem = pl.BlockSpec(memory_space=pltpu.VMEM)
     hbm = pl.BlockSpec(memory_space=pl.ANY)
@@ -461,6 +462,7 @@
     with jax.named_scope("share"):
         mine = lax.all_to_all(jnp.broadcast_to(piece[None], (near,) + piece.shape), NEAR, 0, 0)
         mine = mine.reshape(rows, width)
+        mine, east = lax.optimization_barrier((mine, east))
         theirs = lax.ppermute(mine, "core", swap)
     with jax.named_scope("finish"):
         shape = (1, 2 * SHIFT, 2 * SHIFT, levels, feat)

time: 104 us -> 101 us (0.971)
  the two profiles are of different devices: /device:TPU:8 before, /device:TPU:1 now
where the time goes in v7:
time: 101 us; the launch traced here: 100 us
  starting transfers between devices  31 us (31%)
  waiting for transfers between devices  31 us (31%)
  blocking collectives  20.6 us (20%)
  Pallas kernels  11.8 us (12%)
  local copies, waits for them, and re-layouts  3.94 us (4%)
  between operations  1.05 us (1%)
  other arithmetic  1.04 us (1%)
    all_to_all x1, blocking collectives, shards(): pieces = lax.all_to_all(pair_sum.reshape(near, chunk, width), NEAR, 0, 0)  20.6 us
    ppermute x1, waiting for transfers between devices, shards(): east = lax.ppermute(east, EVERY, pairs(lambda a, o: (a, o + 1)))  12.2 us
    ppermute x1, starting transfers between devices, shards(): lax.ppermute(quad(True, far_cols), EVERY, pairs(lambda a, o: (a - towards...  9.27 us
    pallas_call x1, Pallas kernels, shards(): pl.pallas_call(grads_kernel, in_specs=[vmem] * 8, out_specs=[vmem] * 4, o...  8.9 us
    ppermute x3, waiting for transfers between devices, shards(): lax.ppermute(piece, FAR, [(i, (i + by) % far) for i in range(far)])  6.62 us
    ppermute x3, starting transfers between devices, shards(): lax.ppermute(piece, FAR, [(i, (i + by) % far) for i in range(far)])  6.08 us
    ppermute x1, waiting for transfers between devices, shards(): lax.ppermute(quad(False, near_cols), EVERY, pairs(lambda a, o: (a - towar...  5.17 us
    all_to_all x1, starting transfers between devices, shards(): lax.all_to_all(jnp.broadcast_to(piece[None], (near,) + piece.shape), NEAR...  3.94 us
  transfers between devices with their start and end apart: 11, of which 9 were waited for; matrix products, arithmetic and copies ran while one was open for 1% of the time, Pallas kernels for 1%

profile of v7, /device:TPU:1, one launch (start us, length us, event | category | flops | bytes accessed | tf_op | source)
XLA Modules:
  0.0 100.4 jit_solution(13180096619390070474)
XLA Ops:
  0.6 1.2 %fusion.2 = (bf16[1,6,6,2,512]{4,3,2,1,0:T(2,128)(2,1)S(1)}, bf16[1,6,6,2,512]{4,3,2,1,0:T(2,128)(2,1)S(1)}, bf16[1,6,6,2,512]{4,3,2,1,0:T(2,128)(2,1)S(1)}, bf16[1,6,6,2,512]{4,3,2,1,0:T(2,128)(2,1)S(1)}) fusion(bf16[1,12,12,2,512]{4,3,2,1,0:T(2,128)(2,1)} %param.5), kind=kLoop, calls=%fused_computation.18 | loop fusion | bytes 589824 | tf_op jit(solution)/shard_map/window_in/slice | solution.py:372
  2.0 1.2 %fusion.1 = (bf16[1,6,6,2,512]{4,3,2,1,0:T(2,128)(2,1)S(1)}, bf16[1,6,6,2,512]{4,3,2,1,0:T(2,128)(2,1)S(1)}, bf16[1,6,6,2,512]{4,3,2,1,0:T(2,128)(2,1)S(1)}, bf16[1,6,6,2,512]{4,3,2,1,0:T(2,128)(2,1)S(1)}) fusion(bf16[1,12,12,2,512]{4,3,2,1,0:T(2,128)(2,1)} %param.7), kind=kLoop, calls=%fused_computation.17 | loop fusion | bytes 589824 | tf_op jit(solution)/shard_map/window_in/slice | solution.py:372
  3.2 0.0 copy-start
  3.2 0.0 copy-start.1
  3.3 3.3 %collective-permute-start = (bf16[2,72,512]{2,1,0:T(8,128)(2,1)S(1)}, bf16[2,72,512]{2,1,0:T(8,128)(2,1)S(1)}, u32[]{:S(2)}, u32[]{:S(2)}) collective-permute-start(bf16[2,72,512]{2,1,0:T(8,128)(2,1)S(1)} %get-tuple-element.50), channel_id=1, source_target_pairs={{0,31},{1,0},{2,1},{3,2},{4,3},{5,4},{6,5},{7,6},{8,7},{9,8},{10,9... | collective-permute-start | bytes 442376 | tf_op jit(solution)/shard_map/window_in/ppermute | solution.py:386
  6.7 9.3 %collective-permute-start.2 = (bf16[2,72,512]{2,1,0:T(8,128)(2,1)S(1)}, bf16[2,72,512]{2,1,0:T(8,128)(2,1)S(1)}, u32[]{:S(2)}, u32[]{:S(2)}) collective-permute-start(bf16[2,72,512]{2,1,0:T(8,128)(2,1)S(1)} %get-tuple-element.49), channel_id=1, source_target_pairs={{0,63},{1,224},{2,33},{3,226},{4,35},{5,228},{6,37},{7,230},{8,39}... | collective-permute-start | bytes 442376 | tf_op jit(solution)/shard_map/window_in/ppermute | solution.py:383
  16.1 0.0 copy-start.2
  16.2 0.1 collective-permute-start.1
  16.3 0.0 copy-done
  16.3 0.0 copy-done.1
  16.3 0.5 weights.1
  16.8 0.0 collective-permute-done.q1
  16.8 1.9 %collective-permute-done.2.q3 = bf16[2,72,512]{2,1,0:T(8,128)(2,1)S(1)} collective-permute-done((bf16[2,72,512]{2,1,0:T(8,128)(2,1)S(1)}, bf16[2,72,512]{2,1,0:T(8,128)(2,1)S(1)}, u32[]{:S(2)}, u32[]{:S(2)}) %collective-permute-start.2) | collective-permute-done | bytes 147488 | tf_op jit(solution)/shard_map/window_in/ppermute | solution.py:383
  18.7 5.2 %collective-permute-done.1.q2 = bf16[2,72,512]{2,1,0:T(8,128)(2,1)S(1)} collective-permute-done((bf16[2,72,512]{2,1,0:T(8,128)(2,1)S(1)}, bf16[2,72,512]{2,1,0:T(8,128)(2,1)S(1)}, u32[]{:S(2)}, u32[]{:S(2)}) %collective-permute-start.1) | collective-permute-done | bytes 147488 | tf_op jit(solution)/shard_map/window_in/ppermute | solution.py:380
  23.9 0.0 copy-done.2
  23.9 8.9 %window_grads.1 = (f32[256,2176]{1,0:T(8,128)S(1)}, bf16[256,2176]{1,0:T(8,128)(2,1)S(1)}, bf16[512,384]{1,0:T(8,128)(2,1)S(1)}, bf16[288,512]{1,0:T(8,128)(2,1)S(1)}) custom-call(bf16[2,72,512]{2,1,0:T(8,128)(2,1)S(1)} %get-tuple-element.52.q0, bf16[2,72,512]{2,1,0:T(8,128)(2,1)S(1)} %collective-permute-done.q1, ...), custom_call_target="tpu_custom_call" | custom-call | tf_op jit(solution)/shard_map/window_grads/pallas_call | solution.py:405
  32.8 0.3 collective-permute-start.3
  33.1 0.7 window_tokens.1
  33.8 2.0 %collective-permute-done.3 = bf16[256,2176]{1,0:T(8,128)(2,1)S(1)} collective-permute-done((bf16[256,2176]{1,0:T(8,128)(2,1)S(1)}, bf16[256,2176]{1,0:T(8,128)(2,1)S(1)}, u32[]{:S(2)}, u32[]{:S(2)}) %collective-permute-start.3) | collective-permute-done | bytes 1114144 | tf_op jit(solution)/shard_map/sum_cores/ppermute | solution.py:420
  35.8 0.4 fusion
  36.2 20.6 %all_to_all.10 = bf16[32,8,2176]{2,1,0:T(8,128)(2,1)S(1)} all-to-all(bf16[32,8,2176]{2,1,0:T(8,128)(2,1)S(1)} %bitcast.10), channel_id=1, replica_groups=mesh['xh'=2,'y'=4,'zh'=4,'zl'=2,'xl'=2,'core'=2] {'xh','y','zl','xl'}, dimensions={0} | all-to-all | bytes 2228224 | tf_op jit(solution)/shard_map/sum_near/all_to_all | solution.py:440
  56.8 0.2 convert_reduce_fusion.mine._
  57.0 2.0 %collective-permute-start.7 = (bf16[2,2,6,6,2,512]{5,4,3,2,1,0:T(2,128)(2,1)S(1)}, bf16[2,2,6,6,2,512]{5,4,3,2,1,0:T(2,128)(2,1)S(1)}, u32[]{:S(2)}, u32[]{:S(2)}) collective-permute-start(bf16[2,2,6,6,2,512]{5,4,3,2,1,0:T(2,128)(2,1)S(1)} %get-tuple-element.37), channel_id=1, source_target_pairs={{0,32},{1,225},{2,34},{3,227},{4,36},{5,229},{6,38},{7,231},{8,40}... | collective-permute-start | bytes 884744 | tf_op jit(solution)/shard_map/window_out/ppermute | solution.py:449
  59.0 0.0 collective-permute-start.4
  59.0 4.1 %collective-permute-start.5 = (f32[8,2176]{1,0:T(8,128)S(1)}, f32[8,2176]{1,0:T(8,128)S(1)}, u32[]{:S(2)}, u32[]{:S(2)}) collective-permute-start(f32[8,2176]{1,0:T(8,128)S(1)} %convert_reduce_fusion.mine._), channel_id=1, source_target_pairs={{0,16},{8,24},{16,0},{24,8},{1,17},{9,25},{17,1},{25,9},{2,18},{10... | collective-permute-start | bytes 208904 | tf_op jit(solution)/shard_map/sum_far/ppermute | solution.py:444
  63.1 2.0 %collective-permute-start.6 = (f32[8,2176]{1,0:T(8,128)S(1)}, f32[8,2176]{1,0:T(8,128)S(1)}, u32[]{:S(2)}, u32[]{:S(2)}) collective-permute-start(f32[8,2176]{1,0:T(8,128)S(1)} %convert_reduce_fusion.mine._), channel_id=1, source_target_pairs={{0,24},{8,0},{16,8},{24,16},{1,25},{9,1},{17,9},{25,17},{2,26},{10... | collective-permute-start | bytes 208904 | tf_op jit(solution)/shard_map/sum_far/ppermute | solution.py:444
  65.1 1.2 %collective-permute-done.4.next1 = f32[8,2176]{1,0:T(8,128)S(1)} collective-permute-done((f32[8,2176]{1,0:T(8,128)S(1)}, f32[8,2176]{1,0:T(8,128)S(1)}, u32[]{:S(2)}, u32[]{:S(2)}) %collective-permute-start.4) | collective-permute-done | bytes 69664 | tf_op jit(solution)/shard_map/sum_far/ppermute | solution.py:444
  66.3 2.1 %collective-permute-done.5.next2 = f32[8,2176]{1,0:T(8,128)S(1)} collective-permute-done((f32[8,2176]{1,0:T(8,128)S(1)}, f32[8,2176]{1,0:T(8,128)S(1)}, u32[]{:S(2)}, u32[]{:S(2)}) %collective-permute-start.5) | collective-permute-done | bytes 69664 | tf_op jit(solution)/shard_map/sum_far/ppermute | solution.py:444
  68.5 3.3 %collective-permute-done.6.next3 = f32[8,2176]{1,0:T(8,128)S(1)} collective-permute-done((f32[8,2176]{1,0:T(8,128)S(1)}, f32[8,2176]{1,0:T(8,128)S(1)}, u32[]{:S(2)}, u32[]{:S(2)}) %collective-permute-start.6) | collective-permute-done | bytes 69664 | tf_op jit(solution)/shard_map/sum_far/ppermute | solution.py:444
  71.7 0.1 sum_far.1
  71.8 0.0 collective-permute-done.7.north
  71.8 1.1 %broadcast_in_dim.10 = bf16[32,8,2176]{2,1,0:T(8,128)(2,1)} broadcast(bf16[8,2176]{1,0:T(8,128)(2,1)S(1)} %sum_far.1), dimensions={1,2} | broadcast | bytes 1148928 | tf_op jit(solution)/shard_map/share/broadcast_in_dim | solution.py:463
  72.9 3.9 %all-to-all-start.1 = ((bf16[32,8,2176]{2,1,0:T(8,128)(2,1)}), bf16[32,8,2176]{2,1,0:T(8,128)(2,1)S(1)}, u32[]{:S(2)}, u32[]{:S(2)}) async-start(bf16[32,8,2176]{2,1,0:T(8,128)(2,1)} %broadcast_in_dim.10), calls=%async_computation.1 | async-start | bytes 2228224 | tf_op jit(solution)/shard_map/share/all_to_all | solution.py:463
  76.8 0.1 slice.43
  77.0 0.4 pad_maximum_fusion
  77.4 2.9 %collective-permute-start.8 = (bf16[2,2,6,6,2,512]{5,4,3,2,1,0:T(2,128)(2,1)S(1)}, bf16[2,2,6,6,2,512]{5,4,3,2,1,0:T(2,128)(2,1)S(1)}, u32[]{:S(2)}, u32[]{:S(2)}) collective-permute-start(bf16[2,2,6,6,2,512]{5,4,3,2,1,0:T(2,128)(2,1)S(1)} %pad_maximum_fusion), channel_id=1, source_target_pairs={{0,1},{1,2},{2,3},{3,4},{4,5},{5,6},{6,7},{7,8},{8,9},{9,10},{10,1... | collective-permute-start | bytes 884744 | tf_op jit(solution)/shard_map/window_out/ppermute | solution.py:461
  80.2 12.2 %collective-permute-done.8.east = bf16[2,2,6,6,2,512]{5,4,3,2,1,0:T(2,128)(2,1)S(1)} collective-permute-done((bf16[2,2,6,6,2,512]{5,4,3,2,1,0:T(2,128)(2,1)S(1)}, bf16[2,2,6,6,2,512]{5,4,3,2,1,0:T(2,128)(2,1)S(1)}, u32[]{:S(2)}, u32[]{:S(2)}) %collective-permute-start.8) | collective-permute-done | bytes 294944 | tf_op jit(solution)/shard_map/window_out/ppermute | solution.py:461
  92.5 0.6 all-to-all-done.1
  93.1 3.1 %collective-permute-start.9 = (bf16[256,2176]{1,0:T(8,128)(2,1)S(1)}, bf16[256,2176]{1,0:T(8,128)(2,1)S(1)}, u32[]{:S(2)}, u32[]{:S(2)}) collective-permute-start(bf16[256,2176]{1,0:T(8,128)(2,1)S(1)} %bitcast.5), channel_id=1, source_target_pairs={{0,1},{1,0},{2,3},{3,2},{4,5},{5,4},{6,7},{7,6},{8,9},{9,8},{10,11... | collective-permute-start | bytes 3342344 | tf_op jit(solution)/shard_map/share/ppermute | solution.py:466
  96.2 2.4 %collective-permute-done.9.theirs = bf16[256,2176]{1,0:T(8,128)(2,1)S(1)} collective-permute-done((bf16[256,2176]{1,0:T(8,128)(2,1)S(1)}, bf16[256,2176]{1,0:T(8,128)(2,1)S(1)}, u32[]{:S(2)}, u32[]{:S(2)}) %collective-permute-start.9) | collective-permute-done | bytes 1114144 | tf_op jit(solution)/shard_map/share/ppermute | solution.py:466
  98.6 1.6 %finish.1 = (bf16[1,12,12,2,512]{4,3,2,1,0:T(2,128)(2,1)}, bf16[1,12,12,2,512]{4,3,2,1,0:T(2,128)(2,1)}, bf16[512,1536]{1,0:T(8,128)(2,1)}, bf16[512,512]{1,0:T(8,128)(2,1)}, f32[1,512]{1,0:T(1,128)}) custom-call(bf16[256,2176]{1,0:T(8,128)(2,1)S(1)} %bitcast.6, bf16[256,2176]{1,0:T(8,128)(2,1)S(1)} %collective-permute-done.9.theirs, ...), custom_call_target="tpu_custom_call" | custom-call | tf_op jit(solution)/shard_map/finish/pallas_call | solution.py:469
  (17 shorter events, 0.4 us)
Async XLA Ops:
  3.2 13.1 %copy-start = (bf16[512,1536]{1,0:T(8,128)(2,1)S(1)}, bf16[512,1536]{1,0:T(8,128)(2,1)}, u32[]{:S(2)}) copy-start(bf16[512,1536]{1,0:T(8,128)(2,1)} %wqkv.3) | copy-start | bytes 4718596
  3.2 13.1 %copy-start.1 = (bf16[512,512]{1,0:T(8,128)(2,1)S(1)}, bf16[512,512]{1,0:T(8,128)(2,1)}, u32[]{:S(2)}) copy-start(bf16[512,512]{1,0:T(8,128)(2,1)} %wout.3) | copy-start | bytes 1572868
  3.3 13.4 %collective-permute-start = (bf16[2,72,512]{2,1,0:T(8,128)(2,1)S(1)}, bf16[2,72,512]{2,1,0:T(8,128)(2,1)S(1)}, u32[]{:S(2)}, u32[]{:S(2)}) collective-permute-start(bf16[2,72,512]{2,1,0:T(8,128)(2,1)S(1)} %get-tuple-element.50), channel_id=1, source_target_pairs={{0,31},{1,0},{2,1},{3,2},{4,3},{5,4},{6,5},{7,6},{8,7},{9,8},{10,9... | collective-permute-start | bytes 442376 | tf_op jit(solution)/shard_map/window_in/ppermute | solution.py:386
  6.7 12.0 %collective-permute-start.2 = (bf16[2,72,512]{2,1,0:T(8,128)(2,1)S(1)}, bf16[2,72,512]{2,1,0:T(8,128)(2,1)S(1)}, u32[]{:S(2)}, u32[]{:S(2)}) collective-permute-start(bf16[2,72,512]{2,1,0:T(8,128)(2,1)S(1)} %get-tuple-element.49), channel_id=1, source_target_pairs={{0,63},{1,224},{2,33},{3,226},{4,35},{5,228},{6,37},{7,230},{8,39}... | collective-permute-start | bytes 442376 | tf_op jit(solution)/shard_map/window_in/ppermute | solution.py:383
  16.1 7.8 %copy-start.2 = (f32[512]{0:T(512)S(1)}, f32[512]{0:T(512)}, u32[]{:S(2)}) copy-start(f32[512]{0:T(512)} %param.6) | copy-start | bytes 6148
  16.2 7.7 %collective-permute-start.1 = (bf16[2,72,512]{2,1,0:T(8,128)(2,1)S(1)}, bf16[2,72,512]{2,1,0:T(8,128)(2,1)S(1)}, u32[]{:S(2)}, u32[]{:S(2)}) collective-permute-start(bf16[2,72,512]{2,1,0:T(8,128)(2,1)S(1)} %get-tuple-element.51), channel_id=1, source_target_pairs={{0,224},{1,33},{2,226},{3,35},{4,228},{5,37},{6,230},{7,39},{8,232... | collective-permute-start | bytes 442376 | tf_op jit(solution)/shard_map/window_in/ppermute | solution.py:380
  32.8 3.0 %collective-permute-start.3 = (bf16[256,2176]{1,0:T(8,128)(2,1)S(1)}, bf16[256,2176]{1,0:T(8,128)(2,1)S(1)}, u32[]{:S(2)}, u32[]{:S(2)}) collective-permute-start(bf16[256,2176]{1,0:T(8,128)(2,1)S(1)} %get-tuple-element.30), channel_id=1, source_target_pairs={{0,1},{1,0},{2,3},{3,2},{4,5},{5,4},{6,7},{7,6},{8,9},{9,8},{10,11... | collective-permute-start | bytes 3342344 | tf_op jit(solution)/shard_map/sum_cores/ppermute | solution.py:420
  57.0 14.8 %collective-permute-start.7 = (bf16[2,2,6,6,2,512]{5,4,3,2,1,0:T(2,128)(2,1)S(1)}, bf16[2,2,6,6,2,512]{5,4,3,2,1,0:T(2,128)(2,1)S(1)}, u32[]{:S(2)}, u32[]{:S(2)}) collective-permute-start(bf16[2,2,6,6,2,512]{5,4,3,2,1,0:T(2,128)(2,1)S(1)} %get-tuple-element.37), channel_id=1, source_target_pairs={{0,32},{1,225},{2,34},{3,227},{4,36},{5,229},{6,38},{7,231},{8,40}... | collective-permute-start | bytes 884744 | tf_op jit(solution)/shard_map/window_out/ppermute | solution.py:449
  59.0 7.3 %collective-permute-start.4 = (f32[8,2176]{1,0:T(8,128)S(1)}, f32[8,2176]{1,0:T(8,128)S(1)}, u32[]{:S(2)}, u32[]{:S(2)}) collective-permute-start(f32[8,2176]{1,0:T(8,128)S(1)} %convert_reduce_fusion.mine._), channel_id=1, source_target_pairs={{0,8},{8,16},{16,24},{24,0},{1,9},{9,17},{17,25},{25,1},{2,10},{10... | collective-permute-start | bytes 208904 | tf_op jit(solution)/shard_map/sum_far/ppermute | solution.py:444
  59.0 9.4 %collective-permute-start.5 = (f32[8,2176]{1,0:T(8,128)S(1)}, f32[8,2176]{1,0:T(8,128)S(1)}, u32[]{:S(2)}, u32[]{:S(2)}) collective-permute-start(f32[8,2176]{1,0:T(8,128)S(1)} %convert_reduce_fusion.mine._), channel_id=1, source_target_pairs={{0,16},{8,24},{16,0},{24,8},{1,17},{9,25},{17,1},{25,9},{2,18},{10... | collective-permute-start | bytes 208904 | tf_op jit(solution)/shard_map/sum_far/ppermute | solution.py:444
  63.1 8.6 %collective-permute-start.6 = (f32[8,2176]{1,0:T(8,128)S(1)}, f32[8,2176]{1,0:T(8,128)S(1)}, u32[]{:S(2)}, u32[]{:S(2)}) collective-permute-start(f32[8,2176]{1,0:T(8,128)S(1)} %convert_reduce_fusion.mine._), channel_id=1, source_target_pairs={{0,24},{8,0},{16,8},{24,16},{1,25},{9,1},{17,9},{25,17},{2,26},{10... | collective-permute-start | bytes 208904 | tf_op jit(solution)/shard_map/sum_far/ppermute | solution.py:444
  72.9 20.2 %all-to-all-start.1 = ((bf16[32,8,2176]{2,1,0:T(8,128)(2,1)}), bf16[32,8,2176]{2,1,0:T(8,128)(2,1)S(1)}, u32[]{:S(2)}, u32[]{:S(2)}) async-start(bf16[32,8,2176]{2,1,0:T(8,128)(2,1)} %broadcast_in_dim.10), calls=%async_computation.1 | async-start | bytes 2228224 | tf_op jit(solution)/shard_map/share/all_to_all | solution.py:463
  77.4 15.1 %collective-permute-start.8 = (bf16[2,2,6,6,2,512]{5,4,3,2,1,0:T(2,128)(2,1)S(1)}, bf16[2,2,6,6,2,512]{5,4,3,2,1,0:T(2,128)(2,1)S(1)}, u32[]{:S(2)}, u32[]{:S(2)}) collective-permute-start(bf16[2,2,6,6,2,512]{5,4,3,2,1,0:T(2,128)(2,1)S(1)} %pad_maximum_fusion), channel_id=1, source_target_pairs={{0,1},{1,2},{2,3},{3,4},{4,5},{5,6},{6,7},{7,8},{8,9},{9,10},{10,1... | collective-permute-start | bytes 884744 | tf_op jit(solution)/shard_map/window_out/ppermute | solution.py:461
  93.1 5.5 %collective-permute-start.9 = (bf16[256,2176]{1,0:T(8,128)(2,1)S(1)}, bf16[256,2176]{1,0:T(8,128)(2,1)S(1)}, u32[]{:S(2)}, u32[]{:S(2)}) collective-permute-start(bf16[256,2176]{1,0:T(8,128)(2,1)S(1)} %bitcast.5), channel_id=1, source_target_pairs={{0,1},{1,0},{2,3},{3,2},{4,5},{5,4},{6,7},{7,6},{8,9},{9,8},{10,11... | collective-permute-start | bytes 3342344 | tf_op jit(solution)/shard_map/share/ppermute | solution.py:466

commit v8 on v7

--- a/solution.py
+++ b/solution.py
@@ -61,10 +61,22 @@
     wout_near[...] = wout[...]
 
 
+def partial_sums(start, normed_t, g_low, dq_t, dkv_t, attn_t):
+    feat = attn_t.shape[0]
+    tokens = dkv_t.shape[1]
+    pick = pl.ds(start, feat // 2)
+    return (
+        dot(normed_t[pick, :], dq_t[...], ((1,), (1,))),
+        dot(normed_t[pick, :tokens], dkv_t[:feat, :], ((1,), (1,))),
+        dot(normed_t[pick, :tokens], dkv_t[feat:, :], ((1,), (1,))),
+        dot(attn_t[pick, :], g_low[...]),
+    )
+
+
 def grads_kernel(
     q0, q1, q2, q3, gain, wqkv, wqkv_t, wout,
-    keep, send, attn_t, back,
-    wide, normed, normed_t, g_low, q_t, kv_t, kv, do_t, dq_t, dkv_t, gain_col,
+    send, attn_t, back, normed_t, g_low, dq_t, dkv_t, gain_col,
+    wide, normed, q_t, kv_t, kv, do_t,
     diag, side, bias, scores, d_probs, p_low, d_low, acc,
 ):
     quads = (q0, q1, q2, q3)
@@ -76,7 +88,7 @@
     per = 128 // size
     half = tokens // 2
     core = lax.axis_index("core")
-    edge = lax.axis_index(LAT) == jnp.where(core == 0, lax.axis_size(LAT) - 1, 0)
+    edge = lax.axis_index(LAT) == lax.axis_size(LAT) - 1
     inv_root = 1.0 / math.sqrt(size)
     to_exp2 = inv_root * math.log2(math.e)
 
@@ -218,24 +230,10 @@
     gain_col[...] = jnp.where(lanes(column.shape) < 2, column, 0.0)
 
     rows = feat // 2
-    mine = pl.multiple_of(core * rows, rows)
     theirs = pl.multiple_of((1 - core) * rows, rows)
-
-    def partial_sums(start):
-        pick = pl.ds(start, rows)
-        return (
-            dot(normed_t[pick, :], dq_t[...], ((1,), (1,))),
-            dot(normed_t[pick, :tokens], dkv_t[:feat, :], ((1,), (1,))),
-            dot(normed_t[pick, :tokens], dkv_t[feat:, :], ((1,), (1,))),
-            dot(attn_t[pick, :], g_low[...]),
-        )
-
-    for block, value in enumerate(partial_sums(theirs)):
+    for block, value in enumerate(partial_sums(theirs, normed_t, g_low, dq_t, dkv_t, attn_t)):
         send[:, block * feat : (block + 1) * feat] = value.astype(BF16)
-    for block, value in enumerate(partial_sums(mine)):
-        keep[:, block * feat : (block + 1) * feat] = value
     send[:, 4 * feat :] = gain_col[pl.ds(theirs, rows), :].astype(BF16)
-    keep[:, 4 * feat :] = gain_col[pl.ds(mine, rows), :]
 
 
 def grads_scratch(tokens, feat):
@@ -244,14 +242,9 @@
         pltpu.VMEM((tokens, feat), F32),
         pltpu.VMEM((ext, feat), BF16),
         pltpu.VMEM((feat, ext), BF16),
-        pltpu.VMEM((ext, feat), BF16),
-        pltpu.VMEM((feat, ext), BF16),
         pltpu.VMEM((2 * feat, tokens), BF16),
         pltpu.VMEM((tokens, 2 * feat), BF16),
         pltpu.VMEM((feat, ext), BF16),
-        pltpu.VMEM((feat, ext), BF16),
-        pltpu.VMEM((2 * feat, tokens), BF16),
-        pltpu.VMEM((feat, 128), F32),
         pltpu.VMEM((128, 128), BF16),
         pltpu.VMEM((tokens, 128), BF16),
         pltpu.VMEM((128, ext), BF16),
@@ -263,7 +256,16 @@
     ]
 
 
-def tokens_kernel(q0, q1, q2, q3, gain, wout, attn_t, back, own, east, north, wide):
+def tokens_kernel(
+    q0, q1, q2, q3, gain, wout, attn_t, back, normed_t, g_low, dq_t, dkv_t, gain_col,
+    keep, own, east, north, wide,
+):
+    feat = attn_t.shape[0]
+    half = feat // 2
+    mine = pl.multiple_of(lax.axis_index("core") * half, half)
+    for block, value in enumerate(partial_sums(mine, normed_t, g_low, dq_t, dkv_t, attn_t)):
+        keep[:, block * feat : (block + 1) * feat] = value
+    keep[:, 4 * feat :] = gain_col[pl.ds(mine, half), :]
     quads, outs = (q0, q1, q2, q3), (own, east, north.at[0], north.at[1])
     rows = q0.shape[1]
     gather_quads(quads, 0, wide)
@@ -307,11 +309,6 @@
     out[:, main:] = split_low(gain_total(total[:, main:]), 3)
 
 
-def half_rows(core):
-    first = jnp.where(core == 0, SHIFT, 0)
-    return first, SHIFT - first
-
-
 def finish_kernel(
     mine, theirs, own, north, east,
     mixed, grad_tokens, grad_qkv, grad_out, gain_grad, gains, sems,
@@ -334,12 +331,11 @@
         column = half[:, main:].astype(F32).T
         gains[:, pl.ds(at, rows)] = column[0:1] + column[1:2] + column[2:3]
     copy(gains, gain_grad)
-    own_rows, other_rows = half_rows(core)
     for quad, at, lon in (
-        (own, own_rows, SHIFT),
-        (north.at[0], other_rows, SHIFT),
-        (east.at[0], other_rows, 0),
-        (east.at[1], own_rows, 0),
+        (own, SHIFT, SHIFT),
+        (north.at[0], 0, SHIFT),
+        (east.at[0], SHIFT, 0),
+        (east.at[1], 0, 0),
     ):
         block = (0, pl.ds(at, SHIFT), pl.ds(lon, SHIFT))
         copy(quad.at[0], mixed.at[block])
@@ -353,10 +349,6 @@
     lat_n, lon_n = lax.axis_size(LAT), lax.axis_size(LON)
     quad_tokens = SHIFT * SHIFT * levels
     n_tokens = 4 * quad_tokens
-    own_rows, other_rows = half_rows(lax.axis_index("core"))
-
-    def towards(lon):
-        return 1 if lon % 2 == 0 else -1
 
     def pairs(target):
         return [
@@ -365,31 +357,25 @@
             for o in range(lon_n)
         ]
 
-    low_first = own_rows == 0
-
-    def quad(own, cols):
-        low, high = (
-            jnp.stack([full[0, rows, cols] for full in (tokens, cotangent)])
-            for rows in (slice(0, SHIFT), slice(SHIFT, lat_rows))
-        )
-        both = jnp.where(low_first == own, low, high)
-        return both.reshape(2, quad_tokens, feat)
-
-    near_cols, far_cols = slice(SHIFT, lon_cols), slice(0, SHIFT)
-    with jax.named_scope("window_in"):
-        north = lax.ppermute(
-            quad(False, near_cols), EVERY, pairs(lambda a, o: (a - towards(o), o))
-        )
-        corner = lax.ppermute(
-            quad(True, far_cols), EVERY, pairs(lambda a, o: (a - towards(o - 1), o - 1))
-        )
-        east = lax.ppermute(quad(False, far_cols), EVERY, pairs(lambda a, o: (a, o - 1)))
-        quads = [quad(True, near_cols), east, north, corner]
-    gain_row = layer_norm_gain[None, :]
     vmem = pl.BlockSpec(memory_space=pltpu.VMEM)
     hbm = pl.BlockSpec(memory_space=pl.ANY)
     params = pltpu.CompilerParams(vmem_limit_bytes=40 * 1024 * 1024)
+    with jax.named_scope("window_in"):
+
+        def quad(rows, cols):
+            both = jnp.stack([tokens[0, rows, cols], cotangent[0, rows, cols]])
+            return both.reshape(2, quad_tokens, feat)
+
+        low, high = slice(0, SHIFT), slice(SHIFT, 2 * SHIFT)
+        own, east = quad(high, high), quad(high, low)
+        north, corner = quad(low, high), quad(low, low)
+        east = lax.ppermute(east, EVERY, pairs(lambda a, o: (a, o - 1)))
+        north = lax.ppermute(north, EVERY, pairs(lambda a, o: (a - 1, o)))
+        corner = lax.ppermute(corner, EVERY, pairs(lambda a, o: (a - 1, o - 1)))
+        quads = [own, east, north, corner]
+    gain_row = layer_norm_gain[None, :]
     rows, width = feat // 2, 4 * feat + 128
+    ext = n_tokens // 128 * 128 + 128
     with jax.named_scope("weights"):
         w_qkv_t, w_out_near = pl.pallas_call(
             weights_kernel,
@@ -402,15 +388,19 @@
             compiler_params=params,
         )(w_qkv, w_out)
     with jax.named_scope("window_grads"):
-        keep, send, attn_t, back = pl.pallas_call(
+        send, *shared = pl.pallas_call(
             grads_kernel,
             in_specs=[vmem] * 8,
-            out_specs=[vmem] * 4,
+            out_specs=[vmem] * 8,
             out_shape=[
-                jax.ShapeDtypeStruct((rows, width), F32),
                 jax.ShapeDtypeStruct((rows, width), BF16),
-                jax.ShapeDtypeStruct((feat, n_tokens // 128 * 128 + 128), BF16),
+                jax.ShapeDtypeStruct((feat, ext), BF16),
                 jax.ShapeDtypeStruct((n_tokens, feat), BF16),
+                jax.ShapeDtypeStruct((feat, ext), BF16),
+                jax.ShapeDtypeStruct((ext, feat), BF16),
+                jax.ShapeDtypeStruct((feat, ext), BF16),
+                jax.ShapeDtypeStruct((2 * feat, n_tokens), BF16),
+                jax.ShapeDtypeStruct((feat, 128), F32),
             ],
             scratch_shapes=grads_scratch(n_tokens, feat),
             compiler_params=params,
@@ -419,17 +409,20 @@
     with jax.named_scope("sum_cores"):
         other = lax.ppermute(send, "core", swap)
     with jax.named_scope("window_tokens"):
-        own, east, north = pl.pallas_call(
+        keep, own, east, north = pl.pallas_call(
             tokens_kernel,
-            in_specs=[vmem] * 8,
-            out_specs=[vmem] * 3,
+            in_specs=[vmem] * 13,
+            out_specs=[vmem] * 4,
             out_shape=[
-                jax.ShapeDtypeStruct(lead + (2, SHIFT, SHIFT, levels, feat), BF16)
-                for lead in ((), (), (2,))
+                jax.ShapeDtypeStruct((rows, width), F32),
+                *(
+                    jax.ShapeDtypeStruct(lead + (2, SHIFT, SHIFT, levels, feat), BF16)
+                    for lead in ((), (), (2,))
+                ),
             ],
             scratch_shapes=[pltpu.VMEM((n_tokens, feat), F32)],
             compiler_params=params,
-        )(*quads, gain_row, w_out, attn_t, back)
+        )(*quads, gain_row, w_out, *shared)
     with jax.named_scope("sum_cores"):
         pair_sum = add_pair(keep, other)
     pair_sum, north = lax.optimization_barrier((pair_sum, north))
@@ -446,7 +439,7 @@
         ]
     after, north = lax.optimization_barrier((piece, north))
     with jax.named_scope("window_out"):
-        north = lax.ppermute(north, EVERY, pairs(lambda a, o: (a + towards(o), o)))
+        north = lax.ppermute(north, EVERY, pairs(lambda a, o: (a + 1, o)))
     with jax.named_scope("sum_far"):
         piece = pl.pallas_call(
             functools.partial(final_piece_kernel, factor),

time: 101 us -> 99.7 us (0.987)
  waiting for transfers between devices: 31 us -> 18.1 us
  starting transfers between devices: 31 us -> 41.6 us
  blocking collectives: 20.6 us -> 22.3 us
    ppermute x4, waiting for transfers between devices: 7.1 us -> 0.5 us  [the longest x1 0.49 us: shards(): east = lax.ppermute(east, EVERY, pairs(lambda a, o: (a, o - 1)))]
    ppermute x3, starting transfers between devices: 6.08 us -> 9.89 us  [shards(): lax.ppermute(piece, FAR, [(i, (i + by) % far) for i in range(far)])]
    ppermute x3, waiting for transfers between devices: 6.62 us -> 3.47 us  [shards(): lax.ppermute(piece, FAR, [(i, (i + by) % far) for i in range(far)])]
    ppermute x1, starting transfers between devices: 0.27 us -> 2.9 us  [shards(): other = lax.ppermute(send, 'core', swap)]
    all_to_all x1, starting transfers between devices: 3.94 us -> 6.38 us  [shards(): lax.all_to_all(jnp.broadcast_to(piece[None], (near,) + piece.shape), NEAR...]
    ppermute x1, waiting for transfers between devices: 12.2 us -> 10.4 us  [shards(): east = lax.ppermute(east, EVERY, pairs(lambda a, o: (a, o + 1)))]
    ppermute x4, starting transfers between devices: 14.7 us -> 12.9 us  [the longest x1 6.1 us: shards(): north = lax.ppermute(north, EVERY, pairs(lambda a, o: (a - 1, o)))]
    ppermute x1, starting transfers between devices: 2.86 us -> 4.65 us  [shards(): east = lax.ppermute(east, EVERY, pairs(lambda a, o: (a, o + 1)))]
  transfers between devices with their start and end apart: 11 -> 11, of which waited for: 9 -> 6; matrix products, arithmetic and copies ran while one was open for 1% -> 1% of each run, Pallas kernels for 1% -> 2%
where the time goes in v8:
time: 99.7 us; the launch traced here: 99.5 us
  starting transfers between devices  41.6 us (42%)
  blocking collectives  22.3 us (22%)
  waiting for transfers between devices  18.1 us (18%)
  Pallas kernels  11.6 us (12%)
  local copies, waits for them, and re-layouts  3.13 us (3%)
  other arithmetic  1.85 us (2%)
    all_to_all x1, blocking collectives, shards(): pieces = lax.all_to_all(pair_sum.reshape(near, chunk, width), NEAR, 0, 0)  22.3 us
    ppermute x1, waiting for transfers between devices, shards(): east = lax.ppermute(east, EVERY, pairs(lambda a, o: (a, o + 1)))  10.4 us
    ppermute x3, starting transfers between devices, shards(): lax.ppermute(piece, FAR, [(i, (i + by) % far) for i in range(far)])  9.89 us
    pallas_call x1, Pallas kernels, shards(): pl.pallas_call(grads_kernel, in_specs=[vmem] * 8, out_specs=[vmem] * 8, o...  8.36 us
    all_to_all x1, starting transfers between devices, shards(): lax.all_to_all(jnp.broadcast_to(piece[None], (near,) + piece.shape), NEAR...  6.38 us
    ppermute x1, starting transfers between devices, shards(): north = lax.ppermute(north, EVERY, pairs(lambda a, o: (a - 1, o)))  6.1 us
    ppermute x1, starting transfers between devices, shards(): theirs = lax.ppermute(mine, 'core', swap)  4.87 us
    ppermute x1, starting transfers between devices, shards(): east = lax.ppermute(east, EVERY, pairs(lambda a, o: (a, o - 1)))  4.84 us
  transfers between devices with their start and end apart: 11, of which 6 were waited for; matrix products, arithmetic and copies ran while one was open for 1% of the time, Pallas kernels for 2%

profile of v8, /device:TPU:1, one launch (start us, length us, event | category | flops | bytes accessed | tf_op | source)
XLA Modules:
  0.0 99.5 jit_solution(2951570352320632790)
XLA Ops:
  0.6 0.0 copy-start
  0.6 0.0 copy-start.1
  0.7 1.7 %fusion.1 = (bf16[1,6,6,2,512]{4,3,2,1,0:T(2,128)(2,1)S(1)}, bf16[1,6,6,2,512]{4,3,2,1,0:T(2,128)(2,1)S(1)}, bf16[1,6,6,2,512]{4,3,2,1,0:T(2,128)(2,1)S(1)}, bf1...) fusion(bf16[1,12,12,2,512]{4,3,2,1,0:T(2,128)(2,1)} %param.5, ...), kind=kLoop, calls=%fused_computation.9 | loop fusion | bytes 1179648 | tf_op jit(solution)/shard_map/window_in/slice | solution.py:366
  2.4 0.2 pad_maximum_fusion.3
  2.6 0.1 reshape.31
  2.6 6.1 %collective-permute-start.1 = (bf16[2,72,512]{2,1,0:T(8,128)(2,1)S(1)}, bf16[2,72,512]{2,1,0:T(8,128)(2,1)S(1)}, u32[]{:S(2)}, u32[]{:S(2)}) collective-permute-start(bf16[2,72,512]{2,1,0:T(8,128)(2,1)S(1)} %reshape.31), channel_id=1, source_target_pairs={{0,224},{1,225},{2,226},{3,227},{4,228},{5,229},{6,230},{7,231},{8... | collective-permute-start | bytes 442376 | tf_op jit(solution)/shard_map/window_in/ppermute | solution.py:373
  8.7 0.2 pad_maximum_fusion.4
  8.9 0.1 reshape.32
  9.0 1.4 %collective-permute-start.2 = (bf16[2,72,512]{2,1,0:T(8,128)(2,1)S(1)}, bf16[2,72,512]{2,1,0:T(8,128)(2,1)S(1)}, u32[]{:S(2)}, u32[]{:S(2)}) collective-permute-start(bf16[2,72,512]{2,1,0:T(8,128)(2,1)S(1)} %reshape.32), channel_id=1, source_target_pairs={{0,255},{1,224},{2,225},{3,226},{4,227},{5,228},{6,229},{7,230},{8... | collective-permute-start | bytes 442376 | tf_op jit(solution)/shard_map/window_in/ppermute | solution.py:374
  10.4 0.0 copy-start.2
  10.4 0.2 pad_maximum_fusion.2
  10.6 0.1 reshape.30
  10.7 4.8 %collective-permute-start = (bf16[2,72,512]{2,1,0:T(8,128)(2,1)S(1)}, bf16[2,72,512]{2,1,0:T(8,128)(2,1)S(1)}, u32[]{:S(2)}, u32[]{:S(2)}) collective-permute-start(bf16[2,72,512]{2,1,0:T(8,128)(2,1)S(1)} %reshape.30), channel_id=1, source_target_pairs={{0,31},{1,0},{2,1},{3,2},{4,3},{5,4},{6,5},{7,6},{8,7},{9,8},{10,9... | collective-permute-start | bytes 442376 | tf_op jit(solution)/shard_map/window_in/ppermute | solution.py:372
  15.5 0.2 pad_maximum_fusion.1
  15.7 0.1 reshape.29.q0
  15.8 0.0 copy-done
  15.8 0.0 copy-done.1
  15.8 0.5 weights.1
  16.3 0.0 collective-permute-done.1.q2
  16.3 0.0 collective-permute-done.2.q3
  16.3 0.5 collective-permute-done.q1
  16.8 0.0 copy-done.2
  16.8 8.4 %window_grads.1 = (bf16[256,2176]{1,0:T(8,128)(2,1)S(1)}, bf16[512,384]{1,0:T(8,128)(2,1)S(1)}, bf16[288,512]{1,0:T(8,128)(2,1)S(1)}, bf16[512,384]{1,0:T(8,128)...) custom-call(bf16[2,72,512]{2,1,0:T(8,128)(2,1)S(1)} %reshape.29.q0, ...), custom_call_target="tpu_custom_call" | custom-call | tf_op jit(solution)/shard_map/window_grads/pallas_call | solution.py:391
  25.2 2.9 %collective-permute-start.3 = (bf16[256,2176]{1,0:T(8,128)(2,1)S(1)}, bf16[256,2176]{1,0:T(8,128)(2,1)S(1)}, u32[]{:S(2)}, u32[]{:S(2)}) collective-permute-start(bf16[256,2176]{1,0:T(8,128)(2,1)S(1)} %get-tuple-element.42), channel_id=1, source_target_pairs={{0,1},{1,0},{2,3},{3,2},{4,5},{5,4},{6,7},{7,6},{8,9},{9,8},{10,11... | collective-permute-start | bytes 3342344 | tf_op jit(solution)/shard_map/sum_cores/ppermute | solution.py:410
  28.1 1.0 %window_tokens.1 = (f32[256,2176]{1,0:T(8,128)S(1)}, bf16[2,6,6,2,512]{4,3,2,1,0:T(2,128)(2,1)S(1)}, bf16[2,6,6,2,512]{4,3,2,1,0:T(2,128)(2,1)S(1)}, bf16[2,2,6,6,2,512]{5,4,3,2,1,0:T(2,128)(2,1)S(1)}) custom-call(bf16[2,72,512]{2,1,0:T(8,128)(2,1)S(1)} %reshape.29.q0, bf16[2,72,512]{2,1,0:T(8,128)(2,1)S(1)} %collective-permute-done.q1, ...), custom_call_target="tpu_custom_call" | custom-call | tf_op jit(solution)/shard_map/window_tokens/pallas_call | solution.py:412
  29.1 1.3 %collective-permute-done.3 = bf16[256,2176]{1,0:T(8,128)(2,1)S(1)} collective-permute-done((bf16[256,2176]{1,0:T(8,128)(2,1)S(1)}, bf16[256,2176]{1,0:T(8,128)(2,1)S(1)}, u32[]{:S(2)}, u32[]{:S(2)}) %collective-permute-start.3) | collective-permute-done | bytes 1114144 | tf_op jit(solution)/shard_map/sum_cores/ppermute | solution.py:410
  30.4 0.4 fusion
  30.9 22.3 %all_to_all.10 = bf16[32,8,2176]{2,1,0:T(8,128)(2,1)S(1)} all-to-all(bf16[32,8,2176]{2,1,0:T(8,128)(2,1)S(1)} %bitcast.10), channel_id=1, replica_groups=mesh['xh'=2,'y'=4,'zh'=4,'zl'=2,'xl'=2,'core'=2] {'xh','y','zl','xl'}, dimensions={0} | all-to-all | bytes 2228224 | tf_op jit(solution)/shard_map/sum_near/all_to_all | solution.py:433
  53.2 0.2 convert_reduce_fusion.mine._
  53.4 0.5 collective-permute-start.7
  53.9 3.1 %collective-permute-start.4 = (f32[8,2176]{1,0:T(8,128)S(1)}, f32[8,2176]{1,0:T(8,128)S(1)}, u32[]{:S(2)}, u32[]{:S(2)}) collective-permute-start(f32[8,2176]{1,0:T(8,128)S(1)} %convert_reduce_fusion.mine._), channel_id=1, source_target_pairs={{0,8},{8,16},{16,24},{24,0},{1,9},{9,17},{17,25},{25,1},{2,10},{10... | collective-permute-start | bytes 208904 | tf_op jit(solution)/shard_map/sum_far/ppermute | solution.py:437
  57.0 4.1 %collective-permute-start.5 = (f32[8,2176]{1,0:T(8,128)S(1)}, f32[8,2176]{1,0:T(8,128)S(1)}, u32[]{:S(2)}, u32[]{:S(2)}) collective-permute-start(f32[8,2176]{1,0:T(8,128)S(1)} %convert_reduce_fusion.mine._), channel_id=1, source_target_pairs={{0,16},{8,24},{16,0},{24,8},{1,17},{9,25},{17,1},{25,9},{2,18},{10... | collective-permute-start | bytes 208904 | tf_op jit(solution)/shard_map/sum_far/ppermute | solution.py:437
  61.1 2.7 %collective-permute-start.6 = (f32[8,2176]{1,0:T(8,128)S(1)}, f32[8,2176]{1,0:T(8,128)S(1)}, u32[]{:S(2)}, u32[]{:S(2)}) collective-permute-start(f32[8,2176]{1,0:T(8,128)S(1)} %convert_reduce_fusion.mine._), channel_id=1, source_target_pairs={{0,24},{8,0},{16,8},{24,16},{1,25},{9,1},{17,9},{25,17},{2,26},{10... | collective-permute-start | bytes 208904 | tf_op jit(solution)/shard_map/sum_far/ppermute | solution.py:437
  63.8 0.0 collective-permute-done.4.next1
  63.8 1.5 %collective-permute-done.5.next2 = f32[8,2176]{1,0:T(8,128)S(1)} collective-permute-done((f32[8,2176]{1,0:T(8,128)S(1)}, f32[8,2176]{1,0:T(8,128)S(1)}, u32[]{:S(2)}, u32[]{:S(2)}) %collective-permute-start.5) | collective-permute-done | bytes 69664 | tf_op jit(solution)/shard_map/sum_far/ppermute | solution.py:437
  65.3 2.0 %collective-permute-done.6.next3 = f32[8,2176]{1,0:T(8,128)S(1)} collective-permute-done((f32[8,2176]{1,0:T(8,128)S(1)}, f32[8,2176]{1,0:T(8,128)S(1)}, u32[]{:S(2)}, u32[]{:S(2)}) %collective-permute-start.6) | collective-permute-done | bytes 69664 | tf_op jit(solution)/shard_map/sum_far/ppermute | solution.py:437
  67.3 0.1 sum_far.1
  67.4 0.0 collective-permute-done.7.north
  67.4 1.1 %broadcast_in_dim.10 = bf16[32,8,2176]{2,1,0:T(8,128)(2,1)} broadcast(bf16[8,2176]{1,0:T(8,128)(2,1)S(1)} %sum_far.1), dimensions={1,2} | broadcast | bytes 1148928 | tf_op jit(solution)/shard_map/share/broadcast_in_dim | solution.py:456
  68.5 6.4 %all-to-all-start.1 = ((bf16[32,8,2176]{2,1,0:T(8,128)(2,1)}), bf16[32,8,2176]{2,1,0:T(8,128)(2,1)S(1)}, u32[]{:S(2)}, u32[]{:S(2)}) async-start(bf16[32,8,2176]{2,1,0:T(8,128)(2,1)} %broadcast_in_dim.10), calls=%async_computation.1 | async-start | bytes 2228224 | tf_op jit(solution)/shard_map/share/all_to_all | solution.py:456
  74.9 0.1 slice.35
  75.0 0.4 pad_maximum_fusion
  75.4 4.7 %collective-permute-start.8 = (bf16[2,2,6,6,2,512]{5,4,3,2,1,0:T(2,128)(2,1)S(1)}, bf16[2,2,6,6,2,512]{5,4,3,2,1,0:T(2,128)(2,1)S(1)}, u32[]{:S(2)}, u32[]{:S(2)}) collective-permute-start(bf16[2,2,6,6,2,512]{5,4,3,2,1,0:T(2,128)(2,1)S(1)} %pad_maximum_fusion), channel_id=1, source_target_pairs={{0,1},{1,2},{2,3},{3,4},{4,5},{5,6},{6,7},{7,8},{8,9},{9,10},{10,1... | collective-permute-start | bytes 884744 | tf_op jit(solution)/shard_map/window_out/ppermute | solution.py:454
  80.1 10.4 %collective-permute-done.8.east = bf16[2,2,6,6,2,512]{5,4,3,2,1,0:T(2,128)(2,1)S(1)} collective-permute-done((bf16[2,2,6,6,2,512]{5,4,3,2,1,0:T(2,128)(2,1)S(1)}, bf16[2,2,6,6,2,512]{5,4,3,2,1,0:T(2,128)(2,1)S(1)}, u32[]{:S(2)}, u32[]{:S(2)}) %collective-permute-start.8) | collective-permute-done | bytes 294944 | tf_op jit(solution)/shard_map/window_out/ppermute | solution.py:454
  90.5 0.0 all-to-all-done.1
  90.5 4.9 %collective-permute-start.9 = (bf16[256,2176]{1,0:T(8,128)(2,1)S(1)}, bf16[256,2176]{1,0:T(8,128)(2,1)S(1)}, u32[]{:S(2)}, u32[]{:S(2)}) collective-permute-start(bf16[256,2176]{1,0:T(8,128)(2,1)S(1)} %bitcast.5), channel_id=1, source_target_pairs={{0,1},{1,0},{2,3},{3,2},{4,5},{5,4},{6,7},{7,6},{8,9},{9,8},{10,11... | collective-permute-start | bytes 3342344 | tf_op jit(solution)/shard_map/share/ppermute | solution.py:459
  95.3 2.4 %collective-permute-done.9.theirs = bf16[256,2176]{1,0:T(8,128)(2,1)S(1)} collective-permute-done((bf16[256,2176]{1,0:T(8,128)(2,1)S(1)}, bf16[256,2176]{1,0:T(8,128)(2,1)S(1)}, u32[]{:S(2)}, u32[]{:S(2)}) %collective-permute-start.9) | collective-permute-done | bytes 1114144 | tf_op jit(solution)/shard_map/share/ppermute | solution.py:459
  97.7 1.6 %finish.1 = (bf16[1,12,12,2,512]{4,3,2,1,0:T(2,128)(2,1)}, bf16[1,12,12,2,512]{4,3,2,1,0:T(2,128)(2,1)}, bf16[512,1536]{1,0:T(8,128)(2,1)}, bf16[512,512]{1,0:T(8,128)(2,1)}, f32[1,512]{1,0:T(1,128)}) custom-call(bf16[256,2176]{1,0:T(8,128)(2,1)S(1)} %bitcast.6, bf16[256,2176]{1,0:T(8,128)(2,1)S(1)} %collective-permute-done.9.theirs, ...), custom_call_target="tpu_custom_call" | custom-call | tf_op jit(solution)/shard_map/finish/pallas_call | solution.py:462
  (1 shorter events, 0.0 us)
Async XLA Ops:
  0.6 15.2 %copy-start = (bf16[512,1536]{1,0:T(8,128)(2,1)S(1)}, bf16[512,1536]{1,0:T(8,128)(2,1)}, u32[]{:S(2)}) copy-start(bf16[512,1536]{1,0:T(8,128)(2,1)} %wqkv.3) | copy-start | bytes 4718596
  0.6 15.2 %copy-start.1 = (bf16[512,512]{1,0:T(8,128)(2,1)S(1)}, bf16[512,512]{1,0:T(8,128)(2,1)}, u32[]{:S(2)}) copy-start(bf16[512,512]{1,0:T(8,128)(2,1)} %wout.3) | copy-start | bytes 1572868
  2.6 13.7 %collective-permute-start.1 = (bf16[2,72,512]{2,1,0:T(8,128)(2,1)S(1)}, bf16[2,72,512]{2,1,0:T(8,128)(2,1)S(1)}, u32[]{:S(2)}, u32[]{:S(2)}) collective-permute-start(bf16[2,72,512]{2,1,0:T(8,128)(2,1)S(1)} %reshape.31), channel_id=1, source_target_pairs={{0,224},{1,225},{2,226},{3,227},{4,228},{5,229},{6,230},{7,231},{8... | collective-permute-start | bytes 442376 | tf_op jit(solution)/shard_map/window_in/ppermute | solution.py:373
  9.0 7.3 %collective-permute-start.2 = (bf16[2,72,512]{2,1,0:T(8,128)(2,1)S(1)}, bf16[2,72,512]{2,1,0:T(8,128)(2,1)S(1)}, u32[]{:S(2)}, u32[]{:S(2)}) collective-permute-start(bf16[2,72,512]{2,1,0:T(8,128)(2,1)S(1)} %reshape.32), channel_id=1, source_target_pairs={{0,255},{1,224},{2,225},{3,226},{4,227},{5,228},{6,229},{7,230},{8... | collective-permute-start | bytes 442376 | tf_op jit(solution)/shard_map/window_in/ppermute | solution.py:374
  10.4 6.4 %copy-start.2 = (f32[512]{0:T(512)S(1)}, f32[512]{0:T(512)}, u32[]{:S(2)}) copy-start(f32[512]{0:T(512)} %param.6) | copy-start | bytes 6148
  10.7 6.1 %collective-permute-start = (bf16[2,72,512]{2,1,0:T(8,128)(2,1)S(1)}, bf16[2,72,512]{2,1,0:T(8,128)(2,1)S(1)}, u32[]{:S(2)}, u32[]{:S(2)}) collective-permute-start(bf16[2,72,512]{2,1,0:T(8,128)(2,1)S(1)} %reshape.30), channel_id=1, source_target_pairs={{0,31},{1,0},{2,1},{3,2},{4,3},{5,4},{6,5},{7,6},{8,7},{9,8},{10,9... | collective-permute-start | bytes 442376 | tf_op jit(solution)/shard_map/window_in/ppermute | solution.py:372
  25.2 5.3 %collective-permute-start.3 = (bf16[256,2176]{1,0:T(8,128)(2,1)S(1)}, bf16[256,2176]{1,0:T(8,128)(2,1)S(1)}, u32[]{:S(2)}, u32[]{:S(2)}) collective-permute-start(bf16[256,2176]{1,0:T(8,128)(2,1)S(1)} %get-tuple-element.42), channel_id=1, source_target_pairs={{0,1},{1,0},{2,3},{3,2},{4,5},{5,4},{6,7},{7,6},{8,9},{9,8},{10,11... | collective-permute-start | bytes 3342344 | tf_op jit(solution)/shard_map/sum_cores/ppermute | solution.py:410
  53.4 14.0 %collective-permute-start.7 = (bf16[2,2,6,6,2,512]{5,4,3,2,1,0:T(2,128)(2,1)S(1)}, bf16[2,2,6,6,2,512]{5,4,3,2,1,0:T(2,128)(2,1)S(1)}, u32[]{:S(2)}, u32[]{:S(2)}) collective-permute-start(bf16[2,2,6,6,2,512]{5,4,3,2,1,0:T(2,128)(2,1)S(1)} %get-tuple-element.47), channel_id=1, source_target_pairs={{0,32},{1,33},{2,34},{3,35},{4,36},{5,37},{6,38},{7,39},{8,40},{9,... | collective-permute-start | bytes 884744 | tf_op jit(solution)/shard_map/window_out/ppermute | solution.py:442
  53.9 9.9 %collective-permute-start.4 = (f32[8,2176]{1,0:T(8,128)S(1)}, f32[8,2176]{1,0:T(8,128)S(1)}, u32[]{:S(2)}, u32[]{:S(2)}) collective-permute-start(f32[8,2176]{1,0:T(8,128)S(1)} %convert_reduce_fusion.mine._), channel_id=1, source_target_pairs={{0,8},{8,16},{16,24},{24,0},{1,9},{9,17},{17,25},{25,1},{2,10},{10... | collective-permute-start | bytes 208904 | tf_op jit(solution)/shard_map/sum_far/ppermute | solution.py:437
  57.0 8.3 %collective-permute-start.5 = (f32[8,2176]{1,0:T(8,128)S(1)}, f32[8,2176]{1,0:T(8,128)S(1)}, u32[]{:S(2)}, u32[]{:S(2)}) collective-permute-start(f32[8,2176]{1,0:T(8,128)S(1)} %convert_reduce_fusion.mine._), channel_id=1, source_target_pairs={{0,16},{8,24},{16,0},{24,8},{1,17},{9,25},{17,1},{25,9},{2,18},{10... | collective-permute-start | bytes 208904 | tf_op jit(solution)/shard_map/sum_far/ppermute | solution.py:437
  61.1 6.2 %collective-permute-start.6 = (f32[8,2176]{1,0:T(8,128)S(1)}, f32[8,2176]{1,0:T(8,128)S(1)}, u32[]{:S(2)}, u32[]{:S(2)}) collective-permute-start(f32[8,2176]{1,0:T(8,128)S(1)} %convert_reduce_fusion.mine._), channel_id=1, source_target_pairs={{0,24},{8,0},{16,8},{24,16},{1,25},{9,1},{17,9},{25,17},{2,26},{10... | collective-permute-start | bytes 208904 | tf_op jit(solution)/shard_map/sum_far/ppermute | solution.py:437
  68.5 22.0 %all-to-all-start.1 = ((bf16[32,8,2176]{2,1,0:T(8,128)(2,1)}), bf16[32,8,2176]{2,1,0:T(8,128)(2,1)S(1)}, u32[]{:S(2)}, u32[]{:S(2)}) async-start(bf16[32,8,2176]{2,1,0:T(8,128)(2,1)} %broadcast_in_dim.10), calls=%async_computation.1 | async-start | bytes 2228224 | tf_op jit(solution)/shard_map/share/all_to_all | solution.py:456
  75.4 15.1 %collective-permute-start.8 = (bf16[2,2,6,6,2,512]{5,4,3,2,1,0:T(2,128)(2,1)S(1)}, bf16[2,2,6,6,2,512]{5,4,3,2,1,0:T(2,128)(2,1)S(1)}, u32[]{:S(2)}, u32[]{:S(2)}) collective-permute-start(bf16[2,2,6,6,2,512]{5,4,3,2,1,0:T(2,128)(2,1)S(1)} %pad_maximum_fusion), channel_id=1, source_target_pairs={{0,1},{1,2},{2,3},{3,4},{4,5},{5,6},{6,7},{7,8},{8,9},{9,10},{10,1... | collective-permute-start | bytes 884744 | tf_op jit(solution)/shard_map/window_out/ppermute | solution.py:454
  90.5 7.3 %collective-permute-start.9 = (bf16[256,2176]{1,0:T(8,128)(2,1)S(1)}, bf16[256,2176]{1,0:T(8,128)(2,1)S(1)}, u32[]{:S(2)}, u32[]{:S(2)}) collective-permute-start(bf16[256,2176]{1,0:T(8,128)(2,1)S(1)} %bitcast.5), channel_id=1, source_target_pairs={{0,1},{1,0},{2,3},{3,2},{4,5},{5,4},{6,7},{7,6},{8,9},{9,8},{10,11... | collective-permute-start | bytes 3342344 | tf_op jit(solution)/shard_map/share/ppermute | solution.py:459

commit v9 on v8

--- a/solution.py
+++ b/solution.py
@@ -309,28 +309,33 @@
     out[:, main:] = split_low(gain_total(total[:, main:]), 3)
 
 
-def finish_kernel(
-    mine, theirs, own, north, east,
-    mixed, grad_tokens, grad_qkv, grad_out, gain_grad, gains, sems,
-):
-    rows = mine.shape[0]
+def write_half(half, at, grad_qkv, grad_out, gain_grad, gains, copy):
+    rows = half.shape[0]
     wide = grad_qkv.shape[1]
     main = wide + grad_out.shape[1]
-    core = lax.axis_index("core")
-    copies = []
-
+    at = pl.multiple_of(at * rows, rows)
+    copy(half.at[:, :wide], grad_qkv.at[pl.ds(at, rows), :])
+    copy(half.at[:, wide:main], grad_out.at[pl.ds(at, rows), :])
+    column = half[:, main:].astype(F32).T
+    gains[...] = column[0:1] + column[1:2] + column[2:3]
+    copy(gains, gain_grad.at[:, pl.ds(at, rows)])
+
+
+def copier(sems, copies):
     def copy(src, dst):
         item = pltpu.make_async_copy(src, dst, sems.at[len(copies)])
         item.start()
         copies.append(item)
 
-    for n, half in enumerate((mine, theirs)):
-        at = pl.multiple_of((core if n == 0 else 1 - core) * rows, rows)
-        copy(half.at[:, :wide], grad_qkv.at[pl.ds(at, rows), :])
-        copy(half.at[:, wide:main], grad_out.at[pl.ds(at, rows), :])
-        column = half[:, main:].astype(F32).T
-        gains[:, pl.ds(at, rows)] = column[0:1] + column[1:2] + column[2:3]
-    copy(gains, gain_grad)
+    return copy
+
+
+def first_finish_kernel(
+    mine, own, north, east, mixed, grad_tokens, grad_qkv, grad_out, gain_grad, gains, sems
+):
+    copies = []
+    copy = copier(sems, copies)
+    write_half(mine, lax.axis_index("core"), grad_qkv, grad_out, gain_grad, gains, copy)
     for quad, at, lon in (
         (own, SHIFT, SHIFT),
         (north.at[0], 0, SHIFT),
@@ -340,6 +345,14 @@
         block = (0, pl.ds(at, SHIFT), pl.ds(lon, SHIFT))
         copy(quad.at[0], mixed.at[block])
         copy(quad.at[1], grad_tokens.at[block])
+    for item in copies:
+        item.wait()
+
+
+def last_finish_kernel(theirs, _, __, ___, grad_qkv, grad_out, gain_grad, gains, sems):
+    copies = []
+    copy = copier(sems, copies)
+    write_half(theirs, 1 - lax.axis_index("core"), grad_qkv, grad_out, gain_grad, gains, copy)
     for item in copies:
         item.wait()
 
@@ -459,20 +472,28 @@
         theirs = lax.ppermute(mine, "core", swap)
     with jax.named_scope("finish"):
         shape = (1, 2 * SHIFT, 2 * SHIFT, levels, feat)
-        mixed, grad_tokens, grad_qkv, grad_out, gain_gradient = pl.pallas_call(
-            finish_kernel,
-            in_specs=[vmem] * 2 + [hbm] * 3,
+        final = [
+            jax.ShapeDtypeStruct((feat, 3 * feat), BF16),
+            jax.ShapeDtypeStruct((feat, feat), BF16),
+            jax.ShapeDtypeStruct((1, feat), F32),
+        ]
+        mixed, grad_tokens, *halves = pl.pallas_call(
+            first_finish_kernel,
+            in_specs=[vmem] + [hbm] * 3,
             out_specs=[hbm] * 5,
-            out_shape=[
-                jax.ShapeDtypeStruct(shape, BF16),
-                jax.ShapeDtypeStruct(shape, BF16),
-                jax.ShapeDtypeStruct((feat, 3 * feat), BF16),
-                jax.ShapeDtypeStruct((feat, feat), BF16),
-                jax.ShapeDtypeStruct((1, feat), F32),
-            ],
-            scratch_shapes=[pltpu.VMEM((1, feat), F32), pltpu.SemaphoreType.DMA((13,))],
+            out_shape=[jax.ShapeDtypeStruct(shape, BF16)] * 2 + final,
+            scratch_shapes=[pltpu.VMEM((1, rows), F32), pltpu.SemaphoreType.DMA((11,))],
             compiler_params=params,
-        )(mine, theirs, own, north, east)
+        )(mine, own, north, east)
+        grad_qkv, grad_out, gain_gradient = pl.pallas_call(
+            last_finish_kernel,
+            in_specs=[vmem] + [hbm] * 3,
+            out_specs=[hbm] * 3,
+            out_shape=final,
+            input_output_aliases={1: 0, 2: 1, 3: 2},
+            scratch_shapes=[pltpu.VMEM((1, rows), F32), pltpu.SemaphoreType.DMA((3,))],
+            compiler_params=params,
+        )(theirs, *halves)
     return mixed, grad_tokens, gain_gradient[0], grad_qkv, grad_out
 
 

time: 99.7 us -> 99.1 us (level)
  waiting for transfers between devices: 18.1 us -> 16.8 us
    ppermute x1, waiting for transfers between devices: 2.38 us -> 1.12 us  [shards(): theirs = lax.ppermute(mine, 'core', swap)]
    pallas_call x1 -> x2, Pallas kernels: 1.62 us -> 2.25 us  [the longest x1 1.26 us: shards(): pl.pallas_call(first_finish_kernel, in_specs=[vmem] + [hbm] * 3, out_spec...]
  transfers between devices with their start and end apart: 11 -> 11, of which waited for: 6 -> 6; matrix products, arithmetic and copies ran while one was open for 1% -> 1% of each run, Pallas kernels for 2% -> 3%
where the time goes in v9:
time: 99.1 us; the launch traced here: 98.9 us
  starting transfers between devices  41.6 us (42%)
  blocking collectives  22.3 us (23%)
  waiting for transfers between devices  16.8 us (17%)
  Pallas kernels  12.2 us (12%)
  local copies, waits for them, and re-layouts  3.13 us (3%)
  other arithmetic  1.85 us (2%)
    all_to_all x1, blocking collectives, shards(): pieces = lax.all_to_all(pair_sum.reshape(near, chunk, width), NEAR, 0, 0)  22.3 us
    ppermute x1, waiting for transfers between devices, shards(): east = lax.ppermute(east, EVERY, pairs(lambda a, o: (a, o + 1)))  10.4 us
    ppermute x3, starting transfers between devices, shards(): lax.ppermute(piece, FAR, [(i, (i + by) % far) for i in range(far)])  9.89 us
    pallas_call x1, Pallas kernels, shards(): pl.pallas_call(grads_kernel, in_specs=[vmem] * 8, out_specs=[vmem] * 8, o...  8.36 us
    all_to_all x1, starting transfers between devices, shards(): lax.all_to_all(jnp.broadcast_to(piece[None], (near,) + piece.shape), NEAR...  6.38 us
    ppermute x1, starting transfers between devices, shards(): north = lax.ppermute(north, EVERY, pairs(lambda a, o: (a - 1, o)))  6.1 us
    ppermute x1, starting transfers between devices, shards(): theirs = lax.ppermute(mine, 'core', swap)  4.87 us
    ppermute x1, starting transfers between devices, shards(): east = lax.ppermute(east, EVERY, pairs(lambda a, o: (a, o - 1)))  4.84 us
  transfers between devices with their start and end apart: 11, of which 6 were waited for; matrix products, arithmetic and copies ran while one was open for 1% of the time, Pallas kernels for 3%

profile of v9, /device:TPU:1, one launch (start us, length us, event | category | flops | bytes accessed | tf_op | source)
XLA Modules:
  0.0 98.9 jit_solution(13751710007884970292)
XLA Ops:
  0.6 0.0 copy-start
  0.6 0.0 copy-start.1
  0.7 1.7 %fusion.1 = (bf16[1,6,6,2,512]{4,3,2,1,0:T(2,128)(2,1)S(1)}, bf16[1,6,6,2,512]{4,3,2,1,0:T(2,128)(2,1)S(1)}, bf16[1,6,6,2,512]{4,3,2,1,0:T(2,128)(2,1)S(1)}, bf1...) fusion(bf16[1,12,12,2,512]{4,3,2,1,0:T(2,128)(2,1)} %param.5, ...), kind=kLoop, calls=%fused_computation.9 | loop fusion | bytes 1179648 | tf_op jit(solution)/shard_map/window_in/slice | solution.py:379
  2.4 0.2 pad_maximum_fusion.3
  2.6 0.1 reshape.31
  2.6 6.1 %collective-permute-start.1 = (bf16[2,72,512]{2,1,0:T(8,128)(2,1)S(1)}, bf16[2,72,512]{2,1,0:T(8,128)(2,1)S(1)}, u32[]{:S(2)}, u32[]{:S(2)}) collective-permute-start(bf16[2,72,512]{2,1,0:T(8,128)(2,1)S(1)} %reshape.31), channel_id=1, source_target_pairs={{0,224},{1,225},{2,226},{3,227},{4,228},{5,229},{6,230},{7,231},{8... | collective-permute-start | bytes 442376 | tf_op jit(solution)/shard_map/window_in/ppermute | solution.py:386
  8.7 0.2 pad_maximum_fusion.4
  8.9 0.1 reshape.32
  9.0 1.4 %collective-permute-start.2 = (bf16[2,72,512]{2,1,0:T(8,128)(2,1)S(1)}, bf16[2,72,512]{2,1,0:T(8,128)(2,1)S(1)}, u32[]{:S(2)}, u32[]{:S(2)}) collective-permute-start(bf16[2,72,512]{2,1,0:T(8,128)(2,1)S(1)} %reshape.32), channel_id=1, source_target_pairs={{0,255},{1,224},{2,225},{3,226},{4,227},{5,228},{6,229},{7,230},{8... | collective-permute-start | bytes 442376 | tf_op jit(solution)/shard_map/window_in/ppermute | solution.py:387
  10.4 0.2 pad_maximum_fusion.2
  10.6 0.1 reshape.30
  10.7 4.8 %collective-permute-start = (bf16[2,72,512]{2,1,0:T(8,128)(2,1)S(1)}, bf16[2,72,512]{2,1,0:T(8,128)(2,1)S(1)}, u32[]{:S(2)}, u32[]{:S(2)}) collective-permute-start(bf16[2,72,512]{2,1,0:T(8,128)(2,1)S(1)} %reshape.30), channel_id=1, source_target_pairs={{0,31},{1,0},{2,1},{3,2},{4,3},{5,4},{6,5},{7,6},{8,7},{9,8},{10,9... | collective-permute-start | bytes 442376 | tf_op jit(solution)/shard_map/window_in/ppermute | solution.py:385
  15.5 0.2 pad_maximum_fusion.1
  15.7 0.1 reshape.29.q0
  15.8 0.0 copy-done
  15.8 0.0 copy-done.1
  15.8 0.5 weights.1
  16.3 0.0 collective-permute-done.1.q2
  16.3 0.0 collective-permute-done.2.q3
  16.3 0.5 collective-permute-done.q1
  16.8 0.0 copy-done.2
  16.8 8.4 %window_grads.1 = (bf16[256,2176]{1,0:T(8,128)(2,1)S(1)}, bf16[512,384]{1,0:T(8,128)(2,1)S(1)}, bf16[288,512]{1,0:T(8,128)(2,1)S(1)}, bf16[512,384]{1,0:T(8,128)...) custom-call(bf16[2,72,512]{2,1,0:T(8,128)(2,1)S(1)} %reshape.29.q0, ...), custom_call_target="tpu_custom_call" | custom-call | tf_op jit(solution)/shard_map/window_grads/pallas_call | solution.py:404
  25.2 2.9 %collective-permute-start.3 = (bf16[256,2176]{1,0:T(8,128)(2,1)S(1)}, bf16[256,2176]{1,0:T(8,128)(2,1)S(1)}, u32[]{:S(2)}, u32[]{:S(2)}) collective-permute-start(bf16[256,2176]{1,0:T(8,128)(2,1)S(1)} %get-tuple-element.45), channel_id=1, source_target_pairs={{0,1},{1,0},{2,3},{3,2},{4,5},{5,4},{6,7},{7,6},{8,9},{9,8},{10,11... | collective-permute-start | bytes 3342344 | tf_op jit(solution)/shard_map/sum_cores/ppermute | solution.py:423
  28.1 1.0 %window_tokens.1 = (f32[256,2176]{1,0:T(8,128)S(1)}, bf16[2,6,6,2,512]{4,3,2,1,0:T(2,128)(2,1)S(1)}, bf16[2,6,6,2,512]{4,3,2,1,0:T(2,128)(2,1)S(1)}, bf16[2,2,6,6,2,512]{5,4,3,2,1,0:T(2,128)(2,1)S(1)}) custom-call(bf16[2,72,512]{2,1,0:T(8,128)(2,1)S(1)} %reshape.29.q0, bf16[2,72,512]{2,1,0:T(8,128)(2,1)S(1)} %collective-permute-done.q1, ...), custom_call_target="tpu_custom_call" | custom-call | tf_op jit(solution)/shard_map/window_tokens/pallas_call | solution.py:425
  29.1 1.3 %collective-permute-done.3 = bf16[256,2176]{1,0:T(8,128)(2,1)S(1)} collective-permute-done((bf16[256,2176]{1,0:T(8,128)(2,1)S(1)}, bf16[256,2176]{1,0:T(8,128)(2,1)S(1)}, u32[]{:S(2)}, u32[]{:S(2)}) %collective-permute-start.3) | collective-permute-done | bytes 1114144 | tf_op jit(solution)/shard_map/sum_cores/ppermute | solution.py:423
  30.4 0.4 fusion
  30.9 22.3 %all_to_all.10 = bf16[32,8,2176]{2,1,0:T(8,128)(2,1)S(1)} all-to-all(bf16[32,8,2176]{2,1,0:T(8,128)(2,1)S(1)} %bitcast.10), channel_id=1, replica_groups=mesh['xh'=2,'y'=4,'zh'=4,'zl'=2,'xl'=2,'core'=2] {'xh','y','zl','xl'}, dimensions={0} | all-to-all | bytes 2228224 | tf_op jit(solution)/shard_map/sum_near/all_to_all | solution.py:446
  53.2 0.2 convert_reduce_fusion.mine._
  53.4 0.5 collective-permute-start.7
  53.9 3.1 %collective-permute-start.4 = (f32[8,2176]{1,0:T(8,128)S(1)}, f32[8,2176]{1,0:T(8,128)S(1)}, u32[]{:S(2)}, u32[]{:S(2)}) collective-permute-start(f32[8,2176]{1,0:T(8,128)S(1)} %convert_reduce_fusion.mine._), channel_id=1, source_target_pairs={{0,8},{8,16},{16,24},{24,0},{1,9},{9,17},{17,25},{25,1},{2,10},{10... | collective-permute-start | bytes 208904 | tf_op jit(solution)/shard_map/sum_far/ppermute | solution.py:450
  57.0 4.1 %collective-permute-start.5 = (f32[8,2176]{1,0:T(8,128)S(1)}, f32[8,2176]{1,0:T(8,128)S(1)}, u32[]{:S(2)}, u32[]{:S(2)}) collective-permute-start(f32[8,2176]{1,0:T(8,128)S(1)} %convert_reduce_fusion.mine._), channel_id=1, source_target_pairs={{0,16},{8,24},{16,0},{24,8},{1,17},{9,25},{17,1},{25,9},{2,18},{10... | collective-permute-start | bytes 208904 | tf_op jit(solution)/shard_map/sum_far/ppermute | solution.py:450
  61.1 2.7 %collective-permute-start.6 = (f32[8,2176]{1,0:T(8,128)S(1)}, f32[8,2176]{1,0:T(8,128)S(1)}, u32[]{:S(2)}, u32[]{:S(2)}) collective-permute-start(f32[8,2176]{1,0:T(8,128)S(1)} %convert_reduce_fusion.mine._), channel_id=1, source_target_pairs={{0,24},{8,0},{16,8},{24,16},{1,25},{9,1},{17,9},{25,17},{2,26},{10... | collective-permute-start | bytes 208904 | tf_op jit(solution)/shard_map/sum_far/ppermute | solution.py:450
  63.8 0.0 collective-permute-done.4.next1
  63.8 1.5 %collective-permute-done.5.next2 = f32[8,2176]{1,0:T(8,128)S(1)} collective-permute-done((f32[8,2176]{1,0:T(8,128)S(1)}, f32[8,2176]{1,0:T(8,128)S(1)}, u32[]{:S(2)}, u32[]{:S(2)}) %collective-permute-start.5) | collective-permute-done | bytes 69664 | tf_op jit(solution)/shard_map/sum_far/ppermute | solution.py:450
  65.3 2.0 %collective-permute-done.6.next3 = f32[8,2176]{1,0:T(8,128)S(1)} collective-permute-done((f32[8,2176]{1,0:T(8,128)S(1)}, f32[8,2176]{1,0:T(8,128)S(1)}, u32[]{:S(2)}, u32[]{:S(2)}) %collective-permute-start.6) | collective-permute-done | bytes 69664 | tf_op jit(solution)/shard_map/sum_far/ppermute | solution.py:450
  67.3 0.1 sum_far.1
  67.4 0.0 collective-permute-done.7.north
  67.4 1.1 %broadcast_in_dim.10 = bf16[32,8,2176]{2,1,0:T(8,128)(2,1)} broadcast(bf16[8,2176]{1,0:T(8,128)(2,1)S(1)} %sum_far.1), dimensions={1,2} | broadcast | bytes 1148928 | tf_op jit(solution)/shard_map/share/broadcast_in_dim | solution.py:469
  68.5 6.4 %all-to-all-start.1 = ((bf16[32,8,2176]{2,1,0:T(8,128)(2,1)}), bf16[32,8,2176]{2,1,0:T(8,128)(2,1)S(1)}, u32[]{:S(2)}, u32[]{:S(2)}) async-start(bf16[32,8,2176]{2,1,0:T(8,128)(2,1)} %broadcast_in_dim.10), calls=%async_computation.1 | async-start | bytes 2228224 | tf_op jit(solution)/shard_map/share/all_to_all | solution.py:469
  74.9 0.1 slice.35
  75.0 0.4 pad_maximum_fusion
  75.4 4.7 %collective-permute-start.8 = (bf16[2,2,6,6,2,512]{5,4,3,2,1,0:T(2,128)(2,1)S(1)}, bf16[2,2,6,6,2,512]{5,4,3,2,1,0:T(2,128)(2,1)S(1)}, u32[]{:S(2)}, u32[]{:S(2)}) collective-permute-start(bf16[2,2,6,6,2,512]{5,4,3,2,1,0:T(2,128)(2,1)S(1)} %pad_maximum_fusion), channel_id=1, source_target_pairs={{0,1},{1,2},{2,3},{3,4},{4,5},{5,6},{6,7},{7,8},{8,9},{9,10},{10,1... | collective-permute-start | bytes 884744 | tf_op jit(solution)/shard_map/window_out/ppermute | solution.py:467
  80.1 10.4 %collective-permute-done.8.east = bf16[2,2,6,6,2,512]{5,4,3,2,1,0:T(2,128)(2,1)S(1)} collective-permute-done((bf16[2,2,6,6,2,512]{5,4,3,2,1,0:T(2,128)(2,1)S(1)}, bf16[2,2,6,6,2,512]{5,4,3,2,1,0:T(2,128)(2,1)S(1)}, u32[]{:S(2)}, u32[]{:S(2)}) %collective-permute-start.8) | collective-permute-done | bytes 294944 | tf_op jit(solution)/shard_map/window_out/ppermute | solution.py:467
  90.5 0.0 all-to-all-done.1
  90.5 4.9 %collective-permute-start.9 = (bf16[256,2176]{1,0:T(8,128)(2,1)S(1)}, bf16[256,2176]{1,0:T(8,128)(2,1)S(1)}, u32[]{:S(2)}, u32[]{:S(2)}) collective-permute-start(bf16[256,2176]{1,0:T(8,128)(2,1)S(1)} %bitcast.5), channel_id=1, source_target_pairs={{0,1},{1,0},{2,3},{3,2},{4,5},{5,4},{6,7},{7,6},{8,9},{9,8},{10,11... | collective-permute-start | bytes 3342344 | tf_op jit(solution)/shard_map/share/ppermute | solution.py:472
  95.3 1.3 %finish.2 = (bf16[1,12,12,2,512]{4,3,2,1,0:T(2,128)(2,1)}, bf16[1,12,12,2,512]{4,3,2,1,0:T(2,128)(2,1)}, bf16[512,1536]{1,0:T(8,128)(2,1)}, bf16[512,512]{1,0:T(8,128)(2,1)}, f32[1,512]{1,0:T(1,128)}) custom-call(bf16[256,2176]{1,0:T(8,128)(2,1)S(1)} %bitcast.6, bf16[2,6,6,2,512]{4,3,2,1,0:T(2,128)(2,1)S(1)} %get-tuple-element.55.own, ...), custom_call_target="tpu_custom_call" | custom-call | tf_op jit(solution)/shard_map/finish/pallas_call | solution.py:480
  96.6 1.1 %collective-permute-done.9.theirs = bf16[256,2176]{1,0:T(8,128)(2,1)S(1)} collective-permute-done((bf16[256,2176]{1,0:T(8,128)(2,1)S(1)}, bf16[256,2176]{1,0:T(8,128)(2,1)S(1)}, u32[]{:S(2)}, u32[]{:S(2)}) %collective-permute-start.9) | collective-permute-done | bytes 1114144 | tf_op jit(solution)/shard_map/share/ppermute | solution.py:472
  97.7 1.0 %finish.3 = (bf16[512,1536]{1,0:T(8,128)(2,1)}, bf16[512,512]{1,0:T(8,128)(2,1)}, f32[1,512]{1,0:T(1,128)}) custom-call(bf16[256,2176]{1,0:T(8,128)(2,1)S(1)} %collective-permute-done.9.theirs, bf16[512,1536]{1,0:T(8,128)(2,1)} %get-tuple-element.59._, ...), custom_call_target="tpu_custom_call", output_to_operand_aliasing={{0}: (1, {}), {1}: (2, {}), {2}: (3, {})} | custom-call | tf_op jit(solution)/shard_map/finish/pallas_call | solution.py:488
  (2 shorter events, 0.0 us)
Async XLA Ops:
  0.6 15.2 %copy-start = (bf16[512,1536]{1,0:T(8,128)(2,1)S(1)}, bf16[512,1536]{1,0:T(8,128)(2,1)}, u32[]{:S(2)}) copy-start(bf16[512,1536]{1,0:T(8,128)(2,1)} %wqkv.3) | copy-start | bytes 4718596
  0.6 15.2 %copy-start.1 = (bf16[512,512]{1,0:T(8,128)(2,1)S(1)}, bf16[512,512]{1,0:T(8,128)(2,1)}, u32[]{:S(2)}) copy-start(bf16[512,512]{1,0:T(8,128)(2,1)} %wout.3) | copy-start | bytes 1572868
  2.6 13.7 %collective-permute-start.1 = (bf16[2,72,512]{2,1,0:T(8,128)(2,1)S(1)}, bf16[2,72,512]{2,1,0:T(8,128)(2,1)S(1)}, u32[]{:S(2)}, u32[]{:S(2)}) collective-permute-start(bf16[2,72,512]{2,1,0:T(8,128)(2,1)S(1)} %reshape.31), channel_id=1, source_target_pairs={{0,224},{1,225},{2,226},{3,227},{4,228},{5,229},{6,230},{7,231},{8... | collective-permute-start | bytes 442376 | tf_op jit(solution)/shard_map/window_in/ppermute | solution.py:386
  9.0 7.3 %collective-permute-start.2 = (bf16[2,72,512]{2,1,0:T(8,128)(2,1)S(1)}, bf16[2,72,512]{2,1,0:T(8,128)(2,1)S(1)}, u32[]{:S(2)}, u32[]{:S(2)}) collective-permute-start(bf16[2,72,512]{2,1,0:T(8,128)(2,1)S(1)} %reshape.32), channel_id=1, source_target_pairs={{0,255},{1,224},{2,225},{3,226},{4,227},{5,228},{6,229},{7,230},{8... | collective-permute-start | bytes 442376 | tf_op jit(solution)/shard_map/window_in/ppermute | solution.py:387
  10.4 6.4 %copy-start.2 = (f32[512]{0:T(512)S(1)}, f32[512]{0:T(512)}, u32[]{:S(2)}) copy-start(f32[512]{0:T(512)} %param.6) | copy-start | bytes 6148
  10.7 6.1 %collective-permute-start = (bf16[2,72,512]{2,1,0:T(8,128)(2,1)S(1)}, bf16[2,72,512]{2,1,0:T(8,128)(2,1)S(1)}, u32[]{:S(2)}, u32[]{:S(2)}) collective-permute-start(bf16[2,72,512]{2,1,0:T(8,128)(2,1)S(1)} %reshape.30), channel_id=1, source_target_pairs={{0,31},{1,0},{2,1},{3,2},{4,3},{5,4},{6,5},{7,6},{8,7},{9,8},{10,9... | collective-permute-start | bytes 442376 | tf_op jit(solution)/shard_map/window_in/ppermute | solution.py:385
  25.2 5.3 %collective-permute-start.3 = (bf16[256,2176]{1,0:T(8,128)(2,1)S(1)}, bf16[256,2176]{1,0:T(8,128)(2,1)S(1)}, u32[]{:S(2)}, u32[]{:S(2)}) collective-permute-start(bf16[256,2176]{1,0:T(8,128)(2,1)S(1)} %get-tuple-element.45), channel_id=1, source_target_pairs={{0,1},{1,0},{2,3},{3,2},{4,5},{5,4},{6,7},{7,6},{8,9},{9,8},{10,11... | collective-permute-start | bytes 3342344 | tf_op jit(solution)/shard_map/sum_cores/ppermute | solution.py:423
  53.4 14.0 %collective-permute-start.7 = (bf16[2,2,6,6,2,512]{5,4,3,2,1,0:T(2,128)(2,1)S(1)}, bf16[2,2,6,6,2,512]{5,4,3,2,1,0:T(2,128)(2,1)S(1)}, u32[]{:S(2)}, u32[]{:S(2)}) collective-permute-start(bf16[2,2,6,6,2,512]{5,4,3,2,1,0:T(2,128)(2,1)S(1)} %get-tuple-element.50), channel_id=1, source_target_pairs={{0,32},{1,33},{2,34},{3,35},{4,36},{5,37},{6,38},{7,39},{8,40},{9,... | collective-permute-start | bytes 884744 | tf_op jit(solution)/shard_map/window_out/ppermute | solution.py:455
  53.9 9.9 %collective-permute-start.4 = (f32[8,2176]{1,0:T(8,128)S(1)}, f32[8,2176]{1,0:T(8,128)S(1)}, u32[]{:S(2)}, u32[]{:S(2)}) collective-permute-start(f32[8,2176]{1,0:T(8,128)S(1)} %convert_reduce_fusion.mine._), channel_id=1, source_target_pairs={{0,8},{8,16},{16,24},{24,0},{1,9},{9,17},{17,25},{25,1},{2,10},{10... | collective-permute-start | bytes 208904 | tf_op jit(solution)/shard_map/sum_far/ppermute | solution.py:450
  57.0 8.3 %collective-permute-start.5 = (f32[8,2176]{1,0:T(8,128)S(1)}, f32[8,2176]{1,0:T(8,128)S(1)}, u32[]{:S(2)}, u32[]{:S(2)}) collective-permute-start(f32[8,2176]{1,0:T(8,128)S(1)} %convert_reduce_fusion.mine._), channel_id=1, source_target_pairs={{0,16},{8,24},{16,0},{24,8},{1,17},{9,25},{17,1},{25,9},{2,18},{10... | collective-permute-start | bytes 208904 | tf_op jit(solution)/shard_map/sum_far/ppermute | solution.py:450
  61.1 6.2 %collective-permute-start.6 = (f32[8,2176]{1,0:T(8,128)S(1)}, f32[8,2176]{1,0:T(8,128)S(1)}, u32[]{:S(2)}, u32[]{:S(2)}) collective-permute-start(f32[8,2176]{1,0:T(8,128)S(1)} %convert_reduce_fusion.mine._), channel_id=1, source_target_pairs={{0,24},{8,0},{16,8},{24,16},{1,25},{9,1},{17,9},{25,17},{2,26},{10... | collective-permute-start | bytes 208904 | tf_op jit(solution)/shard_map/sum_far/ppermute | solution.py:450
  68.5 22.0 %all-to-all-start.1 = ((bf16[32,8,2176]{2,1,0:T(8,128)(2,1)}), bf16[32,8,2176]{2,1,0:T(8,128)(2,1)S(1)}, u32[]{:S(2)}, u32[]{:S(2)}) async-start(bf16[32,8,2176]{2,1,0:T(8,128)(2,1)} %broadcast_in_dim.10), calls=%async_computation.1 | async-start | bytes 2228224 | tf_op jit(solution)/shard_map/share/all_to_all | solution.py:469
  75.4 15.1 %collective-permute-start.8 = (bf16[2,2,6,6,2,512]{5,4,3,2,1,0:T(2,128)(2,1)S(1)}, bf16[2,2,6,6,2,512]{5,4,3,2,1,0:T(2,128)(2,1)S(1)}, u32[]{:S(2)}, u32[]{:S(2)}) collective-permute-start(bf16[2,2,6,6,2,512]{5,4,3,2,1,0:T(2,128)(2,1)S(1)} %pad_maximum_fusion), channel_id=1, source_target_pairs={{0,1},{1,2},{2,3},{3,4},{4,5},{5,6},{6,7},{7,8},{8,9},{9,10},{10,1... | collective-permute-start | bytes 884744 | tf_op jit(solution)/shard_map/window_out/ppermute | solution.py:467
  90.5 7.3 %collective-permute-start.9 = (bf16[256,2176]{1,0:T(8,128)(2,1)S(1)}, bf16[256,2176]{1,0:T(8,128)(2,1)S(1)}, u32[]{:S(2)}, u32[]{:S(2)}) collective-permute-start(bf16[256,2176]{1,0:T(8,128)(2,1)S(1)} %bitcast.5), channel_id=1, source_target_pairs={{0,1},{1,0},{2,3},{3,2},{4,5},{5,4},{6,7},{7,6},{8,9},{9,8},{10,11... | collective-permute-start | bytes 3342344 | tf_op jit(solution)/shard_map/share/ppermute | solution.py:472

commit v10 on v9

--- a/solution.py
+++ b/solution.py
@@ -45,14 +45,16 @@
     return lax.broadcasted_iota(jnp.int32, shape, len(shape) - 1)
 
 
-def split_low(value, terms):
-    lane = lanes(value.shape)
-    out = jnp.zeros_like(value)
-    rest = value
-    for i in range(terms):
-        part = rest.astype(BF16).astype(F32)
-        out = jnp.where(lane == i, part, out)
-        rest = rest - part
+def split_low(tile):
+    lane = lanes(tile.shape)
+    out = jnp.zeros_like(tile)
+    for first in (0, 2):
+        held = jnp.where((lane == first) | (lane == first + 1), tile, 0.0)
+        rest = jnp.broadcast_to(jnp.sum(held, -1, keepdims=True), tile.shape)
+        for i in range(3):
+            part = rest.astype(BF16).astype(F32)
+            out = jnp.where(lane == first // 2 * 3 + i, part, out)
+            rest = rest - part
     return out.astype(BF16)
 
 
@@ -75,7 +77,7 @@
 
 def grads_kernel(
     q0, q1, q2, q3, gain, wqkv, wqkv_t, wout,
-    send, attn_t, back, normed_t, g_low, dq_t, dkv_t, gain_col,
+    send, attn_t, normed_t, g_low, dq_t, dkv_t,
     wide, normed, q_t, kv_t, kv, do_t,
     diag, side, bias, scores, d_probs, p_low, d_low, acc,
 ):
@@ -217,23 +219,11 @@
             collect((n - 1) % 2, *blocks[n - 1])
     collect((len(blocks) - 1) % 2, *blocks[-1])
 
-    from_q = dot(wqkv[:, :feat], dq_t[...])
-    from_kv = dot(wqkv[:, feat:], dkv_t[...])
-    back[:main, :] = (from_q[:, :main] + from_kv[:, :main]).T.astype(BF16)
-    rest = from_q[:, main:].T
-    last = from_kv[:, main:].T
-    for j in range(per):
-        last = last + rest[j * left : (j + 1) * left]
-    back[main:, :] = last.astype(BF16)
-    part_gain = jnp.sum(back[...].astype(F32) * wide[...], 0, keepdims=True)
-    column = jnp.broadcast_to(part_gain, (128, feat)).T
-    gain_col[...] = jnp.where(lanes(column.shape) < 2, column, 0.0)
-
     rows = feat // 2
     theirs = pl.multiple_of((1 - core) * rows, rows)
     for block, value in enumerate(partial_sums(theirs, normed_t, g_low, dq_t, dkv_t, attn_t)):
         send[:, block * feat : (block + 1) * feat] = value.astype(BF16)
-    send[:, 4 * feat :] = gain_col[pl.ds(theirs, rows), :].astype(BF16)
+    send[:, 4 * feat :] = jnp.zeros((rows, 128), BF16)
 
 
 def grads_scratch(tokens, feat):
@@ -257,15 +247,14 @@
 
 
 def tokens_kernel(
-    q0, q1, q2, q3, gain, wout, attn_t, back, normed_t, g_low, dq_t, dkv_t, gain_col,
-    keep, own, east, north, wide,
+    q0, q1, q2, q3, gain, wqkv, wout, attn_t, normed_t, g_low, dq_t, dkv_t,
+    keep, own, east, north, wide, back, gain_col,
 ):
     feat = attn_t.shape[0]
     half = feat // 2
     mine = pl.multiple_of(lax.axis_index("core") * half, half)
     for block, value in enumerate(partial_sums(mine, normed_t, g_low, dq_t, dkv_t, attn_t)):
         keep[:, block * feat : (block + 1) * feat] = value
-    keep[:, 4 * feat :] = gain_col[pl.ds(mine, half), :]
     quads, outs = (q0, q1, q2, q3), (own, east, north.at[0], north.at[1])
     rows = q0.shape[1]
     gather_quads(quads, 0, wide)
@@ -280,6 +269,23 @@
     for j, out in enumerate(outs):
         out[0] = mixed[j * rows : (j + 1) * rows].astype(BF16).reshape(out.shape[1:])
     xhat, inv = normalise(tok)
+    per = 128 // (feat // HEADS)
+    from_q = dot(wqkv[:, :feat], dq_t[...])
+    from_kv = dot(wqkv[:, feat:], dkv_t[...])
+    back[:main, :] = (from_q[:, :main] + from_kv[:, :main]).T.astype(BF16)
+    rest = from_q[:, main:].T
+    last = from_kv[:, main:].T
+    for j in range(per):
+        last = last + rest[j * left : (j + 1) * left]
+    back[main:, :] = last.astype(BF16)
+    part_gain = jnp.sum(back[...].astype(F32) * xhat, 0, keepdims=True)
+    column = jnp.broadcast_to(part_gain, (128, feat)).T
+    gain_col[...] = column
+
+    theirs = pl.multiple_of((1 - lax.axis_index("core")) * half, half)
+    lane = lanes((half, 128))
+    other = jnp.where(lane < 4, gain_col[pl.ds(theirs, half), :], 0.0)
+    keep[:, 4 * feat :] = jnp.where(lane < 2, gain_col[pl.ds(mine, half), :], other)
     scaled = back[...].astype(F32) * gain[...]
     inner = (
         scaled
@@ -292,33 +298,27 @@
         out[1] = grad[j * rows : (j + 1) * rows].astype(BF16).reshape(out.shape[1:])
 
 
-def gain_total(tile):
-    return jnp.where(lanes(tile.shape) == 0, jnp.sum(tile, -1, keepdims=True), 0.0)
-
-
 def add_pair(keep, other):
     total = keep + other.astype(F32)
     rest = total - lax.reduce_precision(total, 8, 7)
-    return jnp.where(lanes(total.shape) == total.shape[1] - 127, rest, total).astype(BF16)
+    lane = lanes(total.shape) - (total.shape[1] - 128)
+    return jnp.where((lane == 1) | (lane == 3), rest, total).astype(BF16)
 
 
 def final_piece_kernel(factor, mine, next1, next2, next3, _, out):
     main = mine.shape[1] - 128
     total = ((mine[...] + next2[...]) + (next1[...] + next3[...])) * factor
     out[:, :main] = total[:, :main].astype(BF16)
-    out[:, main:] = split_low(gain_total(total[:, main:]), 3)
-
-
-def write_half(half, at, grad_qkv, grad_out, gain_grad, gains, copy):
+    out[:, main:] = split_low(total[:, main:])
+
+
+def write_half(half, at, grad_qkv, grad_out, copy):
     rows = half.shape[0]
     wide = grad_qkv.shape[1]
     main = wide + grad_out.shape[1]
     at = pl.multiple_of(at * rows, rows)
     copy(half.at[:, :wide], grad_qkv.at[pl.ds(at, rows), :])
     copy(half.at[:, wide:main], grad_out.at[pl.ds(at, rows), :])
-    column = half[:, main:].astype(F32).T
-    gains[...] = column[0:1] + column[1:2] + column[2:3]
-    copy(gains, gain_grad.at[:, pl.ds(at, rows)])
 
 
 def copier(sems, copies):
@@ -331,11 +331,11 @@
 
 
 def first_finish_kernel(
-    mine, own, north, east, mixed, grad_tokens, grad_qkv, grad_out, gain_grad, gains, sems
+    mine, own, north, east, mixed, grad_tokens, grad_qkv, grad_out, sems
 ):
     copies = []
     copy = copier(sems, copies)
-    write_half(mine, lax.axis_index("core"), grad_qkv, grad_out, gain_grad, gains, copy)
+    write_half(mine, lax.axis_index("core"), grad_qkv, grad_out, copy)
     for quad, at, lon in (
         (own, SHIFT, SHIFT),
         (north.at[0], 0, SHIFT),
@@ -349,10 +349,20 @@
         item.wait()
 
 
-def last_finish_kernel(theirs, _, __, ___, grad_qkv, grad_out, gain_grad, gains, sems):
+def last_finish_kernel(theirs, mine, _, __, grad_qkv, grad_out, gain_grad, gains, sems):
     copies = []
     copy = copier(sems, copies)
-    write_half(theirs, 1 - lax.axis_index("core"), grad_qkv, grad_out, gain_grad, gains, copy)
+    core = lax.axis_index("core")
+    rows = mine.shape[0]
+    write_half(theirs, 1 - core, grad_qkv, grad_out, copy)
+    main = mine.shape[1] - 128
+    sums = []
+    for half in (mine, theirs):
+        column = half[:, main:].astype(F32).T
+        sums.append([column[i : i + 1] + column[i + 1 : i + 2] + column[i + 2 : i + 3] for i in (0, 3)])
+    gains[:, pl.ds(pl.multiple_of(core * rows, rows), rows)] = sums[0][0] + sums[1][1]
+    gains[:, pl.ds(pl.multiple_of((1 - core) * rows, rows), rows)] = sums[1][0] + sums[0][1]
+    copy(gains, gain_grad)
     for item in copies:
         item.wait()
 
@@ -404,16 +414,14 @@
         send, *shared = pl.pallas_call(
             grads_kernel,
             in_specs=[vmem] * 8,
-            out_specs=[vmem] * 8,
+            out_specs=[vmem] * 6,
             out_shape=[
                 jax.ShapeDtypeStruct((rows, width), BF16),
                 jax.ShapeDtypeStruct((feat, ext), BF16),
-                jax.ShapeDtypeStruct((n_tokens, feat), BF16),
                 jax.ShapeDtypeStruct((feat, ext), BF16),
                 jax.ShapeDtypeStruct((ext, feat), BF16),
                 jax.ShapeDtypeStruct((feat, ext), BF16),
                 jax.ShapeDtypeStruct((2 * feat, n_tokens), BF16),
-                jax.ShapeDtypeStruct((feat, 128), F32),
             ],
             scratch_shapes=grads_scratch(n_tokens, feat),
             compiler_params=params,
@@ -424,7 +432,7 @@
     with jax.named_scope("window_tokens"):
         keep, own, east, north = pl.pallas_call(
             tokens_kernel,
-            in_specs=[vmem] * 13,
+            in_specs=[vmem] * 12,
             out_specs=[vmem] * 4,
             out_shape=[
                 jax.ShapeDtypeStruct((rows, width), F32),
@@ -433,9 +441,13 @@
                     for lead in ((), (), (2,))
                 ),
             ],
-            scratch_shapes=[pltpu.VMEM((n_tokens, feat), F32)],
+            scratch_shapes=[
+                pltpu.VMEM((n_tokens, feat), F32),
+                pltpu.VMEM((n_tokens, feat), BF16),
+                pltpu.VMEM((feat, 128), F32),
+            ],
             compiler_params=params,
-        )(*quads, gain_row, w_out, *shared)
+        )(*quads, gain_row, w_qkv, w_out, *shared)
     with jax.named_scope("sum_cores"):
         pair_sum = add_pair(keep, other)
     pair_sum, north = lax.optimization_barrier((pair_sum, north))
@@ -480,20 +492,20 @@
         mixed, grad_tokens, *halves = pl.pallas_call(
             first_finish_kernel,
             in_specs=[vmem] + [hbm] * 3,
-            out_specs=[hbm] * 5,
-            out_shape=[jax.ShapeDtypeStruct(shape, BF16)] * 2 + final,
-            scratch_shapes=[pltpu.VMEM((1, rows), F32), pltpu.SemaphoreType.DMA((11,))],
+            out_specs=[hbm] * 4,
+            out_shape=[jax.ShapeDtypeStruct(shape, BF16)] * 2 + final[:2],
+            scratch_shapes=[pltpu.SemaphoreType.DMA((10,))],
             compiler_params=params,
         )(mine, own, north, east)
         grad_qkv, grad_out, gain_gradient = pl.pallas_call(
             last_finish_kernel,
-            in_specs=[vmem] + [hbm] * 3,
+            in_specs=[vmem] * 2 + [hbm] * 2,
             out_specs=[hbm] * 3,
             out_shape=final,
-            input_output_aliases={1: 0, 2: 1, 3: 2},
-            scratch_shapes=[pltpu.VMEM((1, rows), F32), pltpu.SemaphoreType.DMA((3,))],
+            input_output_aliases={2: 0, 3: 1},
+            scratch_shapes=[pltpu.VMEM((1, feat), F32), pltpu.SemaphoreType.DMA((3,))],
             compiler_params=params,
-        )(theirs, *halves)
+        )(theirs, mine, *halves)
     return mixed, grad_tokens, gain_gradient[0], grad_qkv, grad_out
 
 

time: 99.1 us -> 99.4 us (level)
  starting transfers between devices: 41.6 us -> 39 us
  blocking collectives: 22.3 us -> 24.2 us
    ppermute x1, starting transfers between devices: 1.38 us -> 6.63 us  [shards(): corner = lax.ppermute(corner, EVERY, pairs(lambda a, o: (a - 1, o - 1)))]
    ppermute x1, starting transfers between devices: 6.1 us -> 3.54 us  [shards(): north = lax.ppermute(north, EVERY, pairs(lambda a, o: (a - 1, o)))]
    ppermute x3, starting transfers between devices: 9.89 us -> 7.44 us  [shards(): lax.ppermute(piece, FAR, [(i, (i + by) % far) for i in range(far)])]
    ppermute x1, waiting for transfers between devices: 0.01 us -> 2.35 us  [shards(): corner = lax.ppermute(corner, EVERY, pairs(lambda a, o: (a - 1, o - 1)))]
    all_to_all x1, blocking collectives: 22.3 us -> 24.2 us  [shards(): pieces = lax.all_to_all(pair_sum.reshape(near, chunk, width), NEAR, 0, 0)]
    ppermute x1, starting transfers between devices: 2.9 us -> 1.35 us  [shards(): other = lax.ppermute(send, 'core', swap)]
    ppermute x1, starting transfers between devices: 4.84 us -> 3.32 us  [shards(): east = lax.ppermute(east, EVERY, pairs(lambda a, o: (a, o - 1)))]
    ppermute x1, waiting for transfers between devices: 1.33 us -> 0.11 us  [shards(): other = lax.ppermute(send, 'core', swap)]
  transfers between devices with their start and end apart: 11 -> 11, of which waited for: 6 -> 6; matrix products, arithmetic and copies ran while one was open for 1% -> 1% of each run, Pallas kernels for 3% -> 4%
where the time goes in v10:
time: 99.4 us; the launch traced here: 99.2 us
  starting transfers between devices  39 us (39%)
  blocking collectives  24.2 us (24%)
  waiting for transfers between devices  17.4 us (18%)
  Pallas kernels  12.6 us (13%)
  local copies, waits for them, and re-layouts  3.13 us (3%)
  other arithmetic  1.85 us (2%)
    all_to_all x1, blocking collectives, shards(): pieces = lax.all_to_all(pair_sum.reshape(near, chunk, width), NEAR, 0, 0)  24.2 us
    ppermute x1, waiting for transfers between devices, shards(): east = lax.ppermute(east, EVERY, pairs(lambda a, o: (a, o + 1)))  10.2 us
    pallas_call x1, Pallas kernels, shards(): pl.pallas_call(grads_kernel, in_specs=[vmem] * 8, out_specs=[vmem] * 6, o...  7.55 us
    ppermute x3, starting transfers between devices, shards(): lax.ppermute(piece, FAR, [(i, (i + by) % far) for i in range(far)])  7.44 us
    ppermute x1, starting transfers between devices, shards(): corner = lax.ppermute(corner, EVERY, pairs(lambda a, o: (a - 1, o - 1)))  6.63 us
    all_to_all x1, starting transfers between devices, shards(): lax.all_to_all(jnp.broadcast_to(piece[None], (near,) + piece.shape), NEAR...  6.51 us
    ppermute x1, starting transfers between devices, shards(): theirs = lax.ppermute(mine, 'core', swap)  4.84 us
    ppermute x1, starting transfers between devices, shards(): east = lax.ppermute(east, EVERY, pairs(lambda a, o: (a, o + 1)))  4.82 us
  transfers between devices with their start and end apart: 11, of which 6 were waited for; matrix products, arithmetic and copies ran while one was open for 1% of the time, Pallas kernels for 4%

profile of v10, /device:TPU:1, one launch (start us, length us, event | category | flops | bytes accessed | tf_op | source)
XLA Modules:
  0.0 99.2 jit_solution(17495576393428720952)
XLA Ops:
  0.6 0.0 copy-start
  0.6 0.0 copy-start.1
  0.7 1.7 %fusion.4 = (bf16[1,6,6,2,512]{4,3,2,1,0:T(2,128)(2,1)S(1)}, bf16[1,6,6,2,512]{4,3,2,1,0:T(2,128)(2,1)S(1)}, bf16[1,6,6,2,512]{4,3,2,1,0:T(2,128)(2,1)S(1)}, bf1...) fusion(bf16[1,12,12,2,512]{4,3,2,1,0:T(2,128)(2,1)} %param.5, ...), kind=kLoop, calls=%fused_computation.12 | loop fusion | bytes 1179648 | tf_op jit(solution)/shard_map/window_in/slice | solution.py:389
  2.4 0.2 pad_maximum_fusion.2
  2.6 0.1 reshape.30
  2.6 3.3 %collective-permute-start = (bf16[2,72,512]{2,1,0:T(8,128)(2,1)S(1)}, bf16[2,72,512]{2,1,0:T(8,128)(2,1)S(1)}, u32[]{:S(2)}, u32[]{:S(2)}) collective-permute-start(bf16[2,72,512]{2,1,0:T(8,128)(2,1)S(1)} %reshape.30), channel_id=1, source_target_pairs={{0,31},{1,0},{2,1},{3,2},{4,3},{5,4},{6,5},{7,6},{8,7},{9,8},{10,9... | collective-permute-start | bytes 442376 | tf_op jit(solution)/shard_map/window_in/ppermute | solution.py:395
  6.0 0.2 pad_maximum_fusion.3
  6.2 0.1 reshape.31
  6.2 3.5 %collective-permute-start.1 = (bf16[2,72,512]{2,1,0:T(8,128)(2,1)S(1)}, bf16[2,72,512]{2,1,0:T(8,128)(2,1)S(1)}, u32[]{:S(2)}, u32[]{:S(2)}) collective-permute-start(bf16[2,72,512]{2,1,0:T(8,128)(2,1)S(1)} %reshape.31), channel_id=1, source_target_pairs={{0,224},{1,225},{2,226},{3,227},{4,228},{5,229},{6,230},{7,231},{8... | collective-permute-start | bytes 442376 | tf_op jit(solution)/shard_map/window_in/ppermute | solution.py:396
  9.8 0.2 pad_maximum_fusion.4
  10.0 0.1 reshape.32
  10.0 6.6 %collective-permute-start.2 = (bf16[2,72,512]{2,1,0:T(8,128)(2,1)S(1)}, bf16[2,72,512]{2,1,0:T(8,128)(2,1)S(1)}, u32[]{:S(2)}, u32[]{:S(2)}) collective-permute-start(bf16[2,72,512]{2,1,0:T(8,128)(2,1)S(1)} %reshape.32), channel_id=1, source_target_pairs={{0,255},{1,224},{2,225},{3,226},{4,227},{5,228},{6,229},{7,230},{8... | collective-permute-start | bytes 442376 | tf_op jit(solution)/shard_map/window_in/ppermute | solution.py:397
  16.7 0.2 pad_maximum_fusion.1
  16.9 0.1 reshape.29.q0
  17.0 0.0 copy-done
  17.0 0.0 copy-done.1
  17.0 0.5 weights.1
  17.5 0.0 collective-permute-done.q1
  17.5 0.0 collective-permute-done.1.q2
  17.5 2.4 %collective-permute-done.2.q3 = bf16[2,72,512]{2,1,0:T(8,128)(2,1)S(1)} collective-permute-done((bf16[2,72,512]{2,1,0:T(8,128)(2,1)S(1)}, bf16[2,72,512]{2,1,0:T(8,128)(2,1)S(1)}, u32[]{:S(2)}, u32[]{:S(2)}) %collective-permute-start.2) | collective-permute-done | bytes 147488 | tf_op jit(solution)/shard_map/window_in/ppermute | solution.py:397
  19.8 0.0 copy-done.2
  19.8 7.5 %window_grads.1 = (bf16[256,2176]{1,0:T(8,128)(2,1)S(1)}, bf16[512,384]{1,0:T(8,128)(2,1)S(1)}, bf16[512,384]{1,0:T(8,128)(2,1)S(1)}, bf16[384,512]{1,0:T(8,128)...) custom-call(bf16[2,72,512]{2,1,0:T(8,128)(2,1)S(1)} %reshape.29.q0, ...), custom_call_target="tpu_custom_call" | custom-call | tf_op jit(solution)/shard_map/window_grads/pallas_call | solution.py:414
  27.4 1.3 %collective-permute-start.3 = (bf16[256,2176]{1,0:T(8,128)(2,1)S(1)}, bf16[256,2176]{1,0:T(8,128)(2,1)S(1)}, u32[]{:S(2)}, u32[]{:S(2)}) collective-permute-start(bf16[256,2176]{1,0:T(8,128)(2,1)S(1)} %get-tuple-element.40), channel_id=1, source_target_pairs={{0,1},{1,0},{2,3},{3,2},{4,5},{5,4},{6,7},{7,6},{8,9},{9,8},{10,11... | collective-permute-start | bytes 3342344 | tf_op jit(solution)/shard_map/sum_cores/ppermute | solution.py:431
  28.7 2.3 %window_tokens.1 = (f32[256,2176]{1,0:T(8,128)S(1)}, bf16[2,6,6,2,512]{4,3,2,1,0:T(2,128)(2,1)S(1)}, bf16[2,6,6,2,512]{4,3,2,1,0:T(2,128)(2,1)S(1)}, bf16[2,2,6,6,2,512]{5,4,3,2,1,0:T(2,128)(2,1)S(1)}) custom-call(bf16[2,72,512]{2,1,0:T(8,128)(2,1)S(1)} %reshape.29.q0, bf16[2,72,512]{2,1,0:T(8,128)(2,1)S(1)} %collective-permute-done.q1, ...), custom_call_target="tpu_custom_call" | custom-call | tf_op jit(solution)/shard_map/window_tokens/pallas_call | solution.py:433
  31.0 0.1 collective-permute-done.3
  31.1 0.4 fusion
  31.6 24.2 %all_to_all.10 = bf16[32,8,2176]{2,1,0:T(8,128)(2,1)S(1)} all-to-all(bf16[32,8,2176]{2,1,0:T(8,128)(2,1)S(1)} %bitcast.11), channel_id=1, replica_groups=mesh['xh'=2,'y'=4,'zh'=4,'zl'=2,'xl'=2,'core'=2] {'xh','y','zl','xl'}, dimensions={0} | all-to-all | bytes 2228224 | tf_op jit(solution)/shard_map/sum_near/all_to_all | solution.py:458
  55.8 0.2 convert_reduce_fusion.mine._
  55.9 0.5 collective-permute-start.7
  56.5 0.8 collective-permute-start.4
  57.3 4.2 %collective-permute-start.5 = (f32[8,2176]{1,0:T(8,128)S(1)}, f32[8,2176]{1,0:T(8,128)S(1)}, u32[]{:S(2)}, u32[]{:S(2)}) collective-permute-start(f32[8,2176]{1,0:T(8,128)S(1)} %convert_reduce_fusion.mine._), channel_id=1, source_target_pairs={{0,16},{8,24},{16,0},{24,8},{1,17},{9,25},{17,1},{25,9},{2,18},{10... | collective-permute-start | bytes 208904 | tf_op jit(solution)/shard_map/sum_far/ppermute | solution.py:462
  61.5 2.4 %collective-permute-start.6 = (f32[8,2176]{1,0:T(8,128)S(1)}, f32[8,2176]{1,0:T(8,128)S(1)}, u32[]{:S(2)}, u32[]{:S(2)}) collective-permute-start(f32[8,2176]{1,0:T(8,128)S(1)} %convert_reduce_fusion.mine._), channel_id=1, source_target_pairs={{0,24},{8,0},{16,8},{24,16},{1,25},{9,1},{17,9},{25,17},{2,26},{10... | collective-permute-start | bytes 208904 | tf_op jit(solution)/shard_map/sum_far/ppermute | solution.py:462
  63.9 0.0 collective-permute-done.4.next1
  63.9 1.8 %collective-permute-done.5.next2 = f32[8,2176]{1,0:T(8,128)S(1)} collective-permute-done((f32[8,2176]{1,0:T(8,128)S(1)}, f32[8,2176]{1,0:T(8,128)S(1)}, u32[]{:S(2)}, u32[]{:S(2)}) %collective-permute-start.5) | collective-permute-done | bytes 69664 | tf_op jit(solution)/shard_map/sum_far/ppermute | solution.py:462
  65.7 1.8 %collective-permute-done.6.next3 = f32[8,2176]{1,0:T(8,128)S(1)} collective-permute-done((f32[8,2176]{1,0:T(8,128)S(1)}, f32[8,2176]{1,0:T(8,128)S(1)}, u32[]{:S(2)}, u32[]{:S(2)}) %collective-permute-start.6) | collective-permute-done | bytes 69664 | tf_op jit(solution)/shard_map/sum_far/ppermute | solution.py:462
  67.5 0.1 sum_far.1
  67.6 0.0 collective-permute-done.7.north
  67.6 1.1 %broadcast_in_dim.10 = bf16[32,8,2176]{2,1,0:T(8,128)(2,1)} broadcast(bf16[8,2176]{1,0:T(8,128)(2,1)S(1)} %sum_far.1), dimensions={1,2} | broadcast | bytes 1148928 | tf_op jit(solution)/shard_map/share/broadcast_in_dim | solution.py:481
  68.7 6.5 %all-to-all-start.1 = ((bf16[32,8,2176]{2,1,0:T(8,128)(2,1)}), bf16[32,8,2176]{2,1,0:T(8,128)(2,1)S(1)}, u32[]{:S(2)}, u32[]{:S(2)}) async-start(bf16[32,8,2176]{2,1,0:T(8,128)(2,1)} %broadcast_in_dim.10), calls=%async_computation.1 | async-start | bytes 2228224 | tf_op jit(solution)/shard_map/share/all_to_all | solution.py:481
  75.2 0.1 slice.35
  75.3 0.4 pad_maximum_fusion
  75.7 4.8 %collective-permute-start.8 = (bf16[2,2,6,6,2,512]{5,4,3,2,1,0:T(2,128)(2,1)S(1)}, bf16[2,2,6,6,2,512]{5,4,3,2,1,0:T(2,128)(2,1)S(1)}, u32[]{:S(2)}, u32[]{:S(2)}) collective-permute-start(bf16[2,2,6,6,2,512]{5,4,3,2,1,0:T(2,128)(2,1)S(1)} %pad_maximum_fusion), channel_id=1, source_target_pairs={{0,1},{1,2},{2,3},{3,4},{4,5},{5,6},{6,7},{7,8},{8,9},{9,10},{10,1... | collective-permute-start | bytes 884744 | tf_op jit(solution)/shard_map/window_out/ppermute | solution.py:479
  80.6 10.2 %collective-permute-done.8.east = bf16[2,2,6,6,2,512]{5,4,3,2,1,0:T(2,128)(2,1)S(1)} collective-permute-done((bf16[2,2,6,6,2,512]{5,4,3,2,1,0:T(2,128)(2,1)S(1)}, bf16[2,2,6,6,2,512]{5,4,3,2,1,0:T(2,128)(2,1)S(1)}, u32[]{:S(2)}, u32[]{:S(2)}) %collective-permute-start.8) | collective-permute-done | bytes 294944 | tf_op jit(solution)/shard_map/window_out/ppermute | solution.py:479
  90.8 0.0 all-to-all-done.1
  90.8 4.8 %collective-permute-start.9 = (bf16[256,2176]{1,0:T(8,128)(2,1)S(1)}, bf16[256,2176]{1,0:T(8,128)(2,1)S(1)}, u32[]{:S(2)}, u32[]{:S(2)}) collective-permute-start(bf16[256,2176]{1,0:T(8,128)(2,1)S(1)} %bitcast.5), channel_id=1, source_target_pairs={{0,1},{1,0},{2,3},{3,2},{4,5},{5,4},{6,7},{7,6},{8,9},{9,8},{10,11... | collective-permute-start | bytes 3342344 | tf_op jit(solution)/shard_map/share/ppermute | solution.py:484
  95.6 1.2 %finish.2 = (bf16[1,12,12,2,512]{4,3,2,1,0:T(2,128)(2,1)}, bf16[1,12,12,2,512]{4,3,2,1,0:T(2,128)(2,1)}, bf16[512,1536]{1,0:T(8,128)(2,1)}, bf16[512,512]{1,0:T(8,128)(2,1)}) custom-call(bf16[256,2176]{1,0:T(8,128)(2,1)S(1)} %bitcast.6, bf16[2,6,6,2,512]{4,3,2,1,0:T(2,128)(2,1)S(1)} %get-tuple-element.50.own, ...), custom_call_target="tpu_custom_call" | custom-call | tf_op jit(solution)/shard_map/finish/pallas_call | solution.py:492
  96.9 1.1 %collective-permute-done.9.theirs = bf16[256,2176]{1,0:T(8,128)(2,1)S(1)} collective-permute-done((bf16[256,2176]{1,0:T(8,128)(2,1)S(1)}, bf16[256,2176]{1,0:T(8,128)(2,1)S(1)}, u32[]{:S(2)}, u32[]{:S(2)}) %collective-permute-start.9) | collective-permute-done | bytes 1114144 | tf_op jit(solution)/shard_map/share/ppermute | solution.py:484
  98.0 1.0 %finish.3 = (bf16[512,1536]{1,0:T(8,128)(2,1)}, bf16[512,512]{1,0:T(8,128)(2,1)}, f32[1,512]{1,0:T(1,128)}) custom-call(bf16[256,2176]{1,0:T(8,128)(2,1)S(1)} %collective-permute-done.9.theirs, bf16[256,2176]{1,0:T(8,128)(2,1)S(1)} %bitcast.7, bf16[512,1536]{1,0:T(8,128)(2,1)} %get-tuple-element.54._, ...), custom_call_target="tpu_custom_call", output_to_operand_aliasing={{0}: (2, {}), {1}: (3, {})} | custom-call | tf_op jit(solution)/shard_map/finish/pallas_call | solution.py:500
  (2 shorter events, 0.0 us)
Async XLA Ops:
  0.6 16.3 %copy-start = (bf16[512,1536]{1,0:T(8,128)(2,1)S(1)}, bf16[512,1536]{1,0:T(8,128)(2,1)}, u32[]{:S(2)}) copy-start(bf16[512,1536]{1,0:T(8,128)(2,1)} %wqkv.5) | copy-start | bytes 4718596
  0.6 16.3 %copy-start.1 = (bf16[512,512]{1,0:T(8,128)(2,1)S(1)}, bf16[512,512]{1,0:T(8,128)(2,1)}, u32[]{:S(2)}) copy-start(bf16[512,512]{1,0:T(8,128)(2,1)} %wout.3) | copy-start | bytes 1572868
  2.6 14.8 %collective-permute-start = (bf16[2,72,512]{2,1,0:T(8,128)(2,1)S(1)}, bf16[2,72,512]{2,1,0:T(8,128)(2,1)S(1)}, u32[]{:S(2)}, u32[]{:S(2)}) collective-permute-start(bf16[2,72,512]{2,1,0:T(8,128)(2,1)S(1)} %reshape.30), channel_id=1, source_target_pairs={{0,31},{1,0},{2,1},{3,2},{4,3},{5,4},{6,5},{7,6},{8,7},{9,8},{10,9... | collective-permute-start | bytes 442376 | tf_op jit(solution)/shard_map/window_in/ppermute | solution.py:395
  6.2 11.2 %collective-permute-start.1 = (bf16[2,72,512]{2,1,0:T(8,128)(2,1)S(1)}, bf16[2,72,512]{2,1,0:T(8,128)(2,1)S(1)}, u32[]{:S(2)}, u32[]{:S(2)}) collective-permute-start(bf16[2,72,512]{2,1,0:T(8,128)(2,1)S(1)} %reshape.31), channel_id=1, source_target_pairs={{0,224},{1,225},{2,226},{3,227},{4,228},{5,229},{6,230},{7,231},{8... | collective-permute-start | bytes 442376 | tf_op jit(solution)/shard_map/window_in/ppermute | solution.py:396
  9.8 10.1 %copy-start.2 = (f32[512]{0:T(512)S(1)}, f32[512]{0:T(512)}, u32[]{:S(2)}) copy-start(f32[512]{0:T(512)} %param.6) | copy-start | bytes 6148
  10.0 9.8 %collective-permute-start.2 = (bf16[2,72,512]{2,1,0:T(8,128)(2,1)S(1)}, bf16[2,72,512]{2,1,0:T(8,128)(2,1)S(1)}, u32[]{:S(2)}, u32[]{:S(2)}) collective-permute-start(bf16[2,72,512]{2,1,0:T(8,128)(2,1)S(1)} %reshape.32), channel_id=1, source_target_pairs={{0,255},{1,224},{2,225},{3,226},{4,227},{5,228},{6,229},{7,230},{8... | collective-permute-start | bytes 442376 | tf_op jit(solution)/shard_map/window_in/ppermute | solution.py:397
  27.4 3.7 %collective-permute-start.3 = (bf16[256,2176]{1,0:T(8,128)(2,1)S(1)}, bf16[256,2176]{1,0:T(8,128)(2,1)S(1)}, u32[]{:S(2)}, u32[]{:S(2)}) collective-permute-start(bf16[256,2176]{1,0:T(8,128)(2,1)S(1)} %get-tuple-element.40), channel_id=1, source_target_pairs={{0,1},{1,0},{2,3},{3,2},{4,5},{5,4},{6,7},{7,6},{8,9},{9,8},{10,11... | collective-permute-start | bytes 3342344 | tf_op jit(solution)/shard_map/sum_cores/ppermute | solution.py:431
  55.9 11.7 %collective-permute-start.7 = (bf16[2,2,6,6,2,512]{5,4,3,2,1,0:T(2,128)(2,1)S(1)}, bf16[2,2,6,6,2,512]{5,4,3,2,1,0:T(2,128)(2,1)S(1)}, u32[]{:S(2)}, u32[]{:S(2)}) collective-permute-start(bf16[2,2,6,6,2,512]{5,4,3,2,1,0:T(2,128)(2,1)S(1)} %get-tuple-element.45), channel_id=1, source_target_pairs={{0,32},{1,33},{2,34},{3,35},{4,36},{5,37},{6,38},{7,39},{8,40},{9,... | collective-permute-start | bytes 884744 | tf_op jit(solution)/shard_map/window_out/ppermute | solution.py:467
  56.5 7.4 %collective-permute-start.4 = (f32[8,2176]{1,0:T(8,128)S(1)}, f32[8,2176]{1,0:T(8,128)S(1)}, u32[]{:S(2)}, u32[]{:S(2)}) collective-permute-start(f32[8,2176]{1,0:T(8,128)S(1)} %convert_reduce_fusion.mine._), channel_id=1, source_target_pairs={{0,8},{8,16},{16,24},{24,0},{1,9},{9,17},{17,25},{25,1},{2,10},{10... | collective-permute-start | bytes 208904 | tf_op jit(solution)/shard_map/sum_far/ppermute | solution.py:462
  57.3 8.4 %collective-permute-start.5 = (f32[8,2176]{1,0:T(8,128)S(1)}, f32[8,2176]{1,0:T(8,128)S(1)}, u32[]{:S(2)}, u32[]{:S(2)}) collective-permute-start(f32[8,2176]{1,0:T(8,128)S(1)} %convert_reduce_fusion.mine._), channel_id=1, source_target_pairs={{0,16},{8,24},{16,0},{24,8},{1,17},{9,25},{17,1},{25,9},{2,18},{10... | collective-permute-start | bytes 208904 | tf_op jit(solution)/shard_map/sum_far/ppermute | solution.py:462
  61.5 6.0 %collective-permute-start.6 = (f32[8,2176]{1,0:T(8,128)S(1)}, f32[8,2176]{1,0:T(8,128)S(1)}, u32[]{:S(2)}, u32[]{:S(2)}) collective-permute-start(f32[8,2176]{1,0:T(8,128)S(1)} %convert_reduce_fusion.mine._), channel_id=1, source_target_pairs={{0,24},{8,0},{16,8},{24,16},{1,25},{9,1},{17,9},{25,17},{2,26},{10... | collective-permute-start | bytes 208904 | tf_op jit(solution)/shard_map/sum_far/ppermute | solution.py:462
  68.7 22.1 %all-to-all-start.1 = ((bf16[32,8,2176]{2,1,0:T(8,128)(2,1)}), bf16[32,8,2176]{2,1,0:T(8,128)(2,1)S(1)}, u32[]{:S(2)}, u32[]{:S(2)}) async-start(bf16[32,8,2176]{2,1,0:T(8,128)(2,1)} %broadcast_in_dim.10), calls=%async_computation.1 | async-start | bytes 2228224 | tf_op jit(solution)/shard_map/share/all_to_all | solution.py:481
  75.7 15.1 %collective-permute-start.8 = (bf16[2,2,6,6,2,512]{5,4,3,2,1,0:T(2,128)(2,1)S(1)}, bf16[2,2,6,6,2,512]{5,4,3,2,1,0:T(2,128)(2,1)S(1)}, u32[]{:S(2)}, u32[]{:S(2)}) collective-permute-start(bf16[2,2,6,6,2,512]{5,4,3,2,1,0:T(2,128)(2,1)S(1)} %pad_maximum_fusion), channel_id=1, source_target_pairs={{0,1},{1,2},{2,3},{3,4},{4,5},{5,6},{6,7},{7,8},{8,9},{9,10},{10,1... | collective-permute-start | bytes 884744 | tf_op jit(solution)/shard_map/window_out/ppermute | solution.py:479
  90.8 7.2 %collective-permute-start.9 = (bf16[256,2176]{1,0:T(8,128)(2,1)S(1)}, bf16[256,2176]{1,0:T(8,128)(2,1)S(1)}, u32[]{:S(2)}, u32[]{:S(2)}) collective-permute-start(bf16[256,2176]{1,0:T(8,128)(2,1)S(1)} %bitcast.5), channel_id=1, source_target_pairs={{0,1},{1,0},{2,3},{3,2},{4,5},{5,4},{6,7},{7,6},{8,9},{9,8},{10,11... | collective-permute-start | bytes 3342344 | tf_op jit(solution)/shard_map/share/ppermute | solution.py:484
